TPU v7x, 256 devices: a whole 4x4x8 slice. The times are simulated.
256 devices in a mesh: branch: 64 (over y, z, core), head: 4 (over x).
Axes of the slice: x: 4, y: 4, z: 8, core: 2. Of those that a mesh axis runs over, the one named last changes fastest.
Arguments:
- queries: bfloat16 [8192, 64, 128], P('branch', 'head'), may hold values from -120 to 120
- keys: bfloat16 [8192, 8, 128], P('branch', 'head'), may hold values from -6 to 6
- values: bfloat16 [8192, 8, 128], P('branch', 'head'), may hold values from -6 to 6
- cotangent: bfloat16 [8192, 64, 128], P('branch', 'head'), may hold values from -216 to 216
- rewards: bfloat16 [64], P('branch'), may hold values from 0 to 2
- groups: int32 [64], P('branch'), may hold values from 0 to 15, as said below
- ancestors: int32 [64, 8], P('branch'), may hold values from -1 to 63, as said below
- step_ids: int32 [64, 128], P('branch'), may hold values from 0 to 3, never falling along the last dimension, each value on 1 to 64 neighbouring positions
Outputs:
- query_grad: float32 [8192, 64, 128], P('branch', 'head')
- key_grad: float32 [8192, 8, 128], P('branch', 'head')
- value_grad: float32 [8192, 8, 128], P('branch', 'head')
- grad_rms: float32 [], replicated
Inputs may be any that keep to these rules, and one draw needn't show every extreme that they name: `groups`: each group id names exactly 4 blocks; blocks of one group have the same ancestor list. Row b lists block b's ancestors nearest first, each entry the parent of the one before, then -1 to the end; a block never lists itself; some block has exactly 8 ancestors.
All inputs are finite; a program needn't handle non-finite values.
Results may differ from a plain program's by a relative error of at most 0.02.
Values may be sent and summed in bfloat16 or wider, within the bound.
No kernel may reach another device: no remote copies, remote signals or barrier semaphores. Data moves between devices by JAX's collectives and lax.ppermute only.
A program may use at most 128 MiB of HBM per device.

v0:
```python
import math

import jax
import jax.numpy as jnp
from jax import lax
from jax.sharding import PartitionSpec as P

GROUP = 4


def select_blocks(lineage, pieces):
    block_ids = jnp.arange(pieces.shape[0], dtype=jnp.int32)
    chosen = (lineage[:, None] == block_ids[None, :]).astype(pieces.dtype)
    picked = jnp.einsum("dn,ntgh->dtgh", chosen, pieces, preferred_element_type=jnp.float32)
    return picked.astype(jnp.bfloat16)


def local(queries, keys, values, cotangent, rewards, groups, ancestors, step_ids):
    rows_here, heads_here, head_dim = queries.shape
    kv_here = keys.shape[1]
    head_ratio = heads_here // kv_here
    block_count = lax.axis_size("branch")
    own_block = lax.axis_index("branch")
    lineage = ancestors[0]
    depth_count = lineage.shape[0]
    slot_count = depth_count + 1
    score_scale = 1.0 / math.sqrt(head_dim)
    reward = rewards[0].astype(jnp.float32)
    own_group = groups[0]
    key_stash = select_blocks(lineage, lax.all_gather(keys[None], "branch", axis=0, tiled=True))
    value_stash = select_blocks(lineage, lax.all_gather(values[None], "branch", axis=0, tiled=True))
    flags = (jnp.arange(block_count // GROUP, dtype=jnp.int32) == own_group).astype(jnp.float32)
    group_sums, group_squares = lax.psum((flags * reward, flags * (reward * reward)), "branch")
    group_sum = jnp.sum(flags * group_sums)
    group_sq = jnp.sum(flags * group_squares)
    mean_here = group_sum / GROUP
    spread_here = jnp.sqrt(jnp.maximum(group_sq / GROUP - mean_here * mean_here, 0.25))
    advantage = (reward - mean_here) / spread_here
    trained = (step_ids[0] % 2 == 0).astype(jnp.float32)
    grad_out = ((advantage * trained)[:, None, None] * cotangent.astype(jnp.float32)).astype(
        jnp.bfloat16
    )
    slot_valid = jnp.concatenate([lineage >= 0, jnp.ones((1,), jnp.bool_)])
    key_slot = jnp.arange(slot_count * rows_here) // rows_here
    key_pos = jnp.arange(slot_count * rows_here) % rows_here
    query_pos = jnp.arange(rows_here)
    visible = jnp.where(
        key_slot[None, :] < depth_count,
        slot_valid[key_slot][None, :],
        key_pos[None, :] <= query_pos[:, None],
    )
    query_parts = []
    key_parts = []
    value_parts = []
    for kv_index in range(kv_here):
        first_head = kv_index * head_ratio
        near_keys = jnp.concatenate(
            [key_stash[:, :, kv_index], keys[None, :, kv_index]], 0
        ).reshape(slot_count * rows_here, head_dim)
        near_values = jnp.concatenate(
            [value_stash[:, :, kv_index], values[None, :, kv_index]], 0
        ).reshape(slot_count * rows_here, head_dim)
        query_block = queries[:, first_head : first_head + head_ratio]
        grad_block = grad_out[:, first_head : first_head + head_ratio]
        scores = (
            jnp.einsum("qrd,kd->rqk", query_block, near_keys, preferred_element_type=jnp.float32)
            * score_scale
        )
        top_score = jnp.max(jnp.where(visible, scores, -1e30), axis=-1, keepdims=True)
        exponent = jnp.where(visible, jnp.exp(scores - top_score), 0.0)
        probs = exponent / jnp.sum(exponent, axis=-1, keepdims=True)
        probs_low = probs.astype(jnp.bfloat16)
        attended = jnp.einsum(
            "rqk,kd->qrd", probs_low, near_values, preferred_element_type=jnp.float32
        )
        row_delta = jnp.sum(grad_block.astype(jnp.float32) * attended, axis=-1)
        prob_grad = jnp.einsum(
            "qrd,kd->rqk", grad_block, near_values, preferred_element_type=jnp.float32
        )
        dscore = (probs * (prob_grad - row_delta.T[:, :, None])).astype(jnp.bfloat16)
        query_parts.append(
            jnp.einsum("rqk,kd->qrd", dscore, near_keys, preferred_element_type=jnp.float32)
            * score_scale
        )
        key_term = (
            jnp.einsum("rqk,qrd->kd", dscore, query_block, preferred_element_type=jnp.float32)
            * score_scale
        )
        value_term = jnp.einsum(
            "rqk,qrd->kd", probs_low, grad_block, preferred_element_type=jnp.float32
        )
        key_parts.append(key_term.reshape(slot_count, rows_here, head_dim))
        value_parts.append(value_term.reshape(slot_count, rows_here, head_dim))
    query_grad = jnp.concatenate(query_parts, 1)
    contrib = jnp.stack([jnp.stack(key_parts, 2), jnp.stack(value_parts, 2)], 2)
    slot_ids = jnp.concatenate([lineage, own_block[None]])
    row_count = rows_here * lax.axis_size("branch")
    blocks_here = row_count // rows_here
    inside = slot_valid & (slot_ids >= 0) & (slot_ids < blocks_here)
    target = jnp.where(inside, slot_ids, blocks_here)
    part_rows = (
        jnp.zeros((blocks_here, rows_here, 2, kv_here, head_dim), jnp.float32)
        .at[target]
        .add(contrib, mode="drop")
    )
    gathered_grads = lax.psum_scatter(
        part_rows.reshape(row_count, 2, kv_here, head_dim),
        "branch",
        scatter_dimension=0,
        tiled=True,
    )
    key_grad = gathered_grads[:, 0]
    value_grad = gathered_grads[:, 1]
    local_squares = (
        jnp.sum(query_grad * query_grad)
        + jnp.sum(key_grad * key_grad)
        + jnp.sum(value_grad * value_grad)
    )
    total_squares = lax.psum(local_squares, ("branch", "head"))
    element_count = float(
        block_count * rows_here * lax.axis_size("head") * (heads_here + 2 * kv_here) * head_dim
    )
    grad_rms = jnp.sqrt(total_squares / element_count)
    return (query_grad, key_grad, value_grad, grad_rms)


def solution(mesh):
    in_specs = (
        P("branch", "head", None),
        P("branch", "head", None),
        P("branch", "head", None),
        P("branch", "head", None),
        P("branch"),
        P("branch"),
        P("branch", None),
        P("branch", None),
    )
    out_specs = (
        P("branch", "head", None),
        P("branch", "head", None),
        P("branch", "head", None),
        P(),
    )
    return jax.shard_map(local, mesh=mesh, in_specs=in_specs, out_specs=out_specs, check_vma=False)
```

profile of v0, /device:TPU:32, one launch (start us, length us, event | category | flops | bytes accessed | tf_op | source)
XLA Modules:
  0.0 500.2 jit_solution(16956469091348878286)
XLA Ops:
  7.2 1.5 copy.34
  8.8 1.5 copy.40
  11.7 126.5 %all-reduce = (f32[16]{0:T(128)S(1)}, f32[16]{0:T(128)S(1)}) all-reduce(f32[16]{0:T(128)S(1)} %fusion.69, f32[16]{0:T(128)S(1)} %fusion.68), channel_id=1, replica_groups=mesh['branch'=64,'head'=4] {'branch'}, use_global_device_ids=true, to_apply=%region_2.0 | all-reduce | flops 32 | bytes 256 | tf_op jit(solution)/shard_map/psum | solution.py:33
  145.0 4.3 select_reduce_fusion.2
  151.4 1.8 fusion.73
  153.2 1.3 multiply_convert_fusion
  154.5 1.1 fusion.40
  155.7 5.8 %fusion.28 = bf16[8,128,2,128]{3,0,2,1:T(8,128)(2,1)S(1)} fusion(bf16[64,128,2,128]{3,1,0,2:T(8,128)(2,1)} %bitcast.178, s32[8]{0:T(128)} %bitcast.189), kind=kOutput, calls=%fused_computation.38 | convolution fusion | flops 33817088 | bytes 4718624 | tf_op jit(solution)/shard_map/dn,ntgh->dtgh/dot_general | solution.py:14
  161.5 10.4 %all-gather.7.cloned.1.call-done = bf16[8192,2,128]{2,0,1:T(8,128)(2,1)} async-done(((bf16[128,2,128]{2,0,1:T(8,128)(2,1)}), bf16[8192,2,128]{2,0,1:T(8,128)(2,1)}) %all-gather.7.cloned.1.call-update) | async-done | bytes 4194320 | tf_op jit(solution)/shard_map/all_gather | solution.py:31
  172.0 5.7 %fusion.31 = bf16[8,128,2,128]{3,0,2,1:T(8,128)(2,1)S(1)} fusion(bf16[64,128,2,128]{3,1,0,2:T(8,128)(2,1)} %bitcast.179, s32[8]{0:T(128)S(1)} %bitcast.190), kind=kOutput, calls=%fused_computation.39 | convolution fusion | flops 33817088 | bytes 4718624 | tf_op jit(solution)/shard_map/dn,ntgh->dtgh/dot_general | solution.py:14
  179.4 2.0 fusion.76
  182.6 1.3 fusion.39
  186.6 1.9 fusion.75
  189.7 1.1 fusion.38
  193.1 1.6 pad_maximum_fusion
  194.7 7.8 %broadcast_in_dim.66 = f32[64,128,2,2,128]{4,1,3,2,0:T(8,128)} broadcast(f32[]{:T(128)} %constant.84.clone.1), dimensions={} | broadcast | bytes 16777220 | tf_op jit(solution)/shard_map/broadcast_in_dim | solution.py:102
  202.5 8.6 %scatter_fusion = f32[64,128,2,2,128]{4,1,3,2,0:T(8,128)} fusion(f32[64,128,2,2,128]{4,1,3,2,0:T(8,128)} %broadcast_in_dim.66, s32[9]{0:T(128)S(1)} %fusion.67, f32[9,128,2,2,128]{4,1,3,2,0:T(8,128)} %pad_maximum_fusion), kind=kCustom, calls=%fused_computation | custom fusion | flops 589824 | bytes 7077924 | tf_op jit(solution)/shard_map/scatter-add | solution.py:104
  211.2 11.7 %copy.67 = f32[64,128,2,2,128]{4,1,0,3,2:T(8,128)} copy(f32[64,128,2,2,128]{4,1,3,2,0:T(8,128)} %scatter_fusion) | data formatting | bytes 33554432 | tf_op jit(solution)/shard_map/scatter-add | solution.py:104
  223.4 2.2 fusion.36
  226.5 183.0 %reduce-scatter.2.cloned.1.call-done = f32[128,2,2,128]{3,0,2,1:T(8,128)} async-done(((f32[8192,2,2,128]{3,0,2,1:T(8,128)}), f32[128,2,2,128]{3,0,2,1:T(8,128)}) %reduce-scatter.2.cloned.1.call-update) | async-done | bytes 262160 | tf_op jit(solution)/shard_map/reduce_scatter | solution.py:106
  409.5 1.6 multiply_reduce_fusion.1
  413.1 1.4 copy.68
  414.4 74.9 %psum.23 = f32[]{:T(128)} all-reduce(f32[]{:T(128)S(6)} %add.77), channel_id=1, replica_groups=mesh['branch'=64,'head'=4] {'branch','head'}, use_global_device_ids=true, to_apply=%region_15.16 | all-reduce | flops 1 | bytes 8 | tf_op jit(solution)/shard_map/psum | solution.py:119
  490.0 1.0 slice_bitcast_fusion.4
  (64 shorter events, 18.6 us)
Async XLA Ops:
  7.2 148.5 %all-gather.5.cloned.1.call-start = ((), (), s32[]{:S(2)}) async-start(), calls=%async_computation.2 | async-start | bytes 4259840 | tf_op jit(solution)/shard_map/all_gather | solution.py:30
  8.7 163.3 %all-gather.7.cloned.1.call-start = ((), (), s32[]{:S(2)}) async-start(), calls=%async_computation.3 | async-start | bytes 4259840 | tf_op jit(solution)/shard_map/all_gather | solution.py:31
  10.3 399.2 %reduce-scatter.2.cloned.1.call-start = ((), (), s32[]{:S(2)}) async-start(), calls=%async_computation.1 | async-start | bytes 17039360 | tf_op jit(solution)/shard_map/reduce_scatter | solution.py:106
  143.5 28.5 %copy-start.7 = (s32[1,8]{1,0:T(1,128)S(1)}, s32[1,8]{1,0:T(1,128)}, u32[]{:S(2)}) copy-start(s32[1,8]{1,0:T(1,128)} %param.14) | copy-start | bytes 100
  153.2 25.4 %copy-start.2 = (bf16[128,8,128]{2,1,0:T(8,128)(2,1)}, bf16[128,8,128]{2,1,0:T(8,128)(2,1)S(1)}, u32[]{:S(2)}) copy-start(bf16[128,8,128]{2,1,0:T(8,128)(2,1)S(1)} %get-tuple-element.18) | copy-start | bytes 786436
  155.6 23.8 %copy-start.4 = (pred[128,1152]{0,1:T(8,128)(4,1)}, pred[128,1152]{0,1:T(8,128)(4,1)S(1)}, u32[]{:S(2)}) copy-start(pred[128,1152]{0,1:T(8,128)(4,1)S(1)} %fusion.40) | copy-start | bytes 442372
  172.0 6.2 %copy-start.6 = (bf16[1,128,128]{2,0,1:T(2,128)(2,1)S(1)}, bf16[1,128,128]{2,0,1:T(2,128)(2,1)}, u32[]{:S(2)}) copy-start(bf16[1,128,128]{2,0,1:T(2,128)(2,1)} %copy.56) | copy-start | bytes 98308
  183.9 1.0 copy-start.3
  184.8 0.9 copy-start.1
  184.9 1.7 copy-start.5
  191.7 1.4 copy-start
Sparse Core Ops, SparseCore 0:
  11.4 80.8 all-gather.4
  95.6 76.3 all-gather.6
  223.0 186.4 reduce-scatter.1
where the time goes:
time: 502 us; the launch traced here: 500 us
  blocking collectives  201 us (40%)
  waiting for transfers between devices  194 us (39%)
  local copies, waits for them, and re-layouts  32.2 us (6%)
  other arithmetic  28.3 us (6%)
  matrix products  23.1 us (5%)
  between operations  21.5 us (4%)
    reduce_scatter x1, waiting for transfers between devices, local(): lax.psum_scatter(part_rows.reshape(row_count, 2, kv_here, head_dim), 'bra...  183 us
    psum x1, blocking collectives, local(): lax.psum((flags * reward, flags * (reward * reward)), 'branch')  126 us
    psum x1, blocking collectives, local(): total_squares = lax.psum(local_squares, ('branch', 'head'))  74.9 us
    scatter-add x1, local copies, waits for them, and re-layouts, local(): part_rows = jnp.zeros((blocks_here, rows_here, 2, kv_here, head_dim), jnp...  11.7 us
    dot_general x2, matrix products, select_blocks(): jnp.einsum('dn,ntgh->dtgh', chosen, pieces, preferred_element_type=jnp.fl...  11.5 us
    all_gather x1, waiting for transfers between devices, local(): lax.all_gather(values[None], 'branch', axis=0, tiled=True)  10.4 us
  transfers between devices with their start and end apart: 3, of which 2 were waited for; matrix products, arithmetic and copies ran while one was open for 5% of the time, Pallas kernels for 0%

commit v1 on v0

v1 whole, which is shorter than its diff:
```python
import math

import jax
import jax.numpy as jnp
from jax import lax
from jax.experimental import pallas as pl
from jax.experimental.pallas import tpu as pltpu
from jax.sharding import PartitionSpec as P

NY, NZ, NC = 4, 8, 2
NBLK = NY * NZ * NC
NHEAD = 4
GROUP = 4
DEPTH = 8
TOK = 128
HD = 128
KV = 2
RATIO = 8
LANES = 128
HALF = 8
ENTRIES = DEPTH + 1
CHUNK = 256
F32 = jnp.float32
BF16 = jnp.bfloat16
VMEM = pltpu.VMEM
SMEM = pltpu.SMEM
NT = (((1,), (1,)), ((), ()))
NN = (((1,), (0,)), ((), ()))
TN = (((0,), (0,)), ((), ()))


def index_of(y, z, c):
    return ((y % NY) * NZ + z % NZ) * NC + c % NC


def every():
    return [(y, z, c) for y in range(NY) for z in range(NZ) for c in range(NC)]


def along_y(x, step):
    pairs = [(index_of(y, z, c), index_of(y + step, z, c)) for y, z, c in every()]
    return lax.ppermute(x, "branch", pairs)


def other_core(x):
    pairs = [(index_of(y, z, c), index_of(y, z, c + 1)) for y, z, c in every()]
    return lax.ppermute(x, "branch", pairs)


def along_head(x, step):
    pairs = [(i, (i + step) % NHEAD) for i in range(NHEAD)]
    return lax.ppermute(x, "head", pairs)


def swap_z(x):
    groups = [[index_of(y, z, c) for z in range(NZ)] for y in range(NY) for c in range(NC)]
    return lax.all_to_all(x, "branch", 0, 0, axis_index_groups=groups, tiled=False)


def swap_yz(x):
    groups = [[index_of(y, z, c) for y in range(NY) for z in range(NZ)] for c in range(NC)]
    return lax.all_to_all(x, "branch", 0, 0, axis_index_groups=groups, tiled=False)


def call(body, outs, scratch=(), vmem_mb=32):
    return dict(
        out_shape=outs,
        scratch_shapes=list(scratch),
        compiler_params=pltpu.CompilerParams(vmem_limit_bytes=vmem_mb << 20),
    )


def in_vmem():
    return pl.BlockSpec(memory_space=VMEM)


def in_smem():
    return pl.BlockSpec(memory_space=SMEM)


def plan_kernel(pos, mine, other, picked, table, scale, index_v, index_s, sem):
    y, z, c = pos[0], pos[1], pos[2]
    own = y * NZ + z
    meta_m = mine[...].astype(F32)[:, 16:24, :]
    meta_o = other[...].astype(F32)[:, 16:24, :]
    lane = lax.broadcasted_iota(jnp.int32, (8, LANES), 1)
    lane_f = lane.astype(F32)
    is_block = lane < NBLK
    wide = lax.broadcasted_iota(jnp.int32, (NY * NZ, LANES), 1).astype(F32)
    hit = jnp.maximum(
        jnp.where(meta_m[:, 0, :] == wide, 1.0, 0.0), jnp.where(meta_o[:, 0, :] == wide, 1.0, 0.0)
    )
    inner = jnp.max(hit, axis=0, keepdims=True)
    inner = jnp.where(is_block, jnp.broadcast_to(inner, (8, LANES)), 0.0)
    before = (
        lax.broadcasted_iota(jnp.int32, (LANES, LANES), 0)
        < lax.broadcasted_iota(jnp.int32, (LANES, LANES), 1)
    ).astype(F32).astype(BF16)
    rank = lax.dot_general(inner.astype(BF16), before, NN, preferred_element_type=F32)
    row = lax.broadcasted_iota(jnp.int32, (8, LANES), 0)
    wanted = (row * 2 + c).astype(F32)
    chosen = jnp.where((rank == wanted) & (inner > 0.0), lane_f, 0.0)
    index = jnp.sum(chosen, axis=1, keepdims=True).astype(jnp.int32)
    index_v[...] = jnp.broadcast_to(index, (8, LANES))
    copy = pltpu.make_async_copy(index_v, index_s, sem)
    copy.start()
    for yy in range(NY):
        line = mine[yy * NZ + z].astype(F32)[16:24, :]
        same = (line == lane_f) & is_block
        slot = jnp.sum(jnp.where(same, rank + 1.0, 0.0), axis=1, keepdims=True) - 1.0
        table[yy * 8 : yy * 8 + 8, :] = jnp.broadcast_to(slot.astype(jnp.int32), (8, LANES))
    table[32:40, :] = jnp.where(inner > 0.0, rank, -1.0).astype(jnp.int32)
    here = mine[own].astype(F32)[16:24, :]
    group, reward = here[0:1, :], here[1:2, :]
    in_m = jnp.where(meta_m[:, 0, :] == group, meta_m[:, 1, :], 0.0)
    in_o = jnp.where(meta_o[:, 0, :] == group, meta_o[:, 1, :], 0.0)
    total = jnp.sum(in_m + in_o, axis=0, keepdims=True)
    squares = jnp.sum(in_m * in_m + in_o * in_o, axis=0, keepdims=True)
    mean = total / GROUP
    spread = jnp.sqrt(jnp.maximum(squares / GROUP - mean * mean, 0.25))
    advantage = (reward - mean) / spread
    advantage = jnp.sum(jnp.where(lane[0:1] == NBLK, advantage, 0.0), axis=1, keepdims=True)
    scale[...] = jnp.broadcast_to(advantage, (8, LANES))
    copy.wait()
    for s in range(HALF):
        block = index_s[s, 0]
        place = block // 2

        @pl.when(block % 2 == c)
        def _():
            picked[:, s] = jnp.broadcast_to(mine[place, 0:16, :][None], (NZ, 16, LANES))

        @pl.when(block % 2 != c)
        def _():
            picked[:, s] = jnp.broadcast_to(other[place, 0:16, :][None], (NZ, 16, LANES))


def plan(pos, mine, other):
    return pl.pallas_call(
        plan_kernel,
        in_specs=[in_smem(), in_vmem(), in_vmem()],
        out_specs=(in_vmem(), in_vmem(), in_vmem()),
        **call(
            plan_kernel,
            (
                jax.ShapeDtypeStruct((NZ, HALF, 16, LANES), BF16),
                jax.ShapeDtypeStruct((40, LANES), jnp.int32),
                jax.ShapeDtypeStruct((8, LANES), F32),
            ),
            [
                VMEM((8, LANES), jnp.int32),
                SMEM((8, LANES), jnp.int32),
                pltpu.SemaphoreType.DMA,
            ],
        ),
        name="plan",
    )(pos, mine, other)


def deal_kernel(pos, table, mine, other, *outs):
    y, c = pos[0], pos[2]
    for k in range(NY):
        target = lax.rem(y + k, NY)
        for d in range(DEPTH):
            slot = jnp.maximum(table[target * 8 + d, 0], 0)
            place = slot // 2

            @pl.when(slot % 2 == c)
            def _():
                outs[k][d] = mine[:, place]

            @pl.when(slot % 2 != c)
            def _():
                outs[k][d] = other[:, place]


def deal(pos, table, mine, other):
    return pl.pallas_call(
        deal_kernel,
        in_specs=[in_smem(), in_smem(), in_vmem(), in_vmem()],
        out_specs=(in_vmem(),) * NY,
        **call(deal_kernel, (jax.ShapeDtypeStruct((DEPTH, NZ, 16, LANES), BF16),) * NY),
        name="deal",
    )(pos, table, mine, other)


def attend_kernel(
    pos, table, scale, queries, cotangent, own_kv, a0, a1, a2, a3,
    query_grad, own_grad, c0, c1, c2, c3, squares,
    keys_all, values_all, q_all, g_all, key_sum, value_sum,
):
    y = pos[0]
    parts = (a0, a1, a2, a3)
    contribs = (c0, c1, c2, c3)
    factor = 1.0 / math.sqrt(HD)
    weight = scale[0:1, :]
    total = jnp.zeros((8, LANES), F32)
    for h in range(KV):
        keys_all[0:TOK, :] = own_kv[h]
        values_all[0:TOK, :] = own_kv[KV + h]
        for d in range(DEPTH):
            for k in range(NY):
                at = TOK * (d + 1) + 32 * k
                keys_all[at : at + 32, :] = parts[k][d, 2 * h : 2 * h + 2].reshape(32, LANES)
                values_all[at : at + 32, :] = parts[k][d, 4 + 2 * h : 6 + 2 * h].reshape(32, LANES)
        heads = slice(RATIO * h, RATIO * (h + 1))
        q_all[...] = queries[...].astype(F32)[:, heads, :].reshape(TOK * RATIO, HD).astype(BF16)
        g_all[...] = (
            (cotangent[...].astype(F32)[:, heads, :] * weight[None])
            .reshape(TOK * RATIO, HD)
            .astype(BF16)
        )
        for step in range(TOK * RATIO // CHUNK):
            rows = slice(step * CHUNK, (step + 1) * CHUNK)
            q, g = q_all[rows, :], g_all[rows, :]
            scores = []
            for d in range(ENTRIES):
                s = lax.dot_general(
                    keys_all[d * TOK : (d + 1) * TOK, :], q, NT, preferred_element_type=F32
                ) * factor
                if d == 0:
                    key_pos = lax.broadcasted_iota(jnp.int32, (TOK, CHUNK), 0)
                    query_pos = step * (CHUNK // RATIO) + lax.broadcasted_iota(
                        jnp.int32, (TOK, CHUNK), 1
                    ) // RATIO
                    s = jnp.where(key_pos <= query_pos, s, -1e30)
                else:
                    s = jnp.where(table[y * 8 + d - 1, 0] >= 0, s, -1e30)
                scores.append(s)
            top = scores[0]
            for s in scores[1:]:
                top = jnp.maximum(top, s)
            top = jnp.max(top, axis=0, keepdims=True)
            exps = [jnp.exp(s - top) for s in scores]
            norm = exps[0]
            for e in exps[1:]:
                norm = norm + e
            norm = 1.0 / jnp.sum(norm, axis=0, keepdims=True)
            probs = [e * norm for e in exps]
            lows = [p.astype(BF16) for p in probs]
            pgs = [
                lax.dot_general(
                    values_all[d * TOK : (d + 1) * TOK, :], g, NT, preferred_element_type=F32
                )
                for d in range(ENTRIES)
            ]
            delta = lows[0].astype(F32) * pgs[0]
            for d in range(1, ENTRIES):
                delta = delta + lows[d].astype(F32) * pgs[d]
            delta = jnp.sum(delta, axis=0, keepdims=True)
            dscores = [(probs[d] * (pgs[d] - delta)).astype(BF16) for d in range(ENTRIES)]
            low = jnp.concatenate(lows, 0)
            ds = jnp.concatenate(dscores, 0)
            value_part = lax.dot_general(low, g, NN, preferred_element_type=F32)
            key_part = lax.dot_general(ds, q, NN, preferred_element_type=F32)
            if step == 0:
                value_sum[...] = value_part
                key_sum[...] = key_part
            else:
                value_sum[...] += value_part
                key_sum[...] += key_part
            dq = lax.dot_general(ds, keys_all[...], TN, preferred_element_type=F32) * factor
            total = total + jnp.sum((dq * dq).reshape(CHUNK // 8, 8, HD), axis=0)
            toks = slice(step * (CHUNK // RATIO), (step + 1) * (CHUNK // RATIO))
            query_grad[toks, heads, :] = dq.reshape(CHUNK // RATIO, RATIO, HD)
        own_grad[h] = key_sum[0:TOK, :] * factor
        own_grad[KV + h] = value_sum[0:TOK, :]
        for k in range(NY):
            for d in range(DEPTH):
                at = TOK * (d + 1) + 32 * k
                contribs[k][d, 2 * h : 2 * h + 2] = (
                    (key_sum[at : at + 32, :] * factor).astype(BF16).reshape(2, 16, LANES)
                )
                contribs[k][d, 4 + 2 * h : 6 + 2 * h] = (
                    value_sum[at : at + 32, :].astype(BF16).reshape(2, 16, LANES)
                )
    for k in range(NY):
        piece = lax.rem(y + NY - k, NY)
        for kind in range(2):
            for h in range(KV):
                for half in range(2):
                    rows = pl.ds(pl.multiple_of(half * 64 + piece * 16, 16), 16)
                    contribs[k][DEPTH, kind * 4 + h * 2 + half] = own_grad[kind * 2 + h, rows, :].astype(BF16)
    squares[...] = total


def attend(pos, table, scale, queries, cotangent, own_kv, parts):
    rows = TOK * RATIO
    keys = TOK * ENTRIES
    return pl.pallas_call(
        attend_kernel,
        in_specs=[in_smem(), in_smem()] + [in_vmem()] * 8,
        out_specs=(in_vmem(),) * 7,
        **call(
            attend_kernel,
            (
                jax.ShapeDtypeStruct((TOK, KV * RATIO, HD), F32),
                jax.ShapeDtypeStruct((2 * KV, TOK, HD), F32),
            )
            + (jax.ShapeDtypeStruct((ENTRIES, NZ, 16, LANES), BF16),) * NY
            + (jax.ShapeDtypeStruct((8, LANES), F32),),
            [
                VMEM((keys, HD), BF16),
                VMEM((keys, HD), BF16),
                VMEM((rows, HD), BF16),
                VMEM((rows, HD), BF16),
                VMEM((keys, HD), F32),
                VMEM((keys, HD), F32),
            ],
            vmem_mb=48,
        ),
        name="attend",
    )(pos, table, scale, queries, cotangent, own_kv, *parts)


def gather_kernel(pos, table, r0, r1, r2, r3, keep, send, acc):
    y, z, c = pos[0], pos[1], pos[2]
    acc[...] = jnp.zeros_like(acc)
    for k, r in enumerate((r0, r1, r2, r3)):
        source = lax.rem(y + k, NY)
        for d in range(ENTRIES):
            if d < DEPTH:
                slot = table[source * 8 + d, 0]
            else:
                slot = table[32, (source * NZ + z) * NC + c]

            @pl.when(slot >= 0)
            def _():
                acc[slot % 2, slot // 2] += r[d].astype(F32)

    for s in range(HALF):
        keep[:, s] = acc[c, s]
        send[:, s] = acc[1 - c, s].astype(BF16)


def gather(pos, table, parts):
    return pl.pallas_call(
        gather_kernel,
        in_specs=[in_smem(), in_smem()] + [in_vmem()] * NY,
        out_specs=(in_vmem(), in_vmem()),
        **call(
            gather_kernel,
            (
                jax.ShapeDtypeStruct((NZ, HALF, 16, LANES), F32),
                jax.ShapeDtypeStruct((NZ, HALF, 16, LANES), BF16),
            ),
            [VMEM((2, HALF, NZ, 16, LANES), F32)],
        ),
        name="combine",
    )(pos, table, *parts)


def total_kernel(pos, table, parts, own_grad, squares, sums, pack):
    b = pos[3]
    sums_now = parts[0].astype(F32)
    for z in range(1, NZ):
        sums_now = sums_now + parts[z].astype(F32)
    pack[0:HALF] = sums_now.astype(BF16)
    own = own_grad[...]
    own_sq = jnp.sum((own * own).reshape(2 * KV * TOK // 8, 8, LANES), axis=0)
    leaf = table[32, b] < 0
    tile = squares[...] + jnp.where(leaf, own_sq, 0.0)
    tile = tile + jnp.sum((sums_now * sums_now).reshape(HALF * 2, 8, LANES), axis=0)
    value = jnp.sum(jnp.sum(tile, axis=0, keepdims=True), axis=1, keepdims=True)
    value = jnp.broadcast_to(value, (8, LANES))
    sums[...] = value
    pack[HALF] = split_rows(value, 16)


def split_rows(value, rows):
    high = value.astype(BF16).astype(F32)
    middle = (value - high).astype(BF16).astype(F32)
    low = value - high - middle
    row = lax.broadcasted_iota(jnp.int32, (8, LANES), 0)
    tile = jnp.where(row == 0, high, jnp.where(row == 1, middle, jnp.where(row == 2, low, 0.0)))
    if rows > 8:
        tile = jnp.concatenate([tile, jnp.zeros((rows - 8, LANES), F32)], 0)
    return tile.astype(BF16)


def total_of(pos, table, parts, own_grad, squares):
    return pl.pallas_call(
        total_kernel,
        in_specs=[in_smem(), in_smem()] + [in_vmem()] * 3,
        out_specs=(in_vmem(), in_vmem()),
        **call(
            total_kernel,
            (
                jax.ShapeDtypeStruct((8, LANES), F32),
                jax.ShapeDtypeStruct((HALF + 1, 16, LANES), BF16),
            ),
        ),
        name="total",
    )(pos, table, parts, own_grad, squares)


def route_kernel(pos, table, sums, mine, other, out):
    c = pos[2]
    tail = other[HALF].astype(F32)[0:8, :]
    value = sums[...] + jnp.sum(tail, axis=0, keepdims=True)
    rows = split_rows(value, 8).astype(F32)
    for place in range(NY * NZ):
        slot = table[32, place * NC + c]
        at = jnp.maximum(slot, 0) // 2
        picked = jnp.where(slot % 2 == c, mine[at].astype(F32), other[at].astype(F32))
        out[place] = jnp.concatenate([picked, rows], 0).astype(BF16)


def route(pos, table, sums, mine, other):
    return pl.pallas_call(
        route_kernel,
        in_specs=[in_smem(), in_smem()] + [in_vmem()] * 3,
        out_specs=in_vmem(),
        **call(route_kernel, jax.ShapeDtypeStruct((NY * NZ, 24, LANES), BF16)),
        name="route",
    )(pos, table, sums, mine, other)


def finish_kernel(pos, table, arrived, own_grad, grads, sums):
    b = pos[3]
    inner = table[32, b] >= 0

    @pl.when(inner)
    def _():
        for z in range(NZ):
            kind_head, half = z // 2, z % 2
            for y in range(NY):
                at = half * 64 + y * 16
                grads[kind_head, at : at + 16, :] = arrived[y * NZ + z, 0:16, :].astype(F32)

    @pl.when(jnp.logical_not(inner))
    def _():
        grads[...] = own_grad[...]

    tails = jnp.sum(arrived[...].astype(F32)[:, 16:24, :], axis=0)
    sums[...] = jnp.broadcast_to(jnp.sum(tails, axis=0, keepdims=True), (8, LANES))


def finish(pos, table, arrived, own_grad):
    return pl.pallas_call(
        finish_kernel,
        in_specs=[in_smem(), in_smem(), in_vmem(), in_vmem()],
        out_specs=(in_vmem(), in_vmem()),
        **call(
            finish_kernel,
            (
                jax.ShapeDtypeStruct((2 * KV, TOK, HD), F32),
                jax.ShapeDtypeStruct((8, LANES), F32),
            ),
        ),
        name="finish",
    )(pos, table, arrived, own_grad)


def local(queries, keys, values, cotangent, rewards, groups, ancestors, step_ids):
    b = lax.axis_index("branch")
    pos = jnp.stack([b // (NZ * NC), (b // NC) % NZ, b % NC, b]).astype(jnp.int32)
    own_kv = jnp.stack([keys, values]).transpose(0, 2, 1, 3)
    pieces = (
        own_kv.reshape(2, KV, 2, NY, 16, HD).transpose(3, 0, 1, 2, 4, 5).reshape(NY * NZ, 16, HD)
    )
    own_kv = own_kv.reshape(2 * KV, TOK, HD)
    line = jnp.broadcast_to(ancestors[0].astype(BF16)[:, None], (8, NBLK))
    facts = jnp.concatenate(
        [groups.astype(BF16), rewards, jnp.zeros((6,), BF16)]
    )
    meta = jnp.concatenate([line, jnp.broadcast_to(facts[:, None], (8, LANES - NBLK))], 1)
    packet = jnp.concatenate([pieces, jnp.broadcast_to(meta[None], (NY * NZ, 8, LANES))], 1)
    mine = swap_yz(packet)
    other = other_core(mine)
    trained = (step_ids[0] % 2 == 0)[:, None, None]
    masked = jnp.where(trained, cotangent, jnp.zeros_like(cotangent))
    picked, table, scale = plan(pos, mine, other)
    column = swap_z(picked)
    column_other = other_core(column)
    dealt = deal(pos, table, column, column_other)
    parts = [dealt[0]] + [along_y(dealt[k], k) for k in (1, 2, 3)]
    query_grad, own_grad, c0, c1, c2, c3, squares = attend(
        pos, table, scale, queries, masked, own_kv, parts
    )
    back = [c0] + [along_y(x, -k) for k, x in ((1, c1), (2, c2), (3, c3))]
    keep, send = gather(pos, table, back)
    halves = (keep + other_core(send).astype(F32)).astype(BF16)
    sums, pack = total_of(pos, table, swap_z(halves), own_grad, squares)
    packet_back = route(pos, table, sums, pack, other_core(pack))
    grads, sums = finish(pos, table, swap_yz(packet_back), own_grad)
    mine_sum = sums[0:1, :]
    all_sum = mine_sum
    for k in (1, 2, 3):
        all_sum = all_sum + along_head(mine_sum, k)
    count = float(NBLK * TOK * NHEAD * (KV * RATIO + 2 * KV) * HD)
    grad_rms = jnp.sqrt(all_sum[0, 0] / count)
    out = grads.reshape(2, KV, TOK, HD).transpose(0, 2, 1, 3)
    return query_grad, out[0], out[1], grad_rms


def solution(mesh):
    in_specs = (
        P("branch", "head", None),
        P("branch", "head", None),
        P("branch", "head", None),
        P("branch", "head", None),
        P("branch"),
        P("branch"),
        P("branch", None),
        P("branch", None),
    )
    out_specs = (
        P("branch", "head", None),
        P("branch", "head", None),
        P("branch", "head", None),
        P(),
    )
    return jax.shard_map(local, mesh=mesh, in_specs=in_specs, out_specs=out_specs, check_vma=False)
```

time: 502 us -> 142 us (0.28)
  waiting for transfers between devices: 194 us -> 35.2 us
  blocking collectives: 201 us -> 67.1 us
  local copies, waits for them, and re-layouts: 32.2 us -> 1.16 us
  other arithmetic: 28.3 us -> 1.79 us
  matrix products: 23.1 us -> 0 us
  Pallas kernels: 0 us -> 19.9 us
  between operations: 21.5 us -> 3.35 us
  starting transfers between devices: 0.12 us -> 12.8 us
    psum x2 -> x0, blocking collectives: 201 us -> none  [the longest x1 126 us: local(): lax.psum((flags * reward, flags * (reward * reward)), 'branch')]
    reduce_scatter x1 -> x0, waiting for transfers between devices: 183 us -> none  [local(): lax.psum_scatter(part_rows.reshape(row_count, 2, kv_here, head_dim), 'bra...]
    all_to_all x0 -> x4, blocking collectives: none -> 67.1 us  [the longest x2 37.9 us: swap_yz(): lax.all_to_all(x, 'branch', 0, 0, axis_index_groups=groups, tiled=False)]
    ppermute x0 -> x13, waiting for transfers between devices: none -> 35.2 us  [the longest x6 26.7 us: along_y(): return lax.ppermute(x, 'branch', pairs)]
    dot_general x14 -> x0, matrix products: 23.1 us -> none  [the longest x2 11.5 us: select_blocks(): jnp.einsum('dn,ntgh->dtgh', chosen, pieces, preferred_element_type=jnp.fl...]
    pallas_call x0 -> x7, Pallas kernels: none -> 19.9 us  [the longest x1 12.2 us: attend(): pl.pallas_call(attend_kernel, in_specs=[in_smem(), in_smem()] + [in_vmem(...]
    ppermute x0 -> x13, starting transfers between devices: none -> 12.8 us  [the longest x6 7.54 us: along_y(): return lax.ppermute(x, 'branch', pairs)]
    scatter-add x1 -> x0, local copies, waits for them, and re-layouts: 11.7 us -> none  [local(): part_rows = jnp.zeros((blocks_here, rows_here, 2, kv_here, head_dim), jnp...]
  transfers between devices with their start and end apart: 3 -> 13, of which waited for: 2 -> 10; matrix products, arithmetic and copies ran while one was open for 5% -> 1% of each run, Pallas kernels for 0% -> 0%
where the time goes in v1:
time: 142 us; the launch traced here: 141 us
  blocking collectives  67.1 us (47%)
  waiting for transfers between devices  35.2 us (25%)
  Pallas kernels  19.9 us (14%)
  starting transfers between devices  12.8 us (9%)
  between operations  3.35 us (2%)
  other arithmetic  1.79 us (1%)
    all_to_all x2, blocking collectives, swap_yz(): lax.all_to_all(x, 'branch', 0, 0, axis_index_groups=groups, tiled=False)  37.9 us
    all_to_all x2, blocking collectives, swap_z(): lax.all_to_all(x, 'branch', 0, 0, axis_index_groups=groups, tiled=False)  29.1 us
    ppermute x6, waiting for transfers between devices, along_y(): return lax.ppermute(x, 'branch', pairs)  26.7 us
    pallas_call x1, Pallas kernels, attend(): pl.pallas_call(attend_kernel, in_specs=[in_smem(), in_smem()] + [in_vmem(...  12.2 us
    ppermute x6, starting transfers between devices, along_y(): return lax.ppermute(x, 'branch', pairs)  7.54 us
    ppermute x4, waiting for transfers between devices, other_core(): return lax.ppermute(x, 'branch', pairs)  5.6 us
    ppermute x3, starting transfers between devices, along_head(): return lax.ppermute(x, 'head', pairs)  5.15 us
    ppermute x3, waiting for transfers between devices, along_head(): return lax.ppermute(x, 'head', pairs)  2.93 us
  transfers between devices with their start and end apart: 13, of which 10 were waited for; matrix products, arithmetic and copies ran while one was open for 1% of the time, Pallas kernels for 0%

profile of v1, /device:TPU:32, one launch (start us, length us, event | category | flops | bytes accessed | tf_op | source)
XLA Modules:
  0.0 141.2 jit_solution(5719959594386707171)
XLA Ops:
  2.0 1.1 pad_maximum_fusion.1
  3.4 22.1 %all_to_all.20.mine = bf16[32,24,128]{2,1,0:T(8,128)(2,1)S(1)} all-to-all(bf16[32,24,128]{2,1,0:T(8,128)(2,1)S(1)} %pad_maximum_fusion), channel_id=1, replica_groups={{0,8,16,24,32,40,48,56,64,72,80,88,96,104,112,120,128,136,144,152,160,1..., dimensions={0} | all-to-all | bytes 393216 | tf_op jit(solution)/shard_map/all_to_all | solution.py:62
  25.7 1.4 collective-permute-done.other
  27.0 1.6 %plan.1 = (bf16[8,8,16,128]{3,2,1,0:T(8,128)(2,1)S(1)}, s32[40,128]{1,0:T(8,128)S(1)}, f32[8,128]{1,0:T(8,128)S(1)}) custom-call(s32[4]{0:T(128)S(1)} %pad_add_fusion.pos, bf16[32,24,128]{2,1,0:T(8,128)(2,1)S(1)} %all_to_all.20.mine, bf16[32,24,128]{2,1,0:T(8,128)(2,1)S(1)} %collective-permute-done.other), custom_call_target="tpu_custom_call" | custom-call | tf_op jit(solution)/shard_map/plan/pallas_call | solution.py:139
  28.6 14.2 %all_to_all.21.mine = bf16[8,8,16,128]{3,2,1,0:T(8,128)(2,1)S(1)} all-to-all(bf16[8,8,16,128]{3,2,1,0:T(8,128)(2,1)S(1)} %get-tuple-element.26), channel_id=1, replica_groups={{0,8,16,24,32,40,48,56},{4,12,20,28,36,44,52,60},{64,72,80,88,96,104,11..., dimensions={0} | all-to-all | bytes 524288 | tf_op jit(solution)/shard_map/all_to_all | solution.py:57
  42.8 1.5 %collective-permute-done.1.other = bf16[8,8,16,128]{3,2,1,0:T(8,128)(2,1)S(1)} collective-permute-done((bf16[8,8,16,128]{3,2,1,0:T(8,128)(2,1)S(1)}, bf16[8,8,16,128]{3,2,1,0:T(8,128)(2,1)S(1)}, u32[]{:S(2)}, u32[]{:S(2)}) %collective-permute-start.1) | collective-permute-done | bytes 262176 | tf_op jit(solution)/shard_map/ppermute | solution.py:47
  44.4 1.5 %deal.1 = (bf16[8,8,16,128]{3,2,1,0:T(8,128)(2,1)S(1)}, bf16[8,8,16,128]{3,2,1,0:T(8,128)(2,1)S(1)}, bf16[8,8,16,128]{3,2,1,0:T(8,128)(2,1)S(1)}, bf16[8,8,16,128]{3,2,1,0:T(8,128)(2,1)S(1)}) custom-call(s32[4]{0:T(128)S(1)} %pad_add_fusion.pos, s32[40,128]{1,0:T(8,128)S(1)} %get-tuple-element.24.table, bf16[8,8,16,128]{3,2,1,0:T(8,128)(2,1)S(1)} %all_to_all.21.mine, ...), custom_call_target="tpu_custom_call" | custom-call | tf_op jit(solution)/shard_map/deal/pallas_call | solution.py:178
  46.6 2.0 %collective-permute-start.3 = (bf16[8,8,16,128]{3,2,1,0:T(8,128)(2,1)S(1)}, bf16[8,8,16,128]{3,2,1,0:T(8,128)(2,1)S(1)}, u32[]{:S(2)}, u32[]{:S(2)}) collective-permute-start(bf16[8,8,16,128]{3,2,1,0:T(8,128)(2,1)S(1)} %get-tuple-element.29), channel_id=1, source_target_pairs={{0,128},{4,132},{8,136},{12,140},{16,144},{20,148},{24,152},{28,15... | collective-permute-start | bytes 786440 | tf_op jit(solution)/shard_map/ppermute | solution.py:42
  48.6 1.3 collective-permute-start.4
  50.4 10.7 %collective-permute-done.2.a1 = bf16[8,8,16,128]{3,2,1,0:T(8,128)(2,1)S(1)} collective-permute-done((bf16[8,8,16,128]{3,2,1,0:T(8,128)(2,1)S(1)}, bf16[8,8,16,128]{3,2,1,0:T(8,128)(2,1)S(1)}, u32[]{:S(2)}, u32[]{:S(2)}) %collective-permute-start.2) | collective-permute-done | bytes 262176 | tf_op jit(solution)/shard_map/ppermute | solution.py:42
  61.7 12.2 %attend.1 = (f32[128,16,128]{2,1,0:T(8,128)}, f32[4,128,128]{2,1,0:T(8,128)S(1)}, bf16[9,8,16,128]{3,2,1,0:T(8,128)(2,1)S(1)}, bf16[9,8,16,128]{3,2,1,0:T(8,128)...) custom-call(s32[4]{0:T(128)S(1)} %pad_add_fusion.pos, ...), custom_call_target="tpu_custom_call" | custom-call | tf_op jit(solution)/shard_map/attend/pallas_call | solution.py:290
  73.9 2.6 %collective-permute-start.5 = (bf16[9,8,16,128]{3,2,1,0:T(8,128)(2,1)S(1)}, bf16[9,8,16,128]{3,2,1,0:T(8,128)(2,1)S(1)}, u32[]{:S(2)}, u32[]{:S(2)}) collective-permute-start(bf16[9,8,16,128]{3,2,1,0:T(8,128)(2,1)S(1)} %get-tuple-element.33), channel_id=1, source_target_pairs={{0,192},{4,196},{8,200},{12,204},{16,208},{20,212},{24,216},{28,22... | collective-permute-start | bytes 884744 | tf_op jit(solution)/shard_map/ppermute | solution.py:42
  77.4 11.9 %collective-permute-done.5.r1 = bf16[9,8,16,128]{3,2,1,0:T(8,128)(2,1)S(1)} collective-permute-done((bf16[9,8,16,128]{3,2,1,0:T(8,128)(2,1)S(1)}, bf16[9,8,16,128]{3,2,1,0:T(8,128)(2,1)S(1)}, u32[]{:S(2)}, u32[]{:S(2)}) %collective-permute-start.5) | collective-permute-done | bytes 294944 | tf_op jit(solution)/shard_map/ppermute | solution.py:42
  89.4 3.4 %collective-permute-done.7.r3 = bf16[9,8,16,128]{3,2,1,0:T(8,128)(2,1)S(1)} collective-permute-done((bf16[9,8,16,128]{3,2,1,0:T(8,128)(2,1)S(1)}, bf16[9,8,16,128]{3,2,1,0:T(8,128)(2,1)S(1)}, u32[]{:S(2)}, u32[]{:S(2)}) %collective-permute-start.7) | collective-permute-done | bytes 294944 | tf_op jit(solution)/shard_map/ppermute | solution.py:42
  92.8 1.4 %combine.1 = (f32[8,8,16,128]{3,2,1,0:T(8,128)S(1)}, bf16[8,8,16,128]{3,2,1,0:T(8,128)(2,1)S(1)}) custom-call(s32[4]{0:T(128)S(1)} %pad_add_fusion.pos, s32[40,128]{1,0:T(8,128)S(1)} %get-tuple-element.24.table, bf16[9,8,16,128]{3,2,1,0:T(8,128)(2,1)S(1)} %get-tuple-element.32.r0, bf16[9,8,16,128]{3,2,1,0:T(8,128)(2,1)S(1)} %collective-permute-done.5.r1, ...), custom_call_target="tpu_custom_call" | custom-call | tf_op jit(solution)/shard_map/combine/pallas_call | solution.py:337
  94.3 1.5 %collective-permute-done.8 = bf16[8,8,16,128]{3,2,1,0:T(8,128)(2,1)S(1)} collective-permute-done((bf16[8,8,16,128]{3,2,1,0:T(8,128)(2,1)S(1)}, bf16[8,8,16,128]{3,2,1,0:T(8,128)(2,1)S(1)}, u32[]{:S(2)}, u32[]{:S(2)}) %collective-permute-start.8) | collective-permute-done | bytes 262176 | tf_op jit(solution)/shard_map/ppermute | solution.py:47
  95.9 14.9 %all_to_all.22.parts = bf16[8,8,16,128]{3,2,1,0:T(8,128)(2,1)S(1)} all-to-all(bf16[8,8,16,128]{3,2,1,0:T(8,128)(2,1)S(1)} %add_convert_fusion), channel_id=1, replica_groups={{0,8,16,24,32,40,48,56},{4,12,20,28,36,44,52,60},{64,72,80,88,96,104,11..., dimensions={0} | all-to-all | bytes 524288 | tf_op jit(solution)/shard_map/all_to_all | solution.py:57
  110.8 1.1 total.1
  111.9 1.2 collective-permute-done.9.other
  113.1 1.1 route.1
  114.2 15.8 %all_to_all.23.arrived = bf16[32,24,128]{2,1,0:T(8,128)(2,1)S(1)} all-to-all(bf16[32,24,128]{2,1,0:T(8,128)(2,1)S(1)} %route.1), channel_id=1, replica_groups={{0,8,16,24,32,40,48,56,64,72,80,88,96,104,112,120,128,136,144,152,160,1..., dimensions={0} | all-to-all | bytes 393216 | tf_op jit(solution)/shard_map/all_to_all | solution.py:62
  131.0 3.1 %collective-permute-start.11 = (f32[1,128]{1,0:T(1,128)S(1)}, f32[1,128]{1,0:T(1,128)S(1)}, u32[]{:S(2)}, u32[]{:S(2)}) collective-permute-start(f32[1,128]{1,0:T(1,128)S(1)} %slice.14), channel_id=1, source_target_pairs={{0,2},{1,3},{2,0},{3,1},{4,6},{5,7},{6,4},{7,5},{8,10},{9,11},{10,... | collective-permute-start | bytes 1544 | tf_op jit(solution)/shard_map/ppermute | solution.py:52
  134.1 1.1 collective-permute-start.12
  137.7 2.3 %collective-permute-done.10 = f32[1,128]{1,0:T(1,128)S(1)} collective-permute-done((f32[1,128]{1,0:T(1,128)S(1)}, f32[1,128]{1,0:T(1,128)S(1)}, u32[]{:S(2)}, u32[]{:S(2)}) %collective-permute-start.10) | collective-permute-done | bytes 544 | tf_op jit(solution)/shard_map/ppermute | solution.py:52
  (45 shorter events, 6.6 us)
Async XLA Ops:
  1.3 0.7 copy-start.4
  25.6 1.4 %collective-permute-start = (bf16[32,24,128]{2,1,0:T(8,128)(2,1)S(1)}, bf16[32,24,128]{2,1,0:T(8,128)(2,1)S(1)}, u32[]{:S(2)}, u32[]{:S(2)}) collective-permute-start(bf16[32,24,128]{2,1,0:T(8,128)(2,1)S(1)} %all_to_all.20.mine), channel_id=1, source_target_pairs={{0,4},{4,0},{8,12},{12,8},{16,20},{20,16},{24,28},{28,24},{32,36},... | collective-permute-start | bytes 589832 | tf_op jit(solution)/shard_map/ppermute | solution.py:47
  28.6 14.2 %copy-start.5 = (s32[1,128]{1,0:T(1,128)S(1)}, s32[1,128]{1,0:T(1,128)}, u32[]{:S(2)}) copy-start(s32[1,128]{1,0:T(1,128)} %param.15) | copy-start | bytes 1540
  28.6 21.3 %copy-start.2 = (bf16[128,2,128]{2,1,0:T(2,128)(2,1)S(1)}, bf16[128,2,128]{2,1,0:T(2,128)(2,1)}, u32[]{:S(2)}) copy-start(bf16[128,2,128]{2,1,0:T(2,128)(2,1)} %param.10) | copy-start | bytes 196612
  28.6 21.3 %copy-start.3 = (bf16[128,2,128]{2,1,0:T(2,128)(2,1)S(1)}, bf16[128,2,128]{2,1,0:T(2,128)(2,1)}, u32[]{:S(2)}) copy-start(bf16[128,2,128]{2,1,0:T(2,128)(2,1)} %param.9) | copy-start | bytes 196612
  42.8 1.5 %collective-permute-start.1 = (bf16[8,8,16,128]{3,2,1,0:T(8,128)(2,1)S(1)}, bf16[8,8,16,128]{3,2,1,0:T(8,128)(2,1)S(1)}, u32[]{:S(2)}, u32[]{:S(2)}) collective-permute-start(bf16[8,8,16,128]{3,2,1,0:T(8,128)(2,1)S(1)} %all_to_all.21.mine), channel_id=1, source_target_pairs={{0,4},{4,0},{8,12},{12,8},{16,20},{20,16},{24,28},{28,24},{32,36},... | collective-permute-start | bytes 786440 | tf_op jit(solution)/shard_map/ppermute | solution.py:47
  44.4 5.8 %copy-start.1 = (bf16[128,16,128]{2,1,0:T(8,128)(2,1)S(1)}, bf16[128,16,128]{2,1,0:T(8,128)(2,1)}, u32[]{:S(2)}) copy-start(bf16[128,16,128]{2,1,0:T(8,128)(2,1)} %param.11) | copy-start | bytes 1572868
  45.9 15.2 %collective-permute-start.2 = (bf16[8,8,16,128]{3,2,1,0:T(8,128)(2,1)S(1)}, bf16[8,8,16,128]{3,2,1,0:T(8,128)(2,1)S(1)}, u32[]{:S(2)}, u32[]{:S(2)}) collective-permute-start(bf16[8,8,16,128]{3,2,1,0:T(8,128)(2,1)S(1)} %get-tuple-element.28), channel_id=1, source_target_pairs={{0,64},{4,68},{8,72},{12,76},{16,80},{20,84},{24,88},{28,92},{32,9... | collective-permute-start | bytes 786440 | tf_op jit(solution)/shard_map/ppermute | solution.py:42
  46.6 14.5 %collective-permute-start.3 = (bf16[8,8,16,128]{3,2,1,0:T(8,128)(2,1)S(1)}, bf16[8,8,16,128]{3,2,1,0:T(8,128)(2,1)S(1)}, u32[]{:S(2)}, u32[]{:S(2)}) collective-permute-start(bf16[8,8,16,128]{3,2,1,0:T(8,128)(2,1)S(1)} %get-tuple-element.29), channel_id=1, source_target_pairs={{0,128},{4,132},{8,136},{12,140},{16,144},{20,148},{24,152},{28,15... | collective-permute-start | bytes 786440 | tf_op jit(solution)/shard_map/ppermute | solution.py:42
  48.6 13.1 %collective-permute-start.4 = (bf16[8,8,16,128]{3,2,1,0:T(8,128)(2,1)S(1)}, bf16[8,8,16,128]{3,2,1,0:T(8,128)(2,1)S(1)}, u32[]{:S(2)}, u32[]{:S(2)}) collective-permute-start(bf16[8,8,16,128]{3,2,1,0:T(8,128)(2,1)S(1)} %get-tuple-element.30), channel_id=1, source_target_pairs={{0,192},{4,196},{8,200},{12,204},{16,208},{20,212},{24,216},{28,22... | collective-permute-start | bytes 786440 | tf_op jit(solution)/shard_map/ppermute | solution.py:42
  50.1 11.6 %copy-start = (bf16[128,16,128]{2,1,0:T(8,128)(2,1)S(1)}, bf16[128,16,128]{2,1,0:T(8,128)(2,1)}, u32[]{:S(2)}) copy-start(bf16[128,16,128]{2,1,0:T(8,128)(2,1)} %queries.1) | copy-start | bytes 1572868
  73.9 15.4 %collective-permute-start.5 = (bf16[9,8,16,128]{3,2,1,0:T(8,128)(2,1)S(1)}, bf16[9,8,16,128]{3,2,1,0:T(8,128)(2,1)S(1)}, u32[]{:S(2)}, u32[]{:S(2)}) collective-permute-start(bf16[9,8,16,128]{3,2,1,0:T(8,128)(2,1)S(1)} %get-tuple-element.33), channel_id=1, source_target_pairs={{0,192},{4,196},{8,200},{12,204},{16,208},{20,212},{24,216},{28,22... | collective-permute-start | bytes 884744 | tf_op jit(solution)/shard_map/ppermute | solution.py:42
  76.6 12.8 %collective-permute-start.6 = (bf16[9,8,16,128]{3,2,1,0:T(8,128)(2,1)S(1)}, bf16[9,8,16,128]{3,2,1,0:T(8,128)(2,1)S(1)}, u32[]{:S(2)}, u32[]{:S(2)}) collective-permute-start(bf16[9,8,16,128]{3,2,1,0:T(8,128)(2,1)S(1)} %get-tuple-element.34), channel_id=1, source_target_pairs={{0,128},{4,132},{8,136},{12,140},{16,144},{20,148},{24,152},{28,15... | collective-permute-start | bytes 884744 | tf_op jit(solution)/shard_map/ppermute | solution.py:42
  76.7 16.1 %collective-permute-start.7 = (bf16[9,8,16,128]{3,2,1,0:T(8,128)(2,1)S(1)}, bf16[9,8,16,128]{3,2,1,0:T(8,128)(2,1)S(1)}, u32[]{:S(2)}, u32[]{:S(2)}) collective-permute-start(bf16[9,8,16,128]{3,2,1,0:T(8,128)(2,1)S(1)} %get-tuple-element.35), channel_id=1, source_target_pairs={{0,64},{4,68},{8,72},{12,76},{16,80},{20,84},{24,88},{28,92},{32,9... | collective-permute-start | bytes 884744 | tf_op jit(solution)/shard_map/ppermute | solution.py:42
  94.2 1.6 %collective-permute-start.8 = (bf16[8,8,16,128]{3,2,1,0:T(8,128)(2,1)S(1)}, bf16[8,8,16,128]{3,2,1,0:T(8,128)(2,1)S(1)}, u32[]{:S(2)}, u32[]{:S(2)}) collective-permute-start(bf16[8,8,16,128]{3,2,1,0:T(8,128)(2,1)S(1)} %get-tuple-element.37), channel_id=1, source_target_pairs={{0,4},{4,0},{8,12},{12,8},{16,20},{20,16},{24,28},{28,24},{32,36},... | collective-permute-start | bytes 786440 | tf_op jit(solution)/shard_map/ppermute | solution.py:47
  111.9 1.2 collective-permute-start.9
  131.0 6.1 %collective-permute-start.11 = (f32[1,128]{1,0:T(1,128)S(1)}, f32[1,128]{1,0:T(1,128)S(1)}, u32[]{:S(2)}, u32[]{:S(2)}) collective-permute-start(f32[1,128]{1,0:T(1,128)S(1)} %slice.14), channel_id=1, source_target_pairs={{0,2},{1,3},{2,0},{3,1},{4,6},{5,7},{6,4},{7,5},{8,10},{9,11},{10,... | collective-permute-start | bytes 1544 | tf_op jit(solution)/shard_map/ppermute | solution.py:52
  134.1 3.5 %collective-permute-start.12 = (f32[1,128]{1,0:T(1,128)S(1)}, f32[1,128]{1,0:T(1,128)S(1)}, u32[]{:S(2)}, u32[]{:S(2)}) collective-permute-start(f32[1,128]{1,0:T(1,128)S(1)} %slice.14), channel_id=1, source_target_pairs={{0,3},{1,0},{2,1},{3,2},{4,7},{5,4},{6,5},{7,6},{8,11},{9,8},{10,9... | collective-permute-start | bytes 1544 | tf_op jit(solution)/shard_map/ppermute | solution.py:52
  135.2 4.8 %collective-permute-start.10 = (f32[1,128]{1,0:T(1,128)S(1)}, f32[1,128]{1,0:T(1,128)S(1)}, u32[]{:S(2)}, u32[]{:S(2)}) collective-permute-start(f32[1,128]{1,0:T(1,128)S(1)} %slice.14), channel_id=1, source_target_pairs={{0,1},{1,2},{2,3},{3,0},{4,5},{5,6},{6,7},{7,4},{8,9},{9,10},{10,1... | collective-permute-start | bytes 1544 | tf_op jit(solution)/shard_map/ppermute | solution.py:52

commit v2 on v0

v2 whole, which is shorter than its diff:
```python
import functools
import math

import jax
import jax.numpy as jnp
from jax import lax
from jax.experimental import pallas as pl
from jax.experimental.pallas import tpu as pltpu
from jax.sharding import PartitionSpec as P

NY, NZ, NC = 4, 8, 2
NBLK = NY * NZ * NC
NHEAD = 4
GROUP = 4
DEPTH = 8
TOK = 128
HD = 128
KV = 2
RATIO = 8
LANES = 128
HALF = 8
ROWS = TOK * RATIO
KINDS = 2 * KV
PART = 32 * DEPTH
F32 = jnp.float32
BF16 = jnp.bfloat16
VMEM = pltpu.VMEM
NT = (((1,), (1,)), ((), ()))
NN = (((1,), (0,)), ((), ()))
TN = (((0,), (0,)), ((), ()))


def index_of(y, z, c):
    return ((y % NY) * NZ + z % NZ) * NC + c % NC


def every():
    return [(y, z, c) for y in range(NY) for z in range(NZ) for c in range(NC)]


def along_y(x, step):
    pairs = [(index_of(y, z, c), index_of(y + step, z, c)) for y, z, c in every()]
    return lax.ppermute(x, "branch", pairs)


def other_core(x):
    pairs = [(index_of(y, z, c), index_of(y, z, c + 1)) for y, z, c in every()]
    return lax.ppermute(x, "branch", pairs)


def along_head(x, step):
    pairs = [(i, (i + step) % NHEAD) for i in range(NHEAD)]
    return lax.ppermute(x, "head", pairs)


def swap_z(x):
    groups = [[index_of(y, z, c) for z in range(NZ)] for y in range(NY) for c in range(NC)]
    return lax.all_to_all(x, "branch", 0, 0, axis_index_groups=groups, tiled=False)


def swap_yz(x):
    groups = [[index_of(y, z, c) for y in range(NY) for z in range(NZ)] for c in range(NC)]
    return lax.all_to_all(x, "branch", 0, 0, axis_index_groups=groups, tiled=False)


def call(body, outs, scratch=(), vmem_mb=32):
    return dict(
        out_shape=outs,
        scratch_shapes=list(scratch),
        compiler_params=pltpu.CompilerParams(vmem_limit_bytes=vmem_mb << 20),
    )


def in_vmem():
    return pl.BlockSpec(memory_space=VMEM)


def place():
    b = lax.axis_index("branch")
    return b // (NZ * NC), (b // NC) % NZ, b % NC


LINE = 0
DEAL = 8
BACK = 16
HOLD = 24
INNER = 32
SELF = 40
WORDS = 48


def pack_rows(x, base, first, count):
    row = lax.broadcasted_iota(jnp.int32, (8, LANES), 0)
    weight = jnp.zeros((8, LANES), F32)
    for i in range(count):
        weight = jnp.where(row == first + i, float(base**i), weight)
    return jnp.sum(x * weight, axis=0, keepdims=True)


def plan_kernel(mine, other, picked, table, scale):
    y, z, c = place()
    meta_m = mine[...].astype(F32)[:, 16:24, :]
    meta_o = other[...].astype(F32)[:, 16:24, :]
    row = lax.broadcasted_iota(jnp.int32, (8, LANES), 0)
    row_f = row.astype(F32)
    lane = lax.broadcasted_iota(jnp.int32, (8, LANES), 1)
    lane_f = lane.astype(F32)
    is_block = lane < NBLK
    wide_lane = lax.broadcasted_iota(jnp.int32, (NY * NZ, LANES), 1).astype(F32)
    hit = jnp.maximum(
        jnp.where(meta_m[:, 0, :] == wide_lane, 1.0, 0.0),
        jnp.where(meta_o[:, 0, :] == wide_lane, 1.0, 0.0),
    )
    inner = jnp.max(hit, axis=0, keepdims=True)
    inner = jnp.where(is_block, jnp.broadcast_to(inner, (8, LANES)), 0.0)
    before = (
        lax.broadcasted_iota(jnp.int32, (LANES, LANES), 0)
        < lax.broadcasted_iota(jnp.int32, (LANES, LANES), 1)
    ).astype(F32).astype(BF16)
    rank = lax.dot_general(inner.astype(BF16), before, NN, preferred_element_type=F32)
    slots = jnp.where(inner > 0.0, rank + 1.0, 0.0)

    wanted = (row * 2 + c + 1).astype(F32)
    index = jnp.sum(jnp.where(slots == wanted, lane_f, 0.0), axis=1, keepdims=True)
    index = jnp.broadcast_to(index, (8, LANES))
    low = pack_rows(index, 64, 0, 4).astype(jnp.int32)[0, 0]
    high = pack_rows(index, 64, 4, 4).astype(jnp.int32)[0, 0]
    for s in range(HALF):
        block = ((low if s < 4 else high) >> (6 * (s % 4))) & 63
        at = block >> 1
        piece = jnp.where((block & 1) == c, mine[at].astype(F32), other[at].astype(F32))
        piece = piece[0:16].astype(BF16)
        picked[:, s] = jnp.broadcast_to(piece[None], (NZ, 16, LANES))

    for k in range(NY):
        yy = lax.rem(y + k, NY)
        line = mine[yy * NZ + z].astype(F32)[16:24, :]
        same = (line == lane_f) & is_block
        slot = jnp.sum(jnp.where(same, slots, 0.0), axis=1, keepdims=True)
        slot = jnp.broadcast_to(slot, (8, LANES))
        block = (yy * NZ + z) * NC + c
        own = jnp.sum(jnp.where(lane == block, slots, 0.0), axis=1, keepdims=True)
        own = jnp.broadcast_to(own, (8, LANES))
        depth = jnp.sum(jnp.where(slot > 0.0, 1.0, 0.0), axis=0, keepdims=True)
        entry = jnp.where(row_f == depth, own, slot)
        dealt = jnp.maximum(slot - 1.0, 0.0)
        for half in range(2):
            at = 2 * k + half
            table[DEAL + at : DEAL + at + 1, :] = pack_rows(dealt, 16, 4 * half, 4).astype(jnp.int32)
            table[BACK + at : BACK + at + 1, :] = pack_rows(entry, 32, 4 * half, 4).astype(jnp.int32)
        if k == 0:
            table[LINE : LINE + 8, :] = slot.astype(jnp.int32)
            table[INNER : INNER + 8, :] = own.astype(jnp.int32)
            table[SELF : SELF + 8, :] = jnp.where(row_f == depth, own, 0.0).astype(jnp.int32)
    for i in range(6):
        word = jnp.zeros((8, 1), F32)
        for j in range(3):
            held = jnp.where(slots == float(3 * i + j + 1), lane_f + 1.0, 0.0)
            word = word + jnp.sum(held, axis=1, keepdims=True) * float(128**j)
        table[HOLD + i : HOLD + i + 1, :] = jnp.broadcast_to(word, (8, LANES)).astype(jnp.int32)[0:1]

    here = mine[y * NZ + z].astype(F32)[16:24, :]
    group, reward = here[0:1, :], here[1:2, :]
    in_m = jnp.where(meta_m[:, 0, :] == group, meta_m[:, 1, :], 0.0)
    in_o = jnp.where(meta_o[:, 0, :] == group, meta_o[:, 1, :], 0.0)
    total = jnp.sum(in_m + in_o, axis=0, keepdims=True)
    squares = jnp.sum(in_m * in_m + in_o * in_o, axis=0, keepdims=True)
    mean = total / GROUP
    spread = jnp.sqrt(jnp.maximum(squares / GROUP - mean * mean, 0.25))
    advantage = (reward - mean) / spread
    advantage = jnp.sum(jnp.where(lane[0:1] == NBLK, advantage, 0.0), axis=1, keepdims=True)
    scale[...] = jnp.broadcast_to(advantage, (8, LANES))


def plan(mine, other):
    return pl.pallas_call(
        plan_kernel,
        in_specs=[in_vmem()] * 2,
        out_specs=(in_vmem(),) * 3,
        **call(
            plan_kernel,
            (
                jax.ShapeDtypeStruct((NZ, HALF, 16, LANES), BF16),
                jax.ShapeDtypeStruct((WORDS, LANES), jnp.int32),
                jax.ShapeDtypeStruct((8, LANES), F32),
            ),
        ),
        name="plan",
    )(mine, other)


def deal_kernel(table, mine, other, *outs):
    c = place()[2]
    words = table[DEAL : DEAL + 8, :]
    for k in range(NY):
        for d in range(DEPTH):
            slot = (words[2 * k + d // 4, 0] >> (4 * (d % 4))) & 15
            at = slot >> 1
            outs[k][d] = jnp.where((slot & 1) == c, mine[:, at], other[:, at])


def deal(table, mine, other):
    return pl.pallas_call(
        deal_kernel,
        in_specs=[in_vmem()] * 3,
        out_specs=(in_vmem(),) * NY,
        **call(deal_kernel, (jax.ShapeDtypeStruct((DEPTH, NZ, 16, LANES), BF16),) * NY),
        name="deal",
    )(table, mine, other)


def prepare_kernel(scale, queries, cotangent, q_all, g_all):
    weight = scale[0:1, :]
    for h in range(KV):
        heads = slice(RATIO * h, RATIO * (h + 1))
        q_all[h] = queries[...].astype(F32)[:, heads, :].reshape(ROWS, HD).astype(BF16)
        g_all[h] = (
            (cotangent[...].astype(F32)[:, heads, :] * weight[None]).reshape(ROWS, HD).astype(BF16)
        )


def prepare(scale, queries, cotangent):
    return pl.pallas_call(
        prepare_kernel,
        in_specs=[in_vmem()] * 3,
        out_specs=(in_vmem(),) * 2,
        **call(prepare_kernel, (jax.ShapeDtypeStruct((KV, ROWS, HD), BF16),) * 2),
        cost_estimate=pl.CostEstimate(flops=10**6, bytes_accessed=2**20, transcendentals=0),
        name="prepare",
    )(scale, queries, cotangent)


def rows_of(part, kind, h):
    at = kind * KINDS + 2 * h
    return part[:, at : at + 2].reshape(PART, HD)


def one_part(h, keys, values, q, g, mask, exps, pgs, stats, at):
    s = lax.dot_general(keys, q, NT, preferred_element_type=F32) * (
        math.log2(math.e) / math.sqrt(HD)
    )
    s = mask(s)
    top = jnp.max(s, axis=0, keepdims=True)
    e = jnp.exp2(s - top)
    pg = lax.dot_general(values, g, NT, preferred_element_type=F32)
    exps[h] = e
    pgs[h] = pg
    stats[h, at : at + 1, :] = top
    stats[h, at + 1 : at + 2, :] = jnp.sum(e, axis=0, keepdims=True)
    stats[h, at + 2 : at + 3, :] = jnp.sum(e * pg, axis=0, keepdims=True)


def causal(s):
    key_pos = lax.broadcasted_iota(jnp.int32, s.shape, 0)
    query_pos = lax.broadcasted_iota(jnp.int32, s.shape, 1) // RATIO
    return jnp.where(key_pos <= query_pos, s, -1e30)


def listed(table):
    def mask(s):
        parts = []
        for d in range(DEPTH):
            seen = jnp.concatenate([table[LINE + d : LINE + d + 1, :]] * (ROWS // LANES), 1) > 0
            parts.append(jnp.where(seen, s[32 * d : 32 * d + 32], -1e30))
        return jnp.concatenate(parts, 0)

    return mask


def scores_kernel(table, q_all, g_all, part, after, exps, pgs, stats):
    for h in range(KV):
        keys, values = rows_of(part, 0, h), rows_of(part, 1, h)
        one_part(h, keys, values, q_all[h], g_all[h], listed(table), exps, pgs, stats, 0)


def first_scores_kernel(
    table, q_all, g_all, part, own_kv, exps, pgs, stats, own_exps, own_pgs
):
    for h in range(KV):
        keys, values = rows_of(part, 0, h), rows_of(part, 1, h)
        one_part(h, keys, values, q_all[h], g_all[h], listed(table), exps, pgs, stats, 0)
        one_part(
            h, own_kv[h], own_kv[KV + h], q_all[h], g_all[h], causal, own_exps, own_pgs, stats, 4
        )


def wide(keys):
    return jax.ShapeDtypeStruct((KV, keys, ROWS), F32)


def scores_of(table, q_all, g_all, part, after):
    return pl.pallas_call(
        scores_kernel,
        in_specs=[in_vmem()] * 4 + [pl.BlockSpec(memory_space=pl.ANY)],
        out_specs=(in_vmem(),) * 3,
        **call(
            scores_kernel,
            (wide(PART), wide(PART), jax.ShapeDtypeStruct((KV, 8, ROWS), F32)),
            vmem_mb=16,
        ),
        cost_estimate=cost(PART, 2),
        name="scores",
    )(table, q_all, g_all, part, after)


def first_scores_of(table, q_all, g_all, part, own_kv):
    return pl.pallas_call(
        first_scores_kernel,
        in_specs=[in_vmem()] * 5,
        out_specs=(in_vmem(),) * 5,
        **call(
            first_scores_kernel,
            (wide(PART), wide(PART), jax.ShapeDtypeStruct((KV, 8, ROWS), F32), wide(TOK), wide(TOK)),
            vmem_mb=16,
        ),
        cost_estimate=cost(PART + TOK, 2),
        name="scores_first",
    )(table, q_all, g_all, part, own_kv)


def cost(keys, products):
    return pl.CostEstimate(
        flops=2 * products * KV * ROWS * keys * HD,
        bytes_accessed=8 * KV * ROWS * keys,
        transcendentals=KV * ROWS * keys,
    )


def merge(h, stats):
    rows = [(ref, 0) for ref in stats] + [(stats[0], 4)]
    tops = [ref[h, at : at + 1, :] for ref, at in rows]
    top = tops[0]
    for t in tops[1:]:
        top = jnp.maximum(top, t)
    shares = [jnp.exp2(t - top) for t in tops]
    norm = sum(s * ref[h, at + 1 : at + 2, :] for s, (ref, at) in zip(shares, rows))
    norm = 1.0 / norm
    shares = [s * norm for s in shares]
    delta = sum(s * ref[h, at + 2 : at + 3, :] for s, (ref, at) in zip(shares, rows))
    return shares, delta


def one_grad(h, e, pg, share, delta, q, g, keys):
    p = e * share
    low = p.astype(BF16)
    ds = (p * (pg - delta)).astype(BF16)
    factor = 1.0 / math.sqrt(HD)
    dv = lax.dot_general(low, g, NN, preferred_element_type=F32)
    dk = lax.dot_general(ds, q, NN, preferred_element_type=F32) * factor
    turned = keys.astype(F32).T.astype(BF16)
    dq = lax.dot_general(turned, ds, NN, preferred_element_type=F32)
    return dq, dk, dv


def part_grad(k, h, table, stats, exps, pgs, q_all, g_all, part, own_grad, contrib):
    shares, delta = merge(h, stats)
    dq, dk, dv = one_grad(
        h, exps[h], pgs[h], shares[k], delta, q_all[h], g_all[h], rows_of(part, 0, h)
    )
    piece = lax.rem(place()[0] + NY - k, NY)
    for kind, grad in enumerate((dk, dv)):
        at = kind * KINDS + 2 * h
        own = [
            own_grad[kind * KV + h, pl.ds(pl.multiple_of(half * 64 + piece * 16, 16), 16), :]
            for half in range(2)
        ]
        own = jnp.concatenate(own, 0)
        for d in range(DEPTH):
            mark = table[SELF + d : SELF + d + 1, :] > 0
            both = jnp.where(mark, own, grad[32 * d : 32 * d + 32])
            contrib[d, at : at + 2] = both.astype(BF16).reshape(2, 16, HD)
    return dq


def first_grads_kernel(
    k, table, s0, s1, s2, s3, exps, pgs, q_all, g_all, part, own_exps, own_pgs, own_kv,
    dq_sum, own_grad, contrib,
):
    stats = (s0, s1, s2, s3)
    for h in range(KV):
        shares, delta = merge(h, stats)
        dq, dk, dv = one_grad(
            h, own_exps[h], own_pgs[h], shares[NY], delta, q_all[h], g_all[h], own_kv[h]
        )
        own_grad[h] = dk
        own_grad[KV + h] = dv
        dq_sum[h] = dq + part_grad(
            k, h, table, stats, exps, pgs, q_all, g_all, part, own_grad, contrib
        )


def grads_kernel(
    k, table, s0, s1, s2, s3, exps, pgs, q_all, g_all, part, own_grad, dq_in, dq_sum, contrib
):
    for h in range(KV):
        dq_sum[h] = dq_in[h] + part_grad(
            k, h, table, (s0, s1, s2, s3), exps, pgs, q_all, g_all, part, own_grad, contrib
        )


def last_grads_kernel(
    k, table, s0, s1, s2, s3, exps, pgs, q_all, g_all, part, own_grad, dq_in,
    query_grad, contrib, squares,
):
    total = jnp.zeros((8, HD), F32)
    for h in range(KV):
        dq = dq_in[h] + part_grad(
            k, h, table, (s0, s1, s2, s3), exps, pgs, q_all, g_all, part, own_grad, contrib
        )
        dq = dq.T * (1.0 / math.sqrt(HD))
        total = total + jnp.sum((dq * dq).reshape(ROWS // 8, 8, HD), axis=0)
        query_grad[:, RATIO * h : RATIO * (h + 1), :] = dq.reshape(TOK, RATIO, HD)
    own = own_grad[...]
    own_squares = jnp.sum((own * own).reshape(2 * KV * TOK // 8, 8, HD), axis=0)
    squares[...] = total + jnp.where(table[INNER : INNER + 8, :] > 0, 0.0, own_squares)


DQ_SUM = (KV, HD, TOK * RATIO)
OWN = (2 * KV, TOK, HD)
CONTRIB = (DEPTH, NZ, 16, LANES)


def grads_of(body, name, outs, k, *arrays):
    return pl.pallas_call(
        functools.partial(body, k),
        in_specs=[in_vmem()] * len(arrays),
        out_specs=(in_vmem(),) * len(outs),
        **call(body, outs, vmem_mb=16),
        cost_estimate=pl.CostEstimate(flops=1000, bytes_accessed=1000, transcendentals=0),
        name=name,
    )(*arrays)


def attend(table, scale, queries, cotangent, own_kv, parts):
    q_all, g_all = prepare(scale, queries, cotangent)
    e, pg, st = [None] * NY, [None] * NY, [None] * NY
    e[0], pg[0], st[0], own_e, own_pg = first_scores_of(table, q_all, g_all, parts[0], own_kv)
    after = st[0]
    for k in (1, 2, 3):
        e[k], pg[k], st[k] = scores_of(table, q_all, g_all, parts[k], after)
        after = st[k]
    back = [None] * NY
    dq_type = jax.ShapeDtypeStruct(DQ_SUM, F32)
    own_type = jax.ShapeDtypeStruct(OWN, F32)
    contrib_type = jax.ShapeDtypeStruct(CONTRIB, BF16)
    for k in (2, 1, 3, 0):
        shared = (table, *st, e[k], pg[k], q_all, g_all, parts[k])
        if k == 2:
            dq, own_grad, back[k] = grads_of(
                first_grads_kernel, "grads_first", (dq_type, own_type, contrib_type), k,
                *shared, own_e, own_pg, own_kv,
            )
        elif k:
            dq, back[k] = grads_of(
                grads_kernel, "grads", (dq_type, contrib_type), k, *shared, own_grad, dq
            )
        else:
            query_grad, back[k], squares = grads_of(
                last_grads_kernel, "grads_last",
                (
                    jax.ShapeDtypeStruct((TOK, KV * RATIO, HD), F32),
                    contrib_type,
                    jax.ShapeDtypeStruct((8, LANES), F32),
                ),
                k, *shared, own_grad, dq,
            )
    return query_grad, own_grad, *back, squares


def add_part(k, table, part, acc):
    words = table[BACK + 2 * k : BACK + 2 * k + 2, :]
    for d in range(DEPTH):
        slot = (words[d // 4, 0] >> (5 * (d % 4))) & 31
        at = jnp.maximum(slot - 1, 0)
        acc[at & 1, at >> 1] += jnp.where(slot > 0, part[d].astype(F32), 0.0)


def combine_first_kernel(table, part, acc):
    acc[...] = jnp.zeros_like(acc)
    add_part(1, table, part, acc)


def combine_kernel(table, part, acc_in, acc):
    add_part(2, table, part, acc)


def combine_last_kernel(table, part, part_here, acc_in, keep, send, acc):
    c = place()[2]
    add_part(0, table, part_here, acc)
    add_part(3, table, part, acc)
    for s in range(HALF):
        send[:, s] = acc[1 - c, s].astype(BF16)
        keep[:, s] = acc[c, s]


def combine(table, parts):
    acc_type = jax.ShapeDtypeStruct((2, HALF, NZ, 16, LANES), F32)
    small = pl.CostEstimate(flops=1000, bytes_accessed=1000, transcendentals=0)
    acc = pl.pallas_call(
        combine_first_kernel,
        in_specs=[in_vmem()] * 2,
        out_specs=in_vmem(),
        **call(combine_first_kernel, acc_type, vmem_mb=16),
        cost_estimate=small,
        name="combine_first",
    )(table, parts[1])
    acc = pl.pallas_call(
        combine_kernel,
        in_specs=[in_vmem()] * 3,
        out_specs=in_vmem(),
        input_output_aliases={2: 0},
        **call(combine_kernel, acc_type, vmem_mb=16),
        cost_estimate=small,
        name="combine",
    )(table, parts[2], acc)
    keep, send, _ = pl.pallas_call(
        combine_last_kernel,
        in_specs=[in_vmem()] * 4,
        out_specs=(in_vmem(),) * 3,
        input_output_aliases={3: 2},
        **call(
            combine_last_kernel,
            (
                jax.ShapeDtypeStruct((NZ, HALF, 16, LANES), F32),
                jax.ShapeDtypeStruct((NZ, HALF, 16, LANES), BF16),
                acc_type,
            ),
            vmem_mb=16,
        ),
        cost_estimate=small,
        name="combine_last",
    )(table, parts[3], parts[0], acc)
    return keep, send


def split_rows(value, rows):
    high = value.astype(BF16).astype(F32)
    middle = (value - high).astype(BF16).astype(F32)
    low = value - high - middle
    row = lax.broadcasted_iota(jnp.int32, (8, LANES), 0)
    tile = jnp.where(row == 0, high, jnp.where(row == 1, middle, jnp.where(row == 2, low, 0.0)))
    if rows > 8:
        tile = jnp.concatenate([tile, jnp.zeros((rows - 8, LANES), F32)], 0)
    return tile


def total_kernel(parts, squares, sums, pack):
    sums_now = parts[0].astype(F32)
    for z in range(1, NZ):
        sums_now = sums_now + parts[z].astype(F32)
    pack[0:HALF] = sums_now.astype(BF16)
    tile = squares[...] + jnp.sum((sums_now * sums_now).reshape(HALF * 2, 8, LANES), axis=0)
    value = jnp.broadcast_to(jnp.sum(tile, axis=0, keepdims=True), (8, LANES))
    sums[...] = value
    pack[HALF] = split_rows(value, 16).astype(BF16)


def total_of(parts, squares):
    return pl.pallas_call(
        total_kernel,
        in_specs=[in_vmem()] * 2,
        out_specs=(in_vmem(), in_vmem()),
        **call(
            total_kernel,
            (
                jax.ShapeDtypeStruct((8, LANES), F32),
                jax.ShapeDtypeStruct((HALF + 1, 16, LANES), BF16),
            ),
        ),
        name="total",
    )(parts, squares)


def route_kernel(table, sums, mine, other, out):
    c = place()[2]
    words = table[HOLD : HOLD + 8, :]
    tail = other[HALF].astype(F32)[0:8, :]
    value = sums[...] + jnp.sum(tail, axis=0, keepdims=True)
    blank = jnp.concatenate([jnp.zeros((16, LANES), F32), split_rows(value, 8)], 0)
    out[...] = jnp.broadcast_to(blank.astype(BF16)[None], (NY * NZ, 24, LANES))
    for s in range(2 * HALF):
        block = ((words[s // 3, 0] >> (7 * (s % 3))) & 127) - 1
        piece = jnp.where((s % 2) == c, mine[s // 2], other[s // 2])

        @pl.when((block >= 0) & ((block & 1) == c))
        def _():
            out[block >> 1, 0:16, :] = piece


def route(table, sums, mine, other):
    return pl.pallas_call(
        route_kernel,
        in_specs=[in_vmem()] * 4,
        out_specs=in_vmem(),
        **call(route_kernel, jax.ShapeDtypeStruct((NY * NZ, 24, LANES), BF16)),
        name="route",
    )(table, sums, mine, other)


def tally_kernel(arrived, sums):
    tails = jnp.sum(arrived[...].astype(F32)[:, 16:24, :], axis=0)
    tails = jnp.sum(jnp.sum(tails, axis=0, keepdims=True), axis=1, keepdims=True)
    sums[...] = jnp.broadcast_to(tails, (1, LANES))


def tally(arrived):
    return pl.pallas_call(
        tally_kernel,
        in_specs=[in_vmem()],
        out_specs=in_vmem(),
        **call(tally_kernel, jax.ShapeDtypeStruct((1, LANES), F32)),
        name="tally",
    )(arrived)


def finish_kernel(table, arrived, own_grad, key_grad, value_grad):
    inner = table[INNER : INNER + 1, :] > 0
    for z in range(NZ):
        kind, h, half = z // 4, z // 2 % 2, z % 2
        out = value_grad if kind else key_grad
        for y in range(NY):
            at = half * 64 + y * 16
            piece = arrived[y * NZ + z].astype(F32)[0:16, :]
            own = own_grad[kind * KV + h, at : at + 16, :]
            out[at : at + 16, h, :] = jnp.where(inner, piece, own)


def finish(table, arrived, own_grad):
    return pl.pallas_call(
        finish_kernel,
        in_specs=[in_vmem()] * 3,
        out_specs=(in_vmem(),) * 2,
        **call(finish_kernel, (jax.ShapeDtypeStruct((TOK, KV, HD), F32),) * 2),
        cost_estimate=pl.CostEstimate(flops=1000, bytes_accessed=1000, transcendentals=0),
        name="finish",
    )(table, arrived, own_grad)


def local(queries, keys, values, cotangent, rewards, groups, ancestors, step_ids):
    own_kv = jnp.stack([keys, values]).transpose(0, 2, 1, 3)
    pieces = (
        own_kv.reshape(2, KV, 2, NY, 16, HD).transpose(3, 0, 1, 2, 4, 5).reshape(NY * NZ, 16, HD)
    )
    own_kv = own_kv.reshape(2 * KV, TOK, HD)
    line = jnp.broadcast_to(ancestors[0].astype(BF16)[:, None], (8, NBLK))
    facts = jnp.concatenate(
        [groups.astype(BF16), rewards, jnp.zeros((6,), BF16)]
    )
    meta = jnp.concatenate([line, jnp.broadcast_to(facts[:, None], (8, LANES - NBLK))], 1)
    packet = jnp.concatenate([pieces, jnp.broadcast_to(meta[None], (NY * NZ, 8, LANES))], 1)
    mine = swap_yz(packet)
    other = other_core(mine)
    trained = (step_ids[0] % 2 == 0)[:, None, None]
    masked = jnp.where(trained, cotangent, jnp.zeros_like(cotangent))
    picked, table, scale = plan(mine, other)
    column = swap_z(picked)
    dealt = deal(table, column, other_core(column))
    parts = [dealt[0]] + [along_y(dealt[k], k) for k in (1, 2, 3)]
    query_grad, own_grad, c0, c1, c2, c3, squares = attend(
        table, scale, queries, masked, own_kv, parts
    )
    back = [c0] + [along_y(x, -k) for k, x in ((1, c1), (2, c2), (3, c3))]
    keep, send = combine(table, back)
    halves = (keep + other_core(send).astype(F32)).astype(BF16)
    sums, pack = total_of(swap_z(halves), squares)
    arrived = swap_yz(route(table, sums, pack, other_core(pack)))
    mine_sum = tally(arrived)
    all_sum = mine_sum
    for k in (1, 2, 3):
        all_sum = all_sum + along_head(mine_sum, k)
    key_grad, value_grad = finish(table, arrived, own_grad)
    count = float(NBLK * TOK * NHEAD * (KV * RATIO + 2 * KV) * HD)
    grad_rms = jnp.sqrt(all_sum[0, 0] / count)
    return query_grad, key_grad, value_grad, grad_rms


def solution(mesh):
    in_specs = (
        P("branch", "head", None),
        P("branch", "head", None),
        P("branch", "head", None),
        P("branch", "head", None),
        P("branch"),
        P("branch"),
        P("branch", None),
        P("branch", None),
    )
    out_specs = (
        P("branch", "head", None),
        P("branch", "head", None),
        P("branch", "head", None),
        P(),
    )
    return jax.shard_map(local, mesh=mesh, in_specs=in_specs, out_specs=out_specs, check_vma=False)
```

time: 502 us -> 125 us (0.25)
  waiting for transfers between devices: 194 us -> 28.4 us
  blocking collectives: 201 us -> 66.9 us
  local copies, waits for them, and re-layouts: 32.2 us -> 0.23 us
  other arithmetic: 28.3 us -> 2.38 us
  matrix products: 23.1 us -> 0 us
  between operations: 21.5 us -> 3.48 us
  Pallas kernels: 0 us -> 12.2 us
  starting transfers between devices: 0.12 us -> 11.4 us
    psum x2 -> x0, blocking collectives: 201 us -> none  [the longest x1 126 us: local(): lax.psum((flags * reward, flags * (reward * reward)), 'branch')]
    reduce_scatter x1 -> x0, waiting for transfers between devices: 183 us -> none  [local(): lax.psum_scatter(part_rows.reshape(row_count, 2, kv_here, head_dim), 'bra...]
    all_to_all x0 -> x4, blocking collectives: none -> 66.9 us  [the longest x2 37.9 us: swap_yz(): lax.all_to_all(x, 'branch', 0, 0, axis_index_groups=groups, tiled=False)]
    ppermute x0 -> x13, waiting for transfers between devices: none -> 28.4 us  [the longest x6 19.9 us: along_y(): return lax.ppermute(x, 'branch', pairs)]
    dot_general x14 -> x0, matrix products: 23.1 us -> none  [the longest x2 11.5 us: select_blocks(): jnp.einsum('dn,ntgh->dtgh', chosen, pieces, preferred_element_type=jnp.fl...]
    pallas_call x0 -> x18, Pallas kernels: none -> 12.2 us  [the longest x4 5.6 us: grads_of(): pl.pallas_call(functools.partial(body, k), in_specs=[in_vmem()] * len(arr...]
    scatter-add x1 -> x0, local copies, waits for them, and re-layouts: 11.7 us -> none  [local(): part_rows = jnp.zeros((blocks_here, rows_here, 2, kv_here, head_dim), jnp...]
    ppermute x0 -> x13, starting transfers between devices: none -> 11.4 us  [the longest x6 6.78 us: along_y(): return lax.ppermute(x, 'branch', pairs)]
  transfers between devices with their start and end apart: 3 -> 13, of which waited for: 2 -> 9; matrix products, arithmetic and copies ran while one was open for 5% -> 0% of each run, Pallas kernels for 0% -> 6%
where the time goes in v2:
time: 125 us
  blocking collectives  66.9 us (54%)
  waiting for transfers between devices  28.4 us (23%)
  Pallas kernels  12.2 us (10%)
  starting transfers between devices  11.4 us (9%)
  between operations  3.48 us (3%)
  other arithmetic  2.38 us (2%)
    all_to_all x2, blocking collectives, swap_yz(): lax.all_to_all(x, 'branch', 0, 0, axis_index_groups=groups, tiled=False)  37.9 us
    all_to_all x2, blocking collectives, swap_z(): lax.all_to_all(x, 'branch', 0, 0, axis_index_groups=groups, tiled=False)  28.9 us
    ppermute x6, waiting for transfers between devices, along_y(): return lax.ppermute(x, 'branch', pairs)  19.9 us
    ppermute x6, starting transfers between devices, along_y(): return lax.ppermute(x, 'branch', pairs)  6.78 us
    pallas_call x4, Pallas kernels, grads_of(): pl.pallas_call(functools.partial(body, k), in_specs=[in_vmem()] * len(arr...  5.6 us
    ppermute x4, waiting for transfers between devices, other_core(): return lax.ppermute(x, 'branch', pairs)  5.43 us
    ppermute x3, starting transfers between devices, along_head(): return lax.ppermute(x, 'head', pairs)  4.44 us
    ppermute x3, waiting for transfers between devices, along_head(): return lax.ppermute(x, 'head', pairs)  3.05 us
  transfers between devices with their start and end apart: 13, of which 9 were waited for; matrix products, arithmetic and copies ran while one was open for 0% of the time, Pallas kernels for 6%

profile of v2, /device:TPU:32, one launch (start us, length us, event | category | flops | bytes accessed | tf_op | source)
XLA Modules:
  0.0 125.0 jit_solution(13431483809925855633)
XLA Ops:
  2.7 1.1 pad_maximum_fusion.1
  4.2 22.1 %all_to_all.20.mine = bf16[32,24,128]{2,1,0:T(8,128)(2,1)S(1)} all-to-all(bf16[32,24,128]{2,1,0:T(8,128)(2,1)S(1)} %pad_maximum_fusion), channel_id=1, replica_groups={{0,8,16,24,32,40,48,56,64,72,80,88,96,104,112,120,128,136,144,152,160,1..., dimensions={0} | all-to-all | bytes 393216 | tf_op jit(solution)/shard_map/all_to_all | solution.py:63
  26.3 1.4 %collective-permute-done.other = bf16[32,24,128]{2,1,0:T(8,128)(2,1)S(1)} collective-permute-done((bf16[32,24,128]{2,1,0:T(8,128)(2,1)S(1)}, bf16[32,24,128]{2,1,0:T(8,128)(2,1)S(1)}, u32[]{:S(2)}, u32[]{:S(2)}) %collective-permute-start) | collective-permute-done | bytes 196640 | tf_op jit(solution)/shard_map/ppermute | solution.py:48
  28.1 14.1 %all_to_all.21.mine = bf16[8,8,16,128]{3,2,1,0:T(8,128)(2,1)S(1)} all-to-all(bf16[8,8,16,128]{3,2,1,0:T(8,128)(2,1)S(1)} %get-tuple-element.47), channel_id=1, replica_groups={{0,8,16,24,32,40,48,56},{4,12,20,28,36,44,52,60},{64,72,80,88,96,104,11..., dimensions={0} | all-to-all | bytes 524288 | tf_op jit(solution)/shard_map/all_to_all | solution.py:58
  42.4 1.3 %collective-permute-done.1.other = bf16[8,8,16,128]{3,2,1,0:T(8,128)(2,1)S(1)} collective-permute-done((bf16[8,8,16,128]{3,2,1,0:T(8,128)(2,1)S(1)}, bf16[8,8,16,128]{3,2,1,0:T(8,128)(2,1)S(1)}, u32[]{:S(2)}, u32[]{:S(2)}) %collective-permute-start.1) | collective-permute-done | bytes 262176 | tf_op jit(solution)/shard_map/ppermute | solution.py:48
  44.7 2.0 %collective-permute-start.3 = (bf16[8,8,16,128]{3,2,1,0:T(8,128)(2,1)S(1)}, bf16[8,8,16,128]{3,2,1,0:T(8,128)(2,1)S(1)}, u32[]{:S(2)}, u32[]{:S(2)}) collective-permute-start(bf16[8,8,16,128]{3,2,1,0:T(8,128)(2,1)S(1)} %get-tuple-element.52), channel_id=1, source_target_pairs={{0,128},{4,132},{8,136},{12,140},{16,144},{20,148},{24,152},{28,15... | collective-permute-start | bytes 786440 | tf_op jit(solution)/shard_map/ppermute | solution.py:43
  46.7 1.3 %collective-permute-start.4 = (bf16[8,8,16,128]{3,2,1,0:T(8,128)(2,1)S(1)}, bf16[8,8,16,128]{3,2,1,0:T(8,128)(2,1)S(1)}, u32[]{:S(2)}, u32[]{:S(2)}) collective-permute-start(bf16[8,8,16,128]{3,2,1,0:T(8,128)(2,1)S(1)} %get-tuple-element.54), channel_id=1, source_target_pairs={{0,192},{4,196},{8,200},{12,204},{16,208},{20,212},{24,216},{28,22... | collective-permute-start | bytes 786440 | tf_op jit(solution)/shard_map/ppermute | solution.py:43
  48.5 1.3 %scores_first.1 = (f32[2,256,1024]{2,1,0:T(8,128)S(1)}, f32[2,256,1024]{2,1,0:T(8,128)S(1)}, f32[2,8,1024]{2,1,0:T(8,128)S(1)}, f32[2,128,1024]{2,1,0:T(8,128)S(1)}, f32[2,128,1024]{2,1,0:T(8,128)S(1)}) custom-call(s32[48,128]{1,0:T(8,128)S(1)} %get-tuple-element.43.table, bf16[2,1024,128]{2,1,0:T(8,128)(2,1)S(1)} %get-tuple-element.45.q_all, ...), custom_call_target="tpu_custom_call" | custom-call | flops 402653184 | bytes 6291456 | tf_op jit(solution)/shard_map/scores_first/pallas_call | solution.py:307
  49.8 9.5 %collective-permute-done.2.part = bf16[8,8,16,128]{3,2,1,0:T(8,128)(2,1)S(1)} collective-permute-done((bf16[8,8,16,128]{3,2,1,0:T(8,128)(2,1)S(1)}, bf16[8,8,16,128]{3,2,1,0:T(8,128)(2,1)S(1)}, u32[]{:S(2)}, u32[]{:S(2)}) %collective-permute-start.2) | collective-permute-done | bytes 262176 | tf_op jit(solution)/shard_map/ppermute | solution.py:43
  62.0 1.5 %grads_first.1 = (f32[2,128,1024]{2,1,0:T(8,128)S(1)}, f32[4,128,128]{2,1,0:T(8,128)S(1)}, bf16[8,8,16,128]{3,2,1,0:T(8,128)(2,1)S(1)}) custom-call(s32[48,128]{1,0:T(8,128)S(1)} %get-tuple-element.43.table, f32[2,8,1024]{2,1,0:T(8,128)S(1)} %get-tuple-element.49.after.s0, f32[2,8,1024]{2,1,0:T(8,128)S(1)} %get-tuple-element.51.after.s1, ...), custom_call_target="tpu_custom_call" | custom-call | flops 1000 | bytes 1000 | tf_op jit(solution)/shard_map/grads_first/pallas_call | solution.py:424
  63.4 1.0 grads.2
  64.4 1.5 %collective-permute-start.7 = (bf16[8,8,16,128]{3,2,1,0:T(8,128)(2,1)S(1)}, bf16[8,8,16,128]{3,2,1,0:T(8,128)(2,1)S(1)}, u32[]{:S(2)}, u32[]{:S(2)}) collective-permute-start(bf16[8,8,16,128]{3,2,1,0:T(8,128)(2,1)S(1)} %get-tuple-element.74), channel_id=1, source_target_pairs={{0,192},{4,196},{8,200},{12,204},{16,208},{20,212},{24,216},{28,22... | collective-permute-start | bytes 786440 | tf_op jit(solution)/shard_map/ppermute | solution.py:43
  66.1 1.0 grads.3
  67.1 1.1 collective-permute-start.5
  68.2 2.1 %grads_last.1 = (f32[128,16,128]{2,1,0:T(8,128)}, bf16[8,8,16,128]{3,2,1,0:T(8,128)(2,1)S(1)}, f32[8,128]{1,0:T(8,128)S(1)}) custom-call(s32[48,128]{1,0:T(8,128)S(1)} %get-tuple-element.43.table, f32[2,8,1024]{2,1,0:T(8,128)S(1)} %get-tuple-element.49.after.s0, f32[2,8,1024]{2,1,0:T(8,128)S(1)} %get-tuple-element.51.after.s1, ...), custom_call_target="tpu_custom_call" | custom-call | flops 1000 | bytes 1000 | tf_op jit(solution)/shard_map/grads_last/pallas_call | solution.py:424
  70.3 7.0 %collective-permute-done.7.part = bf16[8,8,16,128]{3,2,1,0:T(8,128)(2,1)S(1)} collective-permute-done((bf16[8,8,16,128]{3,2,1,0:T(8,128)(2,1)S(1)}, bf16[8,8,16,128]{3,2,1,0:T(8,128)(2,1)S(1)}, u32[]{:S(2)}, u32[]{:S(2)}) %collective-permute-start.7) | collective-permute-done | bytes 262176 | tf_op jit(solution)/shard_map/ppermute | solution.py:43
  77.7 3.4 %collective-permute-done.5.part = bf16[8,8,16,128]{3,2,1,0:T(8,128)(2,1)S(1)} collective-permute-done((bf16[8,8,16,128]{3,2,1,0:T(8,128)(2,1)S(1)}, bf16[8,8,16,128]{3,2,1,0:T(8,128)(2,1)S(1)}, u32[]{:S(2)}, u32[]{:S(2)}) %collective-permute-start.5) | collective-permute-done | bytes 262176 | tf_op jit(solution)/shard_map/ppermute | solution.py:43
  81.4 1.5 %collective-permute-done.8 = bf16[8,8,16,128]{3,2,1,0:T(8,128)(2,1)S(1)} collective-permute-done((bf16[8,8,16,128]{3,2,1,0:T(8,128)(2,1)S(1)}, bf16[8,8,16,128]{3,2,1,0:T(8,128)(2,1)S(1)}, u32[]{:S(2)}, u32[]{:S(2)}) %collective-permute-start.8) | collective-permute-done | bytes 262176 | tf_op jit(solution)/shard_map/ppermute | solution.py:48
  83.0 14.9 %all_to_all.22.parts = bf16[8,8,16,128]{3,2,1,0:T(8,128)(2,1)S(1)} all-to-all(bf16[8,8,16,128]{3,2,1,0:T(8,128)(2,1)S(1)} %add_convert_fusion), channel_id=1, replica_groups={{0,8,16,24,32,40,48,56},{4,12,20,28,36,44,52,60},{64,72,80,88,96,104,11..., dimensions={0} | all-to-all | bytes 524288 | tf_op jit(solution)/shard_map/all_to_all | solution.py:58
  98.0 1.2 collective-permute-done.9.other
  99.6 15.8 %all_to_all.23.arrived = bf16[32,24,128]{2,1,0:T(8,128)(2,1)S(1)} all-to-all(bf16[32,24,128]{2,1,0:T(8,128)(2,1)S(1)} %route.1), channel_id=1, replica_groups={{0,8,16,24,32,40,48,56,64,72,80,88,96,104,112,120,128,136,144,152,160,1..., dimensions={0} | all-to-all | bytes 393216 | tf_op jit(solution)/shard_map/all_to_all | solution.py:63
  115.5 2.8 %collective-permute-start.12 = (f32[1,128]{1,0:T(1,128)S(1)}, f32[1,128]{1,0:T(1,128)S(1)}, u32[]{:S(2)}, u32[]{:S(2)}) collective-permute-start(f32[1,128]{1,0:T(1,128)S(1)} %tally.1), channel_id=1, source_target_pairs={{0,3},{1,0},{2,1},{3,2},{4,7},{5,4},{6,5},{7,6},{8,11},{9,8},{10,9... | collective-permute-start | bytes 1544 | tf_op jit(solution)/shard_map/ppermute | solution.py:53
  119.0 0.9 collective-permute-start.10
  120.7 2.5 %collective-permute-done.11 = f32[1,128]{1,0:T(1,128)S(1)} collective-permute-done((f32[1,128]{1,0:T(1,128)S(1)}, f32[1,128]{1,0:T(1,128)S(1)}, u32[]{:S(2)}, u32[]{:S(2)}) %collective-permute-start.11) | collective-permute-done | bytes 544 | tf_op jit(solution)/shard_map/ppermute | solution.py:53
  (50 shorter events, 9.2 us)
Async XLA Ops:
  0.6 41.5 %copy-start.2 = (bf16[128,2,128]{2,1,0:T(2,128)(2,1)S(1)}, bf16[128,2,128]{2,1,0:T(2,128)(2,1)}, u32[]{:S(2)}) copy-start(bf16[128,2,128]{2,1,0:T(2,128)(2,1)} %param.10) | copy-start | bytes 196612
  0.6 41.5 %copy-start.3 = (bf16[128,2,128]{2,1,0:T(2,128)(2,1)S(1)}, bf16[128,2,128]{2,1,0:T(2,128)(2,1)}, u32[]{:S(2)}) copy-start(bf16[128,2,128]{2,1,0:T(2,128)(2,1)} %param.9) | copy-start | bytes 196612
  0.7 41.7 %copy-start.4 = (s32[1,128]{1,0:T(1,128)S(1)}, s32[1,128]{1,0:T(1,128)}, u32[]{:S(2)}) copy-start(s32[1,128]{1,0:T(1,128)} %param.15) | copy-start | bytes 1540
  0.7 47.4 %copy-start.1 = (bf16[128,16,128]{2,1,0:T(8,128)(2,1)S(1)}, bf16[128,16,128]{2,1,0:T(8,128)(2,1)}, u32[]{:S(2)}) copy-start(bf16[128,16,128]{2,1,0:T(8,128)(2,1)} %param.11) | copy-start | bytes 1572868
  3.8 44.5 %copy-start = (bf16[128,16,128]{2,1,0:T(8,128)(2,1)S(1)}, bf16[128,16,128]{2,1,0:T(8,128)(2,1)}, u32[]{:S(2)}) copy-start(bf16[128,16,128]{2,1,0:T(8,128)(2,1)} %queries.1) | copy-start | bytes 1572868
  26.3 1.4 %collective-permute-start = (bf16[32,24,128]{2,1,0:T(8,128)(2,1)S(1)}, bf16[32,24,128]{2,1,0:T(8,128)(2,1)S(1)}, u32[]{:S(2)}, u32[]{:S(2)}) collective-permute-start(bf16[32,24,128]{2,1,0:T(8,128)(2,1)S(1)} %all_to_all.20.mine), channel_id=1, source_target_pairs={{0,4},{4,0},{8,12},{12,8},{16,20},{20,16},{24,28},{28,24},{32,36},... | collective-permute-start | bytes 589832 | tf_op jit(solution)/shard_map/ppermute | solution.py:48
  42.1 1.5 %collective-permute-start.1 = (bf16[8,8,16,128]{3,2,1,0:T(8,128)(2,1)S(1)}, bf16[8,8,16,128]{3,2,1,0:T(8,128)(2,1)S(1)}, u32[]{:S(2)}, u32[]{:S(2)}) collective-permute-start(bf16[8,8,16,128]{3,2,1,0:T(8,128)(2,1)S(1)} %all_to_all.21.mine), channel_id=1, source_target_pairs={{0,4},{4,0},{8,12},{12,8},{16,20},{20,16},{24,28},{28,24},{32,36},... | collective-permute-start | bytes 786440 | tf_op jit(solution)/shard_map/ppermute | solution.py:48
  44.0 15.3 %collective-permute-start.2 = (bf16[8,8,16,128]{3,2,1,0:T(8,128)(2,1)S(1)}, bf16[8,8,16,128]{3,2,1,0:T(8,128)(2,1)S(1)}, u32[]{:S(2)}, u32[]{:S(2)}) collective-permute-start(bf16[8,8,16,128]{3,2,1,0:T(8,128)(2,1)S(1)} %get-tuple-element.50), channel_id=1, source_target_pairs={{0,64},{4,68},{8,72},{12,76},{16,80},{20,84},{24,88},{28,92},{32,9... | collective-permute-start | bytes 786440 | tf_op jit(solution)/shard_map/ppermute | solution.py:43
  44.7 15.4 %collective-permute-start.3 = (bf16[8,8,16,128]{3,2,1,0:T(8,128)(2,1)S(1)}, bf16[8,8,16,128]{3,2,1,0:T(8,128)(2,1)S(1)}, u32[]{:S(2)}, u32[]{:S(2)}) collective-permute-start(bf16[8,8,16,128]{3,2,1,0:T(8,128)(2,1)S(1)} %get-tuple-element.52), channel_id=1, source_target_pairs={{0,128},{4,132},{8,136},{12,140},{16,144},{20,148},{24,152},{28,15... | collective-permute-start | bytes 786440 | tf_op jit(solution)/shard_map/ppermute | solution.py:43
  46.7 14.3 %collective-permute-start.4 = (bf16[8,8,16,128]{3,2,1,0:T(8,128)(2,1)S(1)}, bf16[8,8,16,128]{3,2,1,0:T(8,128)(2,1)S(1)}, u32[]{:S(2)}, u32[]{:S(2)}) collective-permute-start(bf16[8,8,16,128]{3,2,1,0:T(8,128)(2,1)S(1)} %get-tuple-element.54), channel_id=1, source_target_pairs={{0,192},{4,196},{8,200},{12,204},{16,208},{20,212},{24,216},{28,22... | collective-permute-start | bytes 786440 | tf_op jit(solution)/shard_map/ppermute | solution.py:43
  64.4 12.9 %collective-permute-start.7 = (bf16[8,8,16,128]{3,2,1,0:T(8,128)(2,1)S(1)}, bf16[8,8,16,128]{3,2,1,0:T(8,128)(2,1)S(1)}, u32[]{:S(2)}, u32[]{:S(2)}) collective-permute-start(bf16[8,8,16,128]{3,2,1,0:T(8,128)(2,1)S(1)} %get-tuple-element.74), channel_id=1, source_target_pairs={{0,192},{4,196},{8,200},{12,204},{16,208},{20,212},{24,216},{28,22... | collective-permute-start | bytes 786440 | tf_op jit(solution)/shard_map/ppermute | solution.py:43
  66.0 11.6 %collective-permute-start.6 = (bf16[8,8,16,128]{3,2,1,0:T(8,128)(2,1)S(1)}, bf16[8,8,16,128]{3,2,1,0:T(8,128)(2,1)S(1)}, u32[]{:S(2)}, u32[]{:S(2)}) collective-permute-start(bf16[8,8,16,128]{3,2,1,0:T(8,128)(2,1)S(1)} %get-tuple-element.73), channel_id=1, source_target_pairs={{0,128},{4,132},{8,136},{12,140},{16,144},{20,148},{24,152},{28,15... | collective-permute-start | bytes 786440 | tf_op jit(solution)/shard_map/ppermute | solution.py:43
  67.1 14.0 %collective-permute-start.5 = (bf16[8,8,16,128]{3,2,1,0:T(8,128)(2,1)S(1)}, bf16[8,8,16,128]{3,2,1,0:T(8,128)(2,1)S(1)}, u32[]{:S(2)}, u32[]{:S(2)}) collective-permute-start(bf16[8,8,16,128]{3,2,1,0:T(8,128)(2,1)S(1)} %get-tuple-element.71), channel_id=1, source_target_pairs={{0,64},{4,68},{8,72},{12,76},{16,80},{20,84},{24,88},{28,92},{32,9... | collective-permute-start | bytes 786440 | tf_op jit(solution)/shard_map/ppermute | solution.py:43
  81.3 1.6 %collective-permute-start.8 = (bf16[8,8,16,128]{3,2,1,0:T(8,128)(2,1)S(1)}, bf16[8,8,16,128]{3,2,1,0:T(8,128)(2,1)S(1)}, u32[]{:S(2)}, u32[]{:S(2)}) collective-permute-start(bf16[8,8,16,128]{3,2,1,0:T(8,128)(2,1)S(1)} %get-tuple-element.76), channel_id=1, source_target_pairs={{0,4},{4,0},{8,12},{12,8},{16,20},{20,16},{24,28},{28,24},{32,36},... | collective-permute-start | bytes 786440 | tf_op jit(solution)/shard_map/ppermute | solution.py:48
  97.9 1.3 %collective-permute-start.9 = (bf16[9,16,128]{2,1,0:T(8,128)(2,1)S(1)}, bf16[9,16,128]{2,1,0:T(8,128)(2,1)S(1)}, u32[]{:S(2)}, u32[]{:S(2)}) collective-permute-start(bf16[9,16,128]{2,1,0:T(8,128)(2,1)S(1)} %get-tuple-element.79.mine), channel_id=1, source_target_pairs={{0,4},{4,0},{8,12},{12,8},{16,20},{20,16},{24,28},{28,24},{32,36},... | collective-permute-start | bytes 110600 | tf_op jit(solution)/shard_map/ppermute | solution.py:48
  115.5 5.3 %collective-permute-start.12 = (f32[1,128]{1,0:T(1,128)S(1)}, f32[1,128]{1,0:T(1,128)S(1)}, u32[]{:S(2)}, u32[]{:S(2)}) collective-permute-start(f32[1,128]{1,0:T(1,128)S(1)} %tally.1), channel_id=1, source_target_pairs={{0,3},{1,0},{2,1},{3,2},{4,7},{5,4},{6,5},{7,6},{8,11},{9,8},{10,9... | collective-permute-start | bytes 1544 | tf_op jit(solution)/shard_map/ppermute | solution.py:53
  118.2 5.0 %collective-permute-start.11 = (f32[1,128]{1,0:T(1,128)S(1)}, f32[1,128]{1,0:T(1,128)S(1)}, u32[]{:S(2)}, u32[]{:S(2)}) collective-permute-start(f32[1,128]{1,0:T(1,128)S(1)} %tally.1), channel_id=1, source_target_pairs={{0,2},{1,3},{2,0},{3,1},{4,6},{5,7},{6,4},{7,5},{8,10},{9,11},{10,... | collective-permute-start | bytes 1544 | tf_op jit(solution)/shard_map/ppermute | solution.py:53
  119.0 4.8 %collective-permute-start.10 = (f32[1,128]{1,0:T(1,128)S(1)}, f32[1,128]{1,0:T(1,128)S(1)}, u32[]{:S(2)}, u32[]{:S(2)}) collective-permute-start(f32[1,128]{1,0:T(1,128)S(1)} %tally.1), channel_id=1, source_target_pairs={{0,1},{1,2},{2,3},{3,0},{4,5},{5,6},{6,7},{7,4},{8,9},{9,10},{10,1... | collective-permute-start | bytes 1544 | tf_op jit(solution)/shard_map/ppermute | solution.py:53

commit v3 on v2

--- a/solution.py
+++ b/solution.py
@@ -20,8 +20,9 @@
 LANES = 128
 HALF = 8
 ROWS = TOK * RATIO
-KINDS = 2 * KV
+QUAD = 4
 PART = 32 * DEPTH
+HAND = (DEPTH, QUAD, 16, LANES)
 F32 = jnp.float32
 BF16 = jnp.bfloat16
 VMEM = pltpu.VMEM
@@ -87,6 +88,63 @@
 INNER = 32
 SELF = 40
 WORDS = 48
+
+
+def packet_kernel(
+    keys_far, values_far, ancestors_far, group, reward, packet, own_kv,
+    keys, values, ancestors, sems,
+):
+    pairs = (
+        (ancestors_far, ancestors),
+        (keys_far, keys),
+        (values_far, values),
+    )
+    copies = [pltpu.make_async_copy(a, b, sems.at[i]) for i, (a, b) in enumerate(pairs)]
+    for copy in copies:
+        copy.start()
+    for copy in copies[:1]:
+        copy.wait()
+    row = lax.broadcasted_iota(jnp.int32, (8, LANES), 0)
+    lane = lax.broadcasted_iota(jnp.int32, (8, LANES), 1)
+    spot = lax.broadcasted_iota(jnp.int32, (8, DEPTH), 0) == lax.broadcasted_iota(
+        jnp.int32, (8, DEPTH), 1
+    )
+    line = jnp.broadcast_to(ancestors[...].astype(F32), (8, DEPTH))
+    line = jnp.sum(jnp.where(spot, line, 0.0), axis=1, keepdims=True)
+    facts = jnp.where(
+        row == 0, group[0].astype(F32), jnp.where(row == 1, reward[0].astype(F32), 0.0)
+    )
+    meta = jnp.where(lane < NBLK, line, facts)
+    for copy in copies[1:]:
+        copy.wait()
+    for h in range(KV):
+        own_kv[2 * h] = keys[:, h, :]
+        own_kv[2 * h + 1] = values[:, h, :]
+    for z in range(NZ):
+        for y in range(NY):
+            at = (z % 2) * 64 + y * 16
+            rows = own_kv[z // 2, at : at + 16, :].astype(F32)
+            packet[y * NZ + z] = jnp.concatenate([rows, meta], 0).astype(BF16)
+
+
+def packet_of(keys, values, ancestors, group, reward):
+    return pl.pallas_call(
+        packet_kernel,
+        in_specs=[pl.BlockSpec(memory_space=pltpu.HBM)] * 3
+        + [pl.BlockSpec(memory_space=pltpu.SMEM)] * 2,
+        out_specs=(in_vmem(),) * 2,
+        **call(
+            packet_kernel,
+            (
+                jax.ShapeDtypeStruct((NY * NZ, 24, LANES), BF16),
+                jax.ShapeDtypeStruct((2 * KV, TOK, HD), BF16),
+            ),
+            [VMEM(x.shape, x.dtype) for x in (keys, values, ancestors)]
+            + [pltpu.SemaphoreType.DMA((3,))],
+            vmem_mb=62,
+        ),
+        name="packet",
+    )(keys, values, ancestors, group, reward)
 
 
 def pack_rows(x, base, first, count):
@@ -189,9 +247,10 @@
     )(mine, other)
 
 
-def deal_kernel(table, mine, other, *outs):
+def deal_kernel(h, table, mine, other, after, *outs):
     c = place()[2]
     words = table[DEAL : DEAL + 8, :]
+    mine, other = mine.at[QUAD * h : QUAD * (h + 1)], other.at[QUAD * h : QUAD * (h + 1)]
     for k in range(NY):
         for d in range(DEPTH):
             slot = (words[2 * k + d // 4, 0] >> (4 * (d % 4))) & 15
@@ -199,14 +258,14 @@
             outs[k][d] = jnp.where((slot & 1) == c, mine[:, at], other[:, at])
 
 
-def deal(table, mine, other):
-    return pl.pallas_call(
-        deal_kernel,
-        in_specs=[in_vmem()] * 3,
+def deal(h, table, mine, other, after):
+    return pl.pallas_call(
+        functools.partial(deal_kernel, h),
+        in_specs=[in_vmem()] * 3 + [pl.BlockSpec(memory_space=pl.ANY)],
         out_specs=(in_vmem(),) * NY,
-        **call(deal_kernel, (jax.ShapeDtypeStruct((DEPTH, NZ, 16, LANES), BF16),) * NY),
+        **call(deal_kernel, (jax.ShapeDtypeStruct(HAND, BF16),) * NY),
         name="deal",
-    )(table, mine, other)
+    )(table, mine, other, after)
 
 
 def prepare_kernel(scale, queries, cotangent, q_all, g_all):
@@ -230,12 +289,11 @@
     )(scale, queries, cotangent)
 
 
-def rows_of(part, kind, h):
-    at = kind * KINDS + 2 * h
-    return part[:, at : at + 2].reshape(PART, HD)
-
-
-def one_part(h, keys, values, q, g, mask, exps, pgs, stats, at):
+def rows_of(part, kind):
+    return part[:, 2 * kind : 2 * kind + 2].reshape(PART, HD)
+
+
+def one_part(keys, values, q, g, mask, exps, pgs, stats, at):
     s = lax.dot_general(keys, q, NT, preferred_element_type=F32) * (
         math.log2(math.e) / math.sqrt(HD)
     )
@@ -243,11 +301,11 @@
     top = jnp.max(s, axis=0, keepdims=True)
     e = jnp.exp2(s - top)
     pg = lax.dot_general(values, g, NT, preferred_element_type=F32)
-    exps[h] = e
-    pgs[h] = pg
-    stats[h, at : at + 1, :] = top
-    stats[h, at + 1 : at + 2, :] = jnp.sum(e, axis=0, keepdims=True)
-    stats[h, at + 2 : at + 3, :] = jnp.sum(e * pg, axis=0, keepdims=True)
+    exps[...] = e
+    pgs[...] = pg
+    stats[at : at + 1, :] = top
+    stats[at + 1 : at + 2, :] = jnp.sum(e, axis=0, keepdims=True)
+    stats[at + 2 : at + 3, :] = jnp.sum(e * pg, axis=0, keepdims=True)
 
 
 def causal(s):
@@ -267,50 +325,44 @@
     return mask
 
 
-def scores_kernel(table, q_all, g_all, part, after, exps, pgs, stats):
-    for h in range(KV):
-        keys, values = rows_of(part, 0, h), rows_of(part, 1, h)
-        one_part(h, keys, values, q_all[h], g_all[h], listed(table), exps, pgs, stats, 0)
-
-
-def first_scores_kernel(
-    table, q_all, g_all, part, own_kv, exps, pgs, stats, own_exps, own_pgs
-):
-    for h in range(KV):
-        keys, values = rows_of(part, 0, h), rows_of(part, 1, h)
-        one_part(h, keys, values, q_all[h], g_all[h], listed(table), exps, pgs, stats, 0)
-        one_part(
-            h, own_kv[h], own_kv[KV + h], q_all[h], g_all[h], causal, own_exps, own_pgs, stats, 4
-        )
+def scores_kernel(h, table, q_all, g_all, part, after, exps, pgs, stats):
+    keys, values = rows_of(part, 0), rows_of(part, 1)
+    one_part(keys, values, q_all[h], g_all[h], listed(table), exps, pgs, stats, 0)
+
+
+def first_scores_kernel(h, table, q_all, g_all, part, own_kv, exps, pgs, stats, own_exps, own_pgs):
+    keys, values = rows_of(part, 0), rows_of(part, 1)
+    q, g = q_all[h], g_all[h]
+    one_part(keys, values, q, g, listed(table), exps, pgs, stats, 0)
+    one_part(own_kv[2 * h], own_kv[2 * h + 1], q, g, causal, own_exps, own_pgs, stats, 4)
 
 
 def wide(keys):
-    return jax.ShapeDtypeStruct((KV, keys, ROWS), F32)
-
-
-def scores_of(table, q_all, g_all, part, after):
-    return pl.pallas_call(
-        scores_kernel,
+    return jax.ShapeDtypeStruct((keys, ROWS), F32)
+
+
+STATS = jax.ShapeDtypeStruct((8, TOK * RATIO), F32)
+
+
+def scores_of(h, table, q_all, g_all, part, after):
+    return pl.pallas_call(
+        functools.partial(scores_kernel, h),
         in_specs=[in_vmem()] * 4 + [pl.BlockSpec(memory_space=pl.ANY)],
         out_specs=(in_vmem(),) * 3,
-        **call(
-            scores_kernel,
-            (wide(PART), wide(PART), jax.ShapeDtypeStruct((KV, 8, ROWS), F32)),
-            vmem_mb=16,
-        ),
+        **call(scores_kernel, (wide(PART), wide(PART), STATS), vmem_mb=16),
         cost_estimate=cost(PART, 2),
         name="scores",
     )(table, q_all, g_all, part, after)
 
 
-def first_scores_of(table, q_all, g_all, part, own_kv):
-    return pl.pallas_call(
-        first_scores_kernel,
+def first_scores_of(h, table, q_all, g_all, part, own_kv):
+    return pl.pallas_call(
+        functools.partial(first_scores_kernel, h),
         in_specs=[in_vmem()] * 5,
         out_specs=(in_vmem(),) * 5,
         **call(
             first_scores_kernel,
-            (wide(PART), wide(PART), jax.ShapeDtypeStruct((KV, 8, ROWS), F32), wide(TOK), wide(TOK)),
+            (wide(PART), wide(PART), STATS, wide(TOK), wide(TOK)),
             vmem_mb=16,
         ),
         cost_estimate=cost(PART + TOK, 2),
@@ -320,27 +372,30 @@
 
 def cost(keys, products):
     return pl.CostEstimate(
-        flops=2 * products * KV * ROWS * keys * HD,
-        bytes_accessed=8 * KV * ROWS * keys,
-        transcendentals=KV * ROWS * keys,
-    )
-
-
-def merge(h, stats):
+        flops=2 * products * ROWS * keys * HD,
+        bytes_accessed=8 * ROWS * keys,
+        transcendentals=ROWS * keys,
+    )
+
+
+SMALL = pl.CostEstimate(flops=1000, bytes_accessed=1000, transcendentals=0)
+
+
+def merge(stats):
     rows = [(ref, 0) for ref in stats] + [(stats[0], 4)]
-    tops = [ref[h, at : at + 1, :] for ref, at in rows]
+    tops = [ref[at : at + 1, :] for ref, at in rows]
     top = tops[0]
     for t in tops[1:]:
         top = jnp.maximum(top, t)
     shares = [jnp.exp2(t - top) for t in tops]
-    norm = sum(s * ref[h, at + 1 : at + 2, :] for s, (ref, at) in zip(shares, rows))
+    norm = sum(s * ref[at + 1 : at + 2, :] for s, (ref, at) in zip(shares, rows))
     norm = 1.0 / norm
     shares = [s * norm for s in shares]
-    delta = sum(s * ref[h, at + 2 : at + 3, :] for s, (ref, at) in zip(shares, rows))
+    delta = sum(s * ref[at + 2 : at + 3, :] for s, (ref, at) in zip(shares, rows))
     return shares, delta
 
 
-def one_grad(h, e, pg, share, delta, q, g, keys):
+def one_grad(e, pg, share, delta, q, g, keys):
     p = e * share
     low = p.astype(BF16)
     ds = (p * (pg - delta)).astype(BF16)
@@ -353,118 +408,120 @@
 
 
 def part_grad(k, h, table, stats, exps, pgs, q_all, g_all, part, own_grad, contrib):
-    shares, delta = merge(h, stats)
+    shares, delta = merge(stats)
     dq, dk, dv = one_grad(
-        h, exps[h], pgs[h], shares[k], delta, q_all[h], g_all[h], rows_of(part, 0, h)
+        exps[...], pgs[...], shares[k], delta, q_all[h], g_all[h], rows_of(part, 0)
     )
     piece = lax.rem(place()[0] + NY - k, NY)
     for kind, grad in enumerate((dk, dv)):
-        at = kind * KINDS + 2 * h
         own = [
-            own_grad[kind * KV + h, pl.ds(pl.multiple_of(half * 64 + piece * 16, 16), 16), :]
+            own_grad[kind, pl.ds(pl.multiple_of(half * 64 + piece * 16, 16), 16), :]
             for half in range(2)
         ]
         own = jnp.concatenate(own, 0)
         for d in range(DEPTH):
             mark = table[SELF + d : SELF + d + 1, :] > 0
             both = jnp.where(mark, own, grad[32 * d : 32 * d + 32])
-            contrib[d, at : at + 2] = both.astype(BF16).reshape(2, 16, HD)
+            contrib[d, 2 * kind : 2 * kind + 2] = both.astype(BF16).reshape(2, 16, HD)
     return dq
 
 
 def first_grads_kernel(
-    k, table, s0, s1, s2, s3, exps, pgs, q_all, g_all, part, own_exps, own_pgs, own_kv,
+    k, h, table, s0, s1, s2, s3, exps, pgs, q_all, g_all, part, own_exps, own_pgs, own_kv,
     dq_sum, own_grad, contrib,
 ):
     stats = (s0, s1, s2, s3)
-    for h in range(KV):
-        shares, delta = merge(h, stats)
-        dq, dk, dv = one_grad(
-            h, own_exps[h], own_pgs[h], shares[NY], delta, q_all[h], g_all[h], own_kv[h]
-        )
-        own_grad[h] = dk
-        own_grad[KV + h] = dv
-        dq_sum[h] = dq + part_grad(
-            k, h, table, stats, exps, pgs, q_all, g_all, part, own_grad, contrib
-        )
+    shares, delta = merge(stats)
+    dq, dk, dv = one_grad(
+        own_exps[...], own_pgs[...], shares[NY], delta, q_all[h], g_all[h], own_kv[2 * h]
+    )
+    own_grad[0] = dk
+    own_grad[1] = dv
+    dq_sum[...] = dq + part_grad(
+        k, h, table, stats, exps, pgs, q_all, g_all, part, own_grad, contrib
+    )
 
 
 def grads_kernel(
-    k, table, s0, s1, s2, s3, exps, pgs, q_all, g_all, part, own_grad, dq_in, dq_sum, contrib
+    k, h, table, s0, s1, s2, s3, exps, pgs, q_all, g_all, part, own_grad, dq_in, *outs
 ):
-    for h in range(KV):
-        dq_sum[h] = dq_in[h] + part_grad(
-            k, h, table, (s0, s1, s2, s3), exps, pgs, q_all, g_all, part, own_grad, contrib
-        )
-
-
-def last_grads_kernel(
-    k, table, s0, s1, s2, s3, exps, pgs, q_all, g_all, part, own_grad, dq_in,
-    query_grad, contrib, squares,
-):
+    dq_sum, contrib = outs[-2:]
+    dq_sum[...] = dq_in[...] + part_grad(
+        k, h, table, (s0, s1, s2, s3), exps, pgs, q_all, g_all, part, own_grad, contrib
+    )
+
+
+def emit_kernel(table, dq_0, dq_1, own_0, own_1, query_grad, squares):
     total = jnp.zeros((8, HD), F32)
-    for h in range(KV):
-        dq = dq_in[h] + part_grad(
-            k, h, table, (s0, s1, s2, s3), exps, pgs, q_all, g_all, part, own_grad, contrib
-        )
-        dq = dq.T * (1.0 / math.sqrt(HD))
+    own_total = jnp.zeros((8, HD), F32)
+    for h, (dq, own) in enumerate(((dq_0, own_0), (dq_1, own_1))):
+        dq = dq[...].T * (1.0 / math.sqrt(HD))
         total = total + jnp.sum((dq * dq).reshape(ROWS // 8, 8, HD), axis=0)
         query_grad[:, RATIO * h : RATIO * (h + 1), :] = dq.reshape(TOK, RATIO, HD)
-    own = own_grad[...]
-    own_squares = jnp.sum((own * own).reshape(2 * KV * TOK // 8, 8, HD), axis=0)
-    squares[...] = total + jnp.where(table[INNER : INNER + 8, :] > 0, 0.0, own_squares)
-
-
-DQ_SUM = (KV, HD, TOK * RATIO)
-OWN = (2 * KV, TOK, HD)
-CONTRIB = (DEPTH, NZ, 16, LANES)
-
-
-def grads_of(body, name, outs, k, *arrays):
-    return pl.pallas_call(
-        functools.partial(body, k),
+        own = own[...]
+        own_total = own_total + jnp.sum((own * own).reshape(2 * TOK // 8, 8, HD), axis=0)
+    squares[...] = total + jnp.where(table[INNER : INNER + 8, :] > 0, 0.0, own_total)
+
+
+def emit(table, dqs, owns):
+    return pl.pallas_call(
+        emit_kernel,
+        in_specs=[in_vmem()] * 5,
+        out_specs=(in_vmem(),) * 2,
+        **call(
+            emit_kernel,
+            (
+                jax.ShapeDtypeStruct((TOK, KV * RATIO, HD), F32),
+                jax.ShapeDtypeStruct((8, LANES), F32),
+            ),
+            vmem_mb=16,
+        ),
+        cost_estimate=SMALL,
+        name="emit",
+    )(table, *dqs, *owns)
+
+
+def grads_of(body, name, outs, k, h, *arrays):
+    return pl.pallas_call(
+        functools.partial(body, k, h),
         in_specs=[in_vmem()] * len(arrays),
         out_specs=(in_vmem(),) * len(outs),
         **call(body, outs, vmem_mb=16),
-        cost_estimate=pl.CostEstimate(flops=1000, bytes_accessed=1000, transcendentals=0),
+        cost_estimate=SMALL,
         name=name,
     )(*arrays)
 
 
-def attend(table, scale, queries, cotangent, own_kv, parts):
-    q_all, g_all = prepare(scale, queries, cotangent)
+def attend(h, table, q_all, g_all, own_kv, parts, after):
     e, pg, st = [None] * NY, [None] * NY, [None] * NY
-    e[0], pg[0], st[0], own_e, own_pg = first_scores_of(table, q_all, g_all, parts[0], own_kv)
-    after = st[0]
+    e[0], pg[0], st[0], own_e, own_pg = first_scores_of(h, table, q_all, g_all, parts[0], own_kv)
+    after = st[0] if after is None else after
     for k in (1, 2, 3):
-        e[k], pg[k], st[k] = scores_of(table, q_all, g_all, parts[k], after)
+        e[k], pg[k], st[k] = scores_of(h, table, q_all, g_all, parts[k], after)
         after = st[k]
     back = [None] * NY
-    dq_type = jax.ShapeDtypeStruct(DQ_SUM, F32)
-    own_type = jax.ShapeDtypeStruct(OWN, F32)
-    contrib_type = jax.ShapeDtypeStruct(CONTRIB, BF16)
-    for k in (2, 1, 3, 0):
-        shared = (table, *st, e[k], pg[k], q_all, g_all, parts[k])
-        if k == 2:
-            dq, own_grad, back[k] = grads_of(
-                first_grads_kernel, "grads_first", (dq_type, own_type, contrib_type), k,
-                *shared, own_e, own_pg, own_kv,
-            )
-        elif k:
-            dq, back[k] = grads_of(
-                grads_kernel, "grads", (dq_type, contrib_type), k, *shared, own_grad, dq
-            )
-        else:
-            query_grad, back[k], squares = grads_of(
-                last_grads_kernel, "grads_last",
-                (
-                    jax.ShapeDtypeStruct((TOK, KV * RATIO, HD), F32),
-                    contrib_type,
-                    jax.ShapeDtypeStruct((8, LANES), F32),
-                ),
-                k, *shared, own_grad, dq,
-            )
-    return query_grad, own_grad, *back, squares
+    dq_type = jax.ShapeDtypeStruct((HD, ROWS), F32)
+    own_type = jax.ShapeDtypeStruct((2, TOK, HD), F32)
+    contrib_type = jax.ShapeDtypeStruct(HAND, BF16)
+
+    def shared(k):
+        return (table, *st, e[k], pg[k], q_all, g_all, parts[k])
+
+    dq, own_grad, back[2] = grads_of(
+        first_grads_kernel, "grads_first", (dq_type, own_type, contrib_type), 2, h,
+        *shared(2), own_e, own_pg, own_kv,
+    )
+    for k in (1, 3):
+        dq, back[k] = grads_of(
+            grads_kernel, "grads", (dq_type, contrib_type), k, h, *shared(k), own_grad, dq
+        )
+
+    def last(after):
+        return grads_of(
+            grads_kernel, "grads_last", (dq_type, contrib_type), 0, h, *shared(0), own_grad, dq, after
+        )
+
+    return dq, own_grad, back, last
 
 
 def add_part(k, table, part, acc):
@@ -475,7 +532,7 @@
         acc[at & 1, at >> 1] += jnp.where(slot > 0, part[d].astype(F32), 0.0)
 
 
-def combine_first_kernel(table, part, acc):
+def combine_first_kernel(table, part, after, acc):
     acc[...] = jnp.zeros_like(acc)
     add_part(1, table, part, acc)
 
@@ -493,24 +550,23 @@
         keep[:, s] = acc[c, s]
 
 
-def combine(table, parts):
-    acc_type = jax.ShapeDtypeStruct((2, HALF, NZ, 16, LANES), F32)
-    small = pl.CostEstimate(flops=1000, bytes_accessed=1000, transcendentals=0)
+def combine(table, parts, after):
+    acc_type = jax.ShapeDtypeStruct((2, HALF, QUAD, 16, LANES), F32)
     acc = pl.pallas_call(
         combine_first_kernel,
-        in_specs=[in_vmem()] * 2,
+        in_specs=[in_vmem()] * 2 + [pl.BlockSpec(memory_space=pl.ANY)],
         out_specs=in_vmem(),
         **call(combine_first_kernel, acc_type, vmem_mb=16),
-        cost_estimate=small,
+        cost_estimate=SMALL,
         name="combine_first",
-    )(table, parts[1])
+    )(table, parts[1], after)
     acc = pl.pallas_call(
         combine_kernel,
         in_specs=[in_vmem()] * 3,
         out_specs=in_vmem(),
         input_output_aliases={2: 0},
         **call(combine_kernel, acc_type, vmem_mb=16),
-        cost_estimate=small,
+        cost_estimate=SMALL,
         name="combine",
     )(table, parts[2], acc)
     keep, send, _ = pl.pallas_call(
@@ -521,16 +577,32 @@
         **call(
             combine_last_kernel,
             (
-                jax.ShapeDtypeStruct((NZ, HALF, 16, LANES), F32),
-                jax.ShapeDtypeStruct((NZ, HALF, 16, LANES), BF16),
+                jax.ShapeDtypeStruct((QUAD, HALF, 16, LANES), F32),
+                jax.ShapeDtypeStruct((QUAD, HALF, 16, LANES), BF16),
                 acc_type,
             ),
             vmem_mb=16,
         ),
-        cost_estimate=small,
+        cost_estimate=SMALL,
         name="combine_last",
     )(table, parts[3], parts[0], acc)
     return keep, send
+
+
+def join_kernel(k0, r0, k1, r1, halves):
+    for h, (keep, got) in enumerate(((k0, r0), (k1, r1))):
+        halves[QUAD * h : QUAD * (h + 1)] = (keep[...] + got[...].astype(F32)).astype(BF16)
+
+
+def join(*arrays):
+    return pl.pallas_call(
+        join_kernel,
+        in_specs=[in_vmem()] * 4,
+        out_specs=in_vmem(),
+        **call(join_kernel, jax.ShapeDtypeStruct((NZ, HALF, 16, LANES), BF16)),
+        cost_estimate=SMALL,
+        name="join",
+    )(*arrays)
 
 
 def split_rows(value, rows):
@@ -613,62 +685,69 @@
     )(arrived)
 
 
-def finish_kernel(table, arrived, own_grad, key_grad, value_grad):
+def finish_kernel(table, arrived, own_0, own_1, key_grad, value_grad):
     inner = table[INNER : INNER + 1, :] > 0
     for z in range(NZ):
-        kind, h, half = z // 4, z // 2 % 2, z % 2
+        h, kind, half = z // 4, z // 2 % 2, z % 2
         out = value_grad if kind else key_grad
+        own_grad = own_1 if h else own_0
         for y in range(NY):
             at = half * 64 + y * 16
             piece = arrived[y * NZ + z].astype(F32)[0:16, :]
-            own = own_grad[kind * KV + h, at : at + 16, :]
-            out[at : at + 16, h, :] = jnp.where(inner, piece, own)
-
-
-def finish(table, arrived, own_grad):
+            out[at : at + 16, h, :] = jnp.where(inner, piece, own_grad[kind, at : at + 16, :])
+
+
+def finish(table, arrived, owns):
     return pl.pallas_call(
         finish_kernel,
-        in_specs=[in_vmem()] * 3,
+        in_specs=[in_vmem()] * 4,
         out_specs=(in_vmem(),) * 2,
         **call(finish_kernel, (jax.ShapeDtypeStruct((TOK, KV, HD), F32),) * 2),
-        cost_estimate=pl.CostEstimate(flops=1000, bytes_accessed=1000, transcendentals=0),
+        cost_estimate=SMALL,
         name="finish",
-    )(table, arrived, own_grad)
+    )(table, arrived, *owns)
 
 
 def local(queries, keys, values, cotangent, rewards, groups, ancestors, step_ids):
-    own_kv = jnp.stack([keys, values]).transpose(0, 2, 1, 3)
-    pieces = (
-        own_kv.reshape(2, KV, 2, NY, 16, HD).transpose(3, 0, 1, 2, 4, 5).reshape(NY * NZ, 16, HD)
-    )
-    own_kv = own_kv.reshape(2 * KV, TOK, HD)
-    line = jnp.broadcast_to(ancestors[0].astype(BF16)[:, None], (8, NBLK))
-    facts = jnp.concatenate(
-        [groups.astype(BF16), rewards, jnp.zeros((6,), BF16)]
-    )
-    meta = jnp.concatenate([line, jnp.broadcast_to(facts[:, None], (8, LANES - NBLK))], 1)
-    packet = jnp.concatenate([pieces, jnp.broadcast_to(meta[None], (NY * NZ, 8, LANES))], 1)
+    packet, own_kv = packet_of(
+        keys, values, ancestors, groups, rewards
+    )
     mine = swap_yz(packet)
     other = other_core(mine)
     trained = (step_ids[0] % 2 == 0)[:, None, None]
     masked = jnp.where(trained, cotangent, jnp.zeros_like(cotangent))
     picked, table, scale = plan(mine, other)
     column = swap_z(picked)
-    dealt = deal(table, column, other_core(column))
-    parts = [dealt[0]] + [along_y(dealt[k], k) for k in (1, 2, 3)]
-    query_grad, own_grad, c0, c1, c2, c3, squares = attend(
-        table, scale, queries, masked, own_kv, parts
-    )
-    back = [c0] + [along_y(x, -k) for k, x in ((1, c1), (2, c2), (3, c3))]
-    keep, send = combine(table, back)
-    halves = (keep + other_core(send).astype(F32)).astype(BF16)
+    column_other = other_core(column)
+    q_all, g_all = prepare(scale, queries, masked)
+    parts = []
+    for h in range(KV):
+        dealt = deal(h, table, column, column_other, g_all)
+        parts.append([dealt[0]] + [along_y(dealt[k], k) for k in (1, 2, 3)])
+    heads, after = [], None
+    for h in range(KV):
+        after, own_grad, sent, last = attend(h, table, q_all, g_all, own_kv, parts[h], after)
+        back = [None] + [along_y(sent[k], -k) for k in (1, 2, 3)]
+        heads.append((own_grad, back, last))
+    owns = [own_grad for own_grad, _, _ in heads]
+    dqs, halves = [], []
+    for h, (_, back, last) in enumerate(heads):
+        dq, back[0] = last(after)
+        dqs.append(dq)
+        after = dq
+        if h == KV - 1:
+            query_grad, squares = emit(table, dqs, owns)
+            after = squares
+        keep, send = combine(table, back, after)
+        halves += [keep, other_core(send)]
+    halves = join(*halves)
     sums, pack = total_of(swap_z(halves), squares)
     arrived = swap_yz(route(table, sums, pack, other_core(pack)))
     mine_sum = tally(arrived)
     all_sum = mine_sum
     for k in (1, 2, 3):
         all_sum = all_sum + along_head(mine_sum, k)
-    key_grad, value_grad = finish(table, arrived, own_grad)
+    key_grad, value_grad = finish(table, arrived, owns)
     count = float(NBLK * TOK * NHEAD * (KV * RATIO + 2 * KV) * HD)
     grad_rms = jnp.sqrt(all_sum[0, 0] / count)
     return query_grad, key_grad, value_grad, grad_rms

time: 125 us -> 122 us (0.976)
  waiting for transfers between devices: 28.4 us -> 13.3 us
  starting transfers between devices: 11.4 us -> 21.4 us
  Pallas kernels: 12.2 us -> 15.8 us
  other arithmetic: 2.38 us -> 0.22 us
    ppermute x6 -> x12, waiting for transfers between devices: 19.9 us -> 5.99 us  [along_y(): return lax.ppermute(x, 'branch', pairs)]
    ppermute x6 -> x12, starting transfers between devices: 6.78 us -> 16.6 us  [along_y(): return lax.ppermute(x, 'branch', pairs)]
    pallas_call x11 -> x24, Pallas kernels: 10.9 us -> 14.3 us  [the longest x8 4.9 us: grads_of(): pl.pallas_call(functools.partial(body, k, h), in_specs=[in_vmem()] * len(...]
    ppermute x4 -> x5, waiting for transfers between devices: 5.43 us -> 4.27 us  [other_core(): return lax.ppermute(x, 'branch', pairs)]
  transfers between devices with their start and end apart: 13 -> 20, of which waited for: 9 -> 10; matrix products, arithmetic and copies ran while one was open for 0% -> 0% of each run, Pallas kernels for 6% -> 10%
where the time goes in v3:
time: 122 us
  blocking collectives  67.1 us (55%)
  starting transfers between devices  21.4 us (18%)
  Pallas kernels  15.8 us (13%)
  waiting for transfers between devices  13.3 us (11%)
  between operations  3.47 us (3%)
    all_to_all x2, blocking collectives, swap_yz(): lax.all_to_all(x, 'branch', 0, 0, axis_index_groups=groups, tiled=False)  38.2 us
    all_to_all x2, blocking collectives, swap_z(): lax.all_to_all(x, 'branch', 0, 0, axis_index_groups=groups, tiled=False)  28.9 us
    ppermute x12, starting transfers between devices, along_y(): return lax.ppermute(x, 'branch', pairs)  16.6 us
    ppermute x12, waiting for transfers between devices, along_y(): return lax.ppermute(x, 'branch', pairs)  5.99 us
    pallas_call x8, Pallas kernels, grads_of(): pl.pallas_call(functools.partial(body, k, h), in_specs=[in_vmem()] * len(...  4.9 us
    ppermute x3, starting transfers between devices, along_head(): return lax.ppermute(x, 'head', pairs)  4.46 us
    ppermute x5, waiting for transfers between devices, other_core(): return lax.ppermute(x, 'branch', pairs)  4.27 us
    ppermute x3, waiting for transfers between devices, along_head(): return lax.ppermute(x, 'head', pairs)  3.03 us
  transfers between devices with their start and end apart: 20, of which 10 were waited for; matrix products, arithmetic and copies ran while one was open for 0% of the time, Pallas kernels for 10%

profile of v3, /device:TPU:32, one launch (start us, length us, event | category | flops | bytes accessed | tf_op | source)
XLA Modules:
  0.0 122.1 jit_solution(16311923803061563850)
XLA Ops:
  1.9 2.2 %packet.1 = (bf16[32,24,128]{2,1,0:T(8,128)(2,1)}, bf16[4,128,128]{2,1,0:T(8,128)(2,1)}) custom-call(bf16[128,2,128]{2,1,0:T(2,128)(2,1)} %keys_far.1, bf16[128,2,128]{2,1,0:T(2,128)(2,1)} %values_far.1, s32[1,8]{1,0:T(1,128)} %ancestors_far.1, s32[1]{0:T(128)S(6)} %copy.21.group, bf16[1]{0:T(256)(128)(2,1)S(6)} %copy.20.reward), custom_call_target="tpu_custom_call" | custom-call | tf_op jit(solution)/shard_map/packet/pallas_call | solution.py:131
  4.1 22.4 %all_to_all.20.mine = bf16[32,24,128]{2,1,0:T(8,128)(2,1)S(1)} all-to-all(bf16[32,24,128]{2,1,0:T(8,128)(2,1)} %get-tuple-element.75), channel_id=1, replica_groups={{0,8,16,24,32,40,48,56,64,72,80,88,96,104,112,120,128,136,144,152,160,1..., dimensions={0} | all-to-all | bytes 393216 | tf_op jit(solution)/shard_map/all_to_all | solution.py:64
  26.5 1.4 %collective-permute-done.other = bf16[32,24,128]{2,1,0:T(8,128)(2,1)S(1)} collective-permute-done((bf16[32,24,128]{2,1,0:T(8,128)(2,1)S(1)}, bf16[32,24,128]{2,1,0:T(8,128)(2,1)S(1)}, u32[]{:S(2)}, u32[]{:S(2)}) %collective-permute-start) | collective-permute-done | bytes 196640 | tf_op jit(solution)/shard_map/ppermute | solution.py:49
  28.3 14.1 %all_to_all.21.mine = bf16[8,8,16,128]{3,2,1,0:T(8,128)(2,1)S(1)} all-to-all(bf16[8,8,16,128]{3,2,1,0:T(8,128)(2,1)S(1)} %get-tuple-element.80), channel_id=1, replica_groups={{0,8,16,24,32,40,48,56},{4,12,20,28,36,44,52,60},{64,72,80,88,96,104,11..., dimensions={0} | all-to-all | bytes 524288 | tf_op jit(solution)/shard_map/all_to_all | solution.py:59
  42.6 0.8 copy-done.1
  44.7 2.0 %collective-permute-start.3 = (bf16[8,4,16,128]{3,2,1,0:T(8,128)(2,1)S(1)}, bf16[8,4,16,128]{3,2,1,0:T(8,128)(2,1)S(1)}, u32[]{:S(2)}, u32[]{:S(2)}) collective-permute-start(bf16[8,4,16,128]{3,2,1,0:T(8,128)(2,1)S(1)} %get-tuple-element.86), channel_id=1, source_target_pairs={{0,128},{4,132},{8,136},{12,140},{16,144},{20,148},{24,152},{28,15... | collective-permute-start | bytes 393224 | tf_op jit(solution)/shard_map/ppermute | solution.py:44
  46.8 1.3 %collective-permute-start.4 = (bf16[8,4,16,128]{3,2,1,0:T(8,128)(2,1)S(1)}, bf16[8,4,16,128]{3,2,1,0:T(8,128)(2,1)S(1)}, u32[]{:S(2)}, u32[]{:S(2)}) collective-permute-start(bf16[8,4,16,128]{3,2,1,0:T(8,128)(2,1)S(1)} %get-tuple-element.88), channel_id=1, source_target_pairs={{0,192},{4,196},{8,200},{12,204},{16,208},{20,212},{24,216},{28,22... | collective-permute-start | bytes 393224 | tf_op jit(solution)/shard_map/ppermute | solution.py:44
  49.1 1.6 %collective-permute-start.6 = (bf16[8,4,16,128]{3,2,1,0:T(8,128)(2,1)S(1)}, bf16[8,4,16,128]{3,2,1,0:T(8,128)(2,1)S(1)}, u32[]{:S(2)}, u32[]{:S(2)}) collective-permute-start(bf16[8,4,16,128]{3,2,1,0:T(8,128)(2,1)S(1)} %get-tuple-element.108), channel_id=1, source_target_pairs={{0,128},{4,132},{8,136},{12,140},{16,144},{20,148},{24,152},{28,15... | collective-permute-start | bytes 393224 | tf_op jit(solution)/shard_map/ppermute | solution.py:44
  51.4 2.8 %collective-permute-done.2.part = bf16[8,4,16,128]{3,2,1,0:T(8,128)(2,1)S(1)} collective-permute-done((bf16[8,4,16,128]{3,2,1,0:T(8,128)(2,1)S(1)}, bf16[8,4,16,128]{3,2,1,0:T(8,128)(2,1)S(1)}, u32[]{:S(2)}, u32[]{:S(2)}) %collective-permute-start.2) | collective-permute-done | bytes 131104 | tf_op jit(solution)/shard_map/ppermute | solution.py:44
  57.3 3.8 %collective-permute-start.10 = (bf16[8,4,16,128]{3,2,1,0:T(8,128)(2,1)S(1)}, bf16[8,4,16,128]{3,2,1,0:T(8,128)(2,1)S(1)}, u32[]{:S(2)}, u32[]{:S(2)}) collective-permute-start(bf16[8,4,16,128]{3,2,1,0:T(8,128)(2,1)S(1)} %get-tuple-element.132), channel_id=1, source_target_pairs={{0,192},{4,196},{8,200},{12,204},{16,208},{20,212},{24,216},{28,22... | collective-permute-start | bytes 393224 | tf_op jit(solution)/shard_map/ppermute | solution.py:44
  62.4 1.5 %collective-permute-start.9 = (bf16[8,4,16,128]{3,2,1,0:T(8,128)(2,1)S(1)}, bf16[8,4,16,128]{3,2,1,0:T(8,128)(2,1)S(1)}, u32[]{:S(2)}, u32[]{:S(2)}) collective-permute-start(bf16[8,4,16,128]{3,2,1,0:T(8,128)(2,1)S(1)} %get-tuple-element.131), channel_id=1, source_target_pairs={{0,128},{4,132},{8,136},{12,140},{16,144},{20,148},{24,152},{28,15... | collective-permute-start | bytes 393224 | tf_op jit(solution)/shard_map/ppermute | solution.py:44
  66.8 1.8 %collective-permute-start.14 = (bf16[8,4,16,128]{3,2,1,0:T(8,128)(2,1)S(1)}, bf16[8,4,16,128]{3,2,1,0:T(8,128)(2,1)S(1)}, u32[]{:S(2)}, u32[]{:S(2)}) collective-permute-start(bf16[8,4,16,128]{3,2,1,0:T(8,128)(2,1)S(1)} %get-tuple-element.138), channel_id=1, source_target_pairs={{0,192},{4,196},{8,200},{12,204},{16,208},{20,212},{24,216},{28,22... | collective-permute-start | bytes 393224 | tf_op jit(solution)/shard_map/ppermute | solution.py:44
  68.6 2.9 %collective-permute-start.13 = (bf16[8,4,16,128]{3,2,1,0:T(8,128)(2,1)S(1)}, bf16[8,4,16,128]{3,2,1,0:T(8,128)(2,1)S(1)}, u32[]{:S(2)}, u32[]{:S(2)}) collective-permute-start(bf16[8,4,16,128]{3,2,1,0:T(8,128)(2,1)S(1)} %get-tuple-element.137), channel_id=1, source_target_pairs={{0,128},{4,132},{8,136},{12,140},{16,144},{20,148},{24,152},{28,15... | collective-permute-start | bytes 393224 | tf_op jit(solution)/shard_map/ppermute | solution.py:44
  73.4 1.3 %emit.1 = (f32[128,16,128]{2,1,0:T(8,128)}, f32[8,128]{1,0:T(8,128)S(1)}) custom-call(s32[48,128]{1,0:T(8,128)S(1)} %get-tuple-element.76.table, f32[128,1024]{1,0:T(8,128)S(1)} %get-tuple-element.124.outs_0_.dq_0.after, f32[128,1024]{1,0:T(8,128)S(1)} %get-tuple-element.127.dq_1, f32[2,128,128]{2,1,0:T(8,128)S(1)} %get-tuple-element.96.own_grad.own_0, ...), custom_call_target="tpu_custom_call" | custom-call | flops 1000 | bytes 1000 | tf_op jit(solution)/shard_map/emit/pallas_call | solution.py:467
  75.8 2.6 %collective-permute-done.12.part = bf16[8,4,16,128]{3,2,1,0:T(8,128)(2,1)S(1)} collective-permute-done((bf16[8,4,16,128]{3,2,1,0:T(8,128)(2,1)S(1)}, bf16[8,4,16,128]{3,2,1,0:T(8,128)(2,1)S(1)}, u32[]{:S(2)}, u32[]{:S(2)}) %collective-permute-start.12) | collective-permute-done | bytes 131104 | tf_op jit(solution)/shard_map/ppermute | solution.py:44
  78.7 1.3 %collective-permute-done.15.r1 = bf16[4,8,16,128]{3,2,1,0:T(8,128)(2,1)S(1)} collective-permute-done((bf16[4,8,16,128]{3,2,1,0:T(8,128)(2,1)S(1)}, bf16[4,8,16,128]{3,2,1,0:T(8,128)(2,1)S(1)}, u32[]{:S(2)}, u32[]{:S(2)}) %collective-permute-start.15) | collective-permute-done | bytes 131104 | tf_op jit(solution)/shard_map/ppermute | solution.py:49
  80.1 14.9 %all_to_all.22.parts = bf16[8,8,16,128]{3,2,1,0:T(8,128)(2,1)S(1)} all-to-all(bf16[8,8,16,128]{3,2,1,0:T(8,128)(2,1)S(1)} %join.1), channel_id=1, replica_groups={{0,8,16,24,32,40,48,56},{4,12,20,28,36,44,52,60},{64,72,80,88,96,104,11..., dimensions={0} | all-to-all | bytes 524288 | tf_op jit(solution)/shard_map/all_to_all | solution.py:59
  95.1 1.2 collective-permute-done.16.other
  96.6 15.8 %all_to_all.23.arrived = bf16[32,24,128]{2,1,0:T(8,128)(2,1)S(1)} all-to-all(bf16[32,24,128]{2,1,0:T(8,128)(2,1)S(1)} %route.1), channel_id=1, replica_groups={{0,8,16,24,32,40,48,56,64,72,80,88,96,104,112,120,128,136,144,152,160,1..., dimensions={0} | all-to-all | bytes 393216 | tf_op jit(solution)/shard_map/all_to_all | solution.py:64
  112.5 2.8 %collective-permute-start.19 = (f32[1,128]{1,0:T(1,128)S(1)}, f32[1,128]{1,0:T(1,128)S(1)}, u32[]{:S(2)}, u32[]{:S(2)}) collective-permute-start(f32[1,128]{1,0:T(1,128)S(1)} %tally.1), channel_id=1, source_target_pairs={{0,3},{1,0},{2,1},{3,2},{4,7},{5,4},{6,5},{7,6},{8,11},{9,8},{10,9... | collective-permute-start | bytes 1544 | tf_op jit(solution)/shard_map/ppermute | solution.py:54
  115.3 0.8 collective-permute-start.18
  116.1 0.9 collective-permute-start.17
  117.0 0.8 finish.1
  117.8 2.5 %collective-permute-done.18 = f32[1,128]{1,0:T(1,128)S(1)} collective-permute-done((f32[1,128]{1,0:T(1,128)S(1)}, f32[1,128]{1,0:T(1,128)S(1)}, u32[]{:S(2)}, u32[]{:S(2)}) %collective-permute-start.18) | collective-permute-done | bytes 544 | tf_op jit(solution)/shard_map/ppermute | solution.py:54
  (64 shorter events, 15.0 us)
Async XLA Ops:
  26.5 15.9 %copy-start.2 = (bf16[128,16,128]{2,1,0:T(8,128)(2,1)S(1)}, bf16[128,16,128]{2,1,0:T(8,128)(2,1)}, u32[]{:S(2)}) copy-start(bf16[128,16,128]{2,1,0:T(8,128)(2,1)} %param.11) | copy-start | bytes 1572868
  26.5 1.4 %collective-permute-start = (bf16[32,24,128]{2,1,0:T(8,128)(2,1)S(1)}, bf16[32,24,128]{2,1,0:T(8,128)(2,1)S(1)}, u32[]{:S(2)}, u32[]{:S(2)}) collective-permute-start(bf16[32,24,128]{2,1,0:T(8,128)(2,1)S(1)} %all_to_all.20.mine), channel_id=1, source_target_pairs={{0,4},{4,0},{8,12},{12,8},{16,20},{20,16},{24,28},{28,24},{32,36},... | collective-permute-start | bytes 589832 | tf_op jit(solution)/shard_map/ppermute | solution.py:49
  28.2 14.1 %copy-start.3 = (s32[1,128]{1,0:T(1,128)S(1)}, s32[1,128]{1,0:T(1,128)}, u32[]{:S(2)}) copy-start(s32[1,128]{1,0:T(1,128)} %param.15) | copy-start | bytes 1540
  42.3 1.5 %collective-permute-start.1 = (bf16[8,8,16,128]{3,2,1,0:T(8,128)(2,1)S(1)}, bf16[8,8,16,128]{3,2,1,0:T(8,128)(2,1)S(1)}, u32[]{:S(2)}, u32[]{:S(2)}) collective-permute-start(bf16[8,8,16,128]{3,2,1,0:T(8,128)(2,1)S(1)} %all_to_all.21.mine), channel_id=1, source_target_pairs={{0,4},{4,0},{8,12},{12,8},{16,20},{20,16},{24,28},{28,24},{32,36},... | collective-permute-start | bytes 786440 | tf_op jit(solution)/shard_map/ppermute | solution.py:49
  42.3 1.0 copy-start.1
  44.1 10.2 %collective-permute-start.2 = (bf16[8,4,16,128]{3,2,1,0:T(8,128)(2,1)S(1)}, bf16[8,4,16,128]{3,2,1,0:T(8,128)(2,1)S(1)}, u32[]{:S(2)}, u32[]{:S(2)}) collective-permute-start(bf16[8,4,16,128]{3,2,1,0:T(8,128)(2,1)S(1)} %get-tuple-element.84), channel_id=1, source_target_pairs={{0,64},{4,68},{8,72},{12,76},{16,80},{20,84},{24,88},{28,92},{32,9... | collective-permute-start | bytes 393224 | tf_op jit(solution)/shard_map/ppermute | solution.py:44
  44.7 10.0 %collective-permute-start.3 = (bf16[8,4,16,128]{3,2,1,0:T(8,128)(2,1)S(1)}, bf16[8,4,16,128]{3,2,1,0:T(8,128)(2,1)S(1)}, u32[]{:S(2)}, u32[]{:S(2)}) collective-permute-start(bf16[8,4,16,128]{3,2,1,0:T(8,128)(2,1)S(1)} %get-tuple-element.86), channel_id=1, source_target_pairs={{0,128},{4,132},{8,136},{12,140},{16,144},{20,148},{24,152},{28,15... | collective-permute-start | bytes 393224 | tf_op jit(solution)/shard_map/ppermute | solution.py:44
  46.8 3.9 %copy-start = (bf16[4,128,128]{2,1,0:T(8,128)(2,1)S(1)}, bf16[4,128,128]{2,1,0:T(8,128)(2,1)}, u32[]{:S(2)}) copy-start(bf16[4,128,128]{2,1,0:T(8,128)(2,1)} %get-tuple-element.82.own_kv) | copy-start | bytes 393220
  46.8 8.6 %collective-permute-start.4 = (bf16[8,4,16,128]{3,2,1,0:T(8,128)(2,1)S(1)}, bf16[8,4,16,128]{3,2,1,0:T(8,128)(2,1)S(1)}, u32[]{:S(2)}, u32[]{:S(2)}) collective-permute-start(bf16[8,4,16,128]{3,2,1,0:T(8,128)(2,1)S(1)} %get-tuple-element.88), channel_id=1, source_target_pairs={{0,192},{4,196},{8,200},{12,204},{16,208},{20,212},{24,216},{28,22... | collective-permute-start | bytes 393224 | tf_op jit(solution)/shard_map/ppermute | solution.py:44
  48.3 14.1 %collective-permute-start.5 = (bf16[8,4,16,128]{3,2,1,0:T(8,128)(2,1)S(1)}, bf16[8,4,16,128]{3,2,1,0:T(8,128)(2,1)S(1)}, u32[]{:S(2)}, u32[]{:S(2)}) collective-permute-start(bf16[8,4,16,128]{3,2,1,0:T(8,128)(2,1)S(1)} %get-tuple-element.106), channel_id=1, source_target_pairs={{0,64},{4,68},{8,72},{12,76},{16,80},{20,84},{24,88},{28,92},{32,9... | collective-permute-start | bytes 393224 | tf_op jit(solution)/shard_map/ppermute | solution.py:44
  49.1 15.3 %collective-permute-start.6 = (bf16[8,4,16,128]{3,2,1,0:T(8,128)(2,1)S(1)}, bf16[8,4,16,128]{3,2,1,0:T(8,128)(2,1)S(1)}, u32[]{:S(2)}, u32[]{:S(2)}) collective-permute-start(bf16[8,4,16,128]{3,2,1,0:T(8,128)(2,1)S(1)} %get-tuple-element.108), channel_id=1, source_target_pairs={{0,128},{4,132},{8,136},{12,140},{16,144},{20,148},{24,152},{28,15... | collective-permute-start | bytes 393224 | tf_op jit(solution)/shard_map/ppermute | solution.py:44
  54.2 10.7 %collective-permute-start.7 = (bf16[8,4,16,128]{3,2,1,0:T(8,128)(2,1)S(1)}, bf16[8,4,16,128]{3,2,1,0:T(8,128)(2,1)S(1)}, u32[]{:S(2)}, u32[]{:S(2)}) collective-permute-start(bf16[8,4,16,128]{3,2,1,0:T(8,128)(2,1)S(1)} %get-tuple-element.110), channel_id=1, source_target_pairs={{0,192},{4,196},{8,200},{12,204},{16,208},{20,212},{24,216},{28,22... | collective-permute-start | bytes 393224 | tf_op jit(solution)/shard_map/ppermute | solution.py:44
  57.3 14.9 %collective-permute-start.10 = (bf16[8,4,16,128]{3,2,1,0:T(8,128)(2,1)S(1)}, bf16[8,4,16,128]{3,2,1,0:T(8,128)(2,1)S(1)}, u32[]{:S(2)}, u32[]{:S(2)}) collective-permute-start(bf16[8,4,16,128]{3,2,1,0:T(8,128)(2,1)S(1)} %get-tuple-element.132), channel_id=1, source_target_pairs={{0,192},{4,196},{8,200},{12,204},{16,208},{20,212},{24,216},{28,22... | collective-permute-start | bytes 393224 | tf_op jit(solution)/shard_map/ppermute | solution.py:44
  62.3 12.5 %collective-permute-start.8 = (bf16[8,4,16,128]{3,2,1,0:T(8,128)(2,1)S(1)}, bf16[8,4,16,128]{3,2,1,0:T(8,128)(2,1)S(1)}, u32[]{:S(2)}, u32[]{:S(2)}) collective-permute-start(bf16[8,4,16,128]{3,2,1,0:T(8,128)(2,1)S(1)} %get-tuple-element.129), channel_id=1, source_target_pairs={{0,64},{4,68},{8,72},{12,76},{16,80},{20,84},{24,88},{28,92},{32,9... | collective-permute-start | bytes 393224 | tf_op jit(solution)/shard_map/ppermute | solution.py:44
  62.4 12.3 %collective-permute-start.9 = (bf16[8,4,16,128]{3,2,1,0:T(8,128)(2,1)S(1)}, bf16[8,4,16,128]{3,2,1,0:T(8,128)(2,1)S(1)}, u32[]{:S(2)}, u32[]{:S(2)}) collective-permute-start(bf16[8,4,16,128]{3,2,1,0:T(8,128)(2,1)S(1)} %get-tuple-element.131), channel_id=1, source_target_pairs={{0,128},{4,132},{8,136},{12,140},{16,144},{20,148},{24,152},{28,15... | collective-permute-start | bytes 393224 | tf_op jit(solution)/shard_map/ppermute | solution.py:44
  66.8 8.4 %collective-permute-start.14 = (bf16[8,4,16,128]{3,2,1,0:T(8,128)(2,1)S(1)}, bf16[8,4,16,128]{3,2,1,0:T(8,128)(2,1)S(1)}, u32[]{:S(2)}, u32[]{:S(2)}) collective-permute-start(bf16[8,4,16,128]{3,2,1,0:T(8,128)(2,1)S(1)} %get-tuple-element.138), channel_id=1, source_target_pairs={{0,192},{4,196},{8,200},{12,204},{16,208},{20,212},{24,216},{28,22... | collective-permute-start | bytes 393224 | tf_op jit(solution)/shard_map/ppermute | solution.py:44
  68.6 7.0 %collective-permute-start.13 = (bf16[8,4,16,128]{3,2,1,0:T(8,128)(2,1)S(1)}, bf16[8,4,16,128]{3,2,1,0:T(8,128)(2,1)S(1)}, u32[]{:S(2)}, u32[]{:S(2)}) collective-permute-start(bf16[8,4,16,128]{3,2,1,0:T(8,128)(2,1)S(1)} %get-tuple-element.137), channel_id=1, source_target_pairs={{0,128},{4,132},{8,136},{12,140},{16,144},{20,148},{24,152},{28,15... | collective-permute-start | bytes 393224 | tf_op jit(solution)/shard_map/ppermute | solution.py:44
  72.1 6.3 %collective-permute-start.12 = (bf16[8,4,16,128]{3,2,1,0:T(8,128)(2,1)S(1)}, bf16[8,4,16,128]{3,2,1,0:T(8,128)(2,1)S(1)}, u32[]{:S(2)}, u32[]{:S(2)}) collective-permute-start(bf16[8,4,16,128]{3,2,1,0:T(8,128)(2,1)S(1)} %get-tuple-element.135), channel_id=1, source_target_pairs={{0,64},{4,68},{8,72},{12,76},{16,80},{20,84},{24,88},{28,92},{32,9... | collective-permute-start | bytes 393224 | tf_op jit(solution)/shard_map/ppermute | solution.py:44
  75.1 3.6 %collective-permute-start.11 = (bf16[4,8,16,128]{3,2,1,0:T(8,128)(2,1)S(1)}, bf16[4,8,16,128]{3,2,1,0:T(8,128)(2,1)S(1)}, u32[]{:S(2)}, u32[]{:S(2)}) collective-permute-start(bf16[4,8,16,128]{3,2,1,0:T(8,128)(2,1)S(1)} %get-tuple-element.134), channel_id=1, source_target_pairs={{0,4},{4,0},{8,12},{12,8},{16,20},{20,16},{24,28},{28,24},{32,36},... | collective-permute-start | bytes 393224 | tf_op jit(solution)/shard_map/ppermute | solution.py:49
  78.6 1.4 %collective-permute-start.15 = (bf16[4,8,16,128]{3,2,1,0:T(8,128)(2,1)S(1)}, bf16[4,8,16,128]{3,2,1,0:T(8,128)(2,1)S(1)}, u32[]{:S(2)}, u32[]{:S(2)}) collective-permute-start(bf16[4,8,16,128]{3,2,1,0:T(8,128)(2,1)S(1)} %get-tuple-element.141), channel_id=1, source_target_pairs={{0,4},{4,0},{8,12},{12,8},{16,20},{20,16},{24,28},{28,24},{32,36},... | collective-permute-start | bytes 393224 | tf_op jit(solution)/shard_map/ppermute | solution.py:49
  95.0 1.3 %collective-permute-start.16 = (bf16[9,16,128]{2,1,0:T(8,128)(2,1)S(1)}, bf16[9,16,128]{2,1,0:T(8,128)(2,1)S(1)}, u32[]{:S(2)}, u32[]{:S(2)}) collective-permute-start(bf16[9,16,128]{2,1,0:T(8,128)(2,1)S(1)} %get-tuple-element.143.mine), channel_id=1, source_target_pairs={{0,4},{4,0},{8,12},{12,8},{16,20},{20,16},{24,28},{28,24},{32,36},... | collective-permute-start | bytes 110600 | tf_op jit(solution)/shard_map/ppermute | solution.py:49
  112.5 5.3 %collective-permute-start.19 = (f32[1,128]{1,0:T(1,128)S(1)}, f32[1,128]{1,0:T(1,128)S(1)}, u32[]{:S(2)}, u32[]{:S(2)}) collective-permute-start(f32[1,128]{1,0:T(1,128)S(1)} %tally.1), channel_id=1, source_target_pairs={{0,3},{1,0},{2,1},{3,2},{4,7},{5,4},{6,5},{7,6},{8,11},{9,8},{10,9... | collective-permute-start | bytes 1544 | tf_op jit(solution)/shard_map/ppermute | solution.py:54
  115.3 5.0 %collective-permute-start.18 = (f32[1,128]{1,0:T(1,128)S(1)}, f32[1,128]{1,0:T(1,128)S(1)}, u32[]{:S(2)}, u32[]{:S(2)}) collective-permute-start(f32[1,128]{1,0:T(1,128)S(1)} %tally.1), channel_id=1, source_target_pairs={{0,2},{1,3},{2,0},{3,1},{4,6},{5,7},{6,4},{7,5},{8,10},{9,11},{10,... | collective-permute-start | bytes 1544 | tf_op jit(solution)/shard_map/ppermute | solution.py:54
  116.1 4.8 %collective-permute-start.17 = (f32[1,128]{1,0:T(1,128)S(1)}, f32[1,128]{1,0:T(1,128)S(1)}, u32[]{:S(2)}, u32[]{:S(2)}) collective-permute-start(f32[1,128]{1,0:T(1,128)S(1)} %tally.1), channel_id=1, source_target_pairs={{0,1},{1,2},{2,3},{3,0},{4,5},{5,6},{6,7},{7,4},{8,9},{9,10},{10,1... | collective-permute-start | bytes 1544 | tf_op jit(solution)/shard_map/ppermute | solution.py:54

commit v4 on v3

v4 whole, which is shorter than its diff:
```python
import functools
import math

import jax
import jax.numpy as jnp
from jax import lax
from jax.experimental import pallas as pl
from jax.experimental.pallas import tpu as pltpu
from jax.sharding import PartitionSpec as P

NY, NZ, NC = 4, 8, 2
NBLK = NY * NZ * NC
NHEAD = 4
GROUP = 4
DEPTH = 8
TOK = 128
HD = 128
KV = 2
RATIO = 8
LANES = 128
HALF = 8
ROWS = TOK * RATIO
QUAD = 4
PART = 32 * DEPTH
HAND = (DEPTH, QUAD, 16, LANES)
F32 = jnp.float32
BF16 = jnp.bfloat16
VMEM = pltpu.VMEM
NT = (((1,), (1,)), ((), ()))
NN = (((1,), (0,)), ((), ()))
TN = (((0,), (0,)), ((), ()))


def index_of(y, z, c):
    return ((y % NY) * NZ + z % NZ) * NC + c % NC


def every():
    return [(y, z, c) for y in range(NY) for z in range(NZ) for c in range(NC)]


def along_y(x, step):
    pairs = [(index_of(y, z, c), index_of(y + step, z, c)) for y, z, c in every()]
    return lax.ppermute(x, "branch", pairs)


def other_core(x):
    pairs = [(index_of(y, z, c), index_of(y, z, c + 1)) for y, z, c in every()]
    return lax.ppermute(x, "branch", pairs)


def along_head(x, step):
    pairs = [(i, (i + step) % NHEAD) for i in range(NHEAD)]
    return lax.ppermute(x, "head", pairs)


def swap_z(x):
    groups = [[index_of(y, z, c) for z in range(NZ)] for y in range(NY) for c in range(NC)]
    return lax.all_to_all(x, "branch", 0, 0, axis_index_groups=groups, tiled=False)


def swap_yz(x):
    groups = [[index_of(y, z, c) for y in range(NY) for z in range(NZ)] for c in range(NC)]
    return lax.all_to_all(x, "branch", 0, 0, axis_index_groups=groups, tiled=False)


def call(body, outs, scratch=(), vmem_mb=32):
    return dict(
        out_shape=outs,
        scratch_shapes=list(scratch),
        compiler_params=pltpu.CompilerParams(vmem_limit_bytes=vmem_mb << 20),
    )


def in_vmem():
    return pl.BlockSpec(memory_space=VMEM)


def place():
    b = lax.axis_index("branch")
    return b // (NZ * NC), (b // NC) % NZ, b % NC


LINE = 0
DEAL = 16
BACK = 32
HOLD = 48
INNER = 56
SELF = 72
WORDS = 88


def row_of(y, z):
    return 32 * y + 8 * (z // 2)


def packet_kernel(
    keys_far, values_far, ancestors_far, group, reward, packet, own_kv,
    keys, values, ancestors, sems,
):
    pairs = (
        (ancestors_far, ancestors),
        (keys_far, keys),
        (values_far, values),
    )
    copies = [pltpu.make_async_copy(a, b, sems.at[i]) for i, (a, b) in enumerate(pairs)]
    for copy in copies:
        copy.start()
    for copy in copies[:1]:
        copy.wait()
    row = lax.broadcasted_iota(jnp.int32, (8, LANES), 0)
    lane = lax.broadcasted_iota(jnp.int32, (8, LANES), 1)
    spot = lax.broadcasted_iota(jnp.int32, (8, DEPTH), 0) == lax.broadcasted_iota(
        jnp.int32, (8, DEPTH), 1
    )
    line = jnp.broadcast_to(ancestors[...].astype(F32), (8, DEPTH))
    line = jnp.sum(jnp.where(spot, line, 0.0), axis=1, keepdims=True)
    facts = jnp.where(
        row == 0, group[0].astype(F32), jnp.where(row == 1, reward[0].astype(F32), 0.0)
    )
    meta = jnp.where(lane < NBLK, line, facts)
    for copy in copies[1:]:
        copy.wait()
    for h in range(KV):
        own_kv[2 * h] = keys[:, h, :]
        own_kv[2 * h + 1] = values[:, h, :]
    whole = [own_kv[i].astype(F32) for i in range(2 * KV)]
    for z in range(NZ):
        for y in range(NY):
            at = row_of(y, z)
            rows = [whole[2 * h + z % 2][at : at + 8] for h in range(KV)]
            packet[y * NZ + z] = jnp.concatenate(rows + [meta], 0).astype(BF16)


def packet_of(keys, values, ancestors, group, reward):
    return pl.pallas_call(
        packet_kernel,
        in_specs=[pl.BlockSpec(memory_space=pltpu.HBM)] * 3
        + [pl.BlockSpec(memory_space=pltpu.SMEM)] * 2,
        out_specs=(in_vmem(),) * 2,
        **call(
            packet_kernel,
            (
                jax.ShapeDtypeStruct((NY * NZ, 24, LANES), BF16),
                jax.ShapeDtypeStruct((2 * KV, TOK, HD), BF16),
            ),
            [VMEM(x.shape, x.dtype) for x in (keys, values, ancestors)]
            + [pltpu.SemaphoreType.DMA((3,))],
            vmem_mb=62,
        ),
        name="packet",
    )(keys, values, ancestors, group, reward)


def pack_rows(x, base, first, count):
    row = lax.broadcasted_iota(jnp.int32, (8, LANES), 0)
    weight = jnp.zeros((8, LANES), F32)
    for i in range(count):
        weight = jnp.where(row == first + i, float(base**i), weight)
    return jnp.sum(x * weight, axis=0, keepdims=True)


def plan_kernel(mine, other, picked, table, scale):
    y, z, c = place()
    meta_m = mine[...].astype(F32)[:, 16:24, :]
    meta_o = other[...].astype(F32)[:, 16:24, :]
    row = lax.broadcasted_iota(jnp.int32, (8, LANES), 0)
    row_f = row.astype(F32)
    lane = lax.broadcasted_iota(jnp.int32, (8, LANES), 1)
    lane_f = lane.astype(F32)
    is_block = lane < NBLK
    wide_lane = lax.broadcasted_iota(jnp.int32, (NY * NZ, LANES), 1).astype(F32)
    hit = jnp.maximum(
        jnp.where(meta_m[:, 0, :] == wide_lane, 1.0, 0.0),
        jnp.where(meta_o[:, 0, :] == wide_lane, 1.0, 0.0),
    )
    inner = jnp.max(hit, axis=0, keepdims=True)
    inner = jnp.where(is_block, jnp.broadcast_to(inner, (8, LANES)), 0.0)
    before = (
        lax.broadcasted_iota(jnp.int32, (LANES, LANES), 0)
        < lax.broadcasted_iota(jnp.int32, (LANES, LANES), 1)
    ).astype(F32).astype(BF16)
    rank = lax.dot_general(inner.astype(BF16), before, NN, preferred_element_type=F32)
    slots = jnp.where(inner > 0.0, rank + 1.0, 0.0)

    words = []
    for first in (0, 8):
        wanted = row_f + float(first + 1)
        index = jnp.sum(jnp.where(slots == wanted, lane_f, 0.0), axis=1, keepdims=True)
        index = jnp.broadcast_to(index, (8, LANES))
        words += [pack_rows(index, 64, at, 4).astype(jnp.int32)[0, 0] for at in (0, 4)]
    pieces = []
    for s in range(2 * HALF):
        block = (words[s // 4] >> (6 * (s % 4))) & 63
        at = block >> 1
        piece = jnp.where((block & 1) == c, mine[at].astype(F32), other[at].astype(F32))
        pieces.append(jnp.where(c == 0, piece[0:8], piece[8:16]))
    for j in range(HALF):
        pair = jnp.concatenate(pieces[2 * j : 2 * j + 2], 0).astype(BF16)
        picked[:, j] = jnp.broadcast_to(pair[None], (NZ, 16, LANES))

    for k in range(NY):
        yy = lax.rem(y + k, NY)
        for u, side in enumerate((mine, other)):
            line = side[yy * NZ + z].astype(F32)[16:24, :]
            same = (line == lane_f) & is_block
            slot = jnp.sum(jnp.where(same, slots, 0.0), axis=1, keepdims=True)
            slot = jnp.broadcast_to(slot, (8, LANES))
            block = (yy * NZ + z) * NC + (c if u == 0 else 1 - c)
            own = jnp.sum(jnp.where(lane == block, slots, 0.0), axis=1, keepdims=True)
            own = jnp.broadcast_to(own, (8, LANES))
            depth = jnp.sum(jnp.where(slot > 0.0, 1.0, 0.0), axis=0, keepdims=True)
            entry = jnp.where(row_f == depth, own, slot)
            dealt = jnp.maximum(slot - 1.0, 0.0)
            for half in range(2):
                at = 8 * u + 2 * k + half
                word = pack_rows(dealt, 16, 4 * half, 4)
                table[DEAL + at : DEAL + at + 1, :] = word.astype(jnp.int32)
                word = pack_rows(entry, 32, 4 * half, 4)
                table[BACK + at : BACK + at + 1, :] = word.astype(jnp.int32)
            if k == 0:
                at = 8 * u
                table[LINE + at : LINE + at + 8, :] = slot.astype(jnp.int32)
                table[INNER + at : INNER + at + 8, :] = own.astype(jnp.int32)
                mark = jnp.where(row_f == depth, own, 0.0)
                table[SELF + at : SELF + at + 8, :] = mark.astype(jnp.int32)
    for i in range(6):
        word = jnp.zeros((8, 1), F32)
        for j in range(3):
            held = jnp.where(slots == float(3 * i + j + 1), lane_f + 1.0, 0.0)
            word = word + jnp.sum(held, axis=1, keepdims=True) * float(128**j)
        table[HOLD + i : HOLD + i + 1, :] = jnp.broadcast_to(word, (8, LANES)).astype(jnp.int32)[0:1]

    for u, side in enumerate((mine, other)):
        here = side[y * NZ + z].astype(F32)[16:24, :]
        group, reward = here[0:1, :], here[1:2, :]
        in_m = jnp.where(meta_m[:, 0, :] == group, meta_m[:, 1, :], 0.0)
        in_o = jnp.where(meta_o[:, 0, :] == group, meta_o[:, 1, :], 0.0)
        total = jnp.sum(in_m + in_o, axis=0, keepdims=True)
        squares = jnp.sum(in_m * in_m + in_o * in_o, axis=0, keepdims=True)
        mean = total / GROUP
        spread = jnp.sqrt(jnp.maximum(squares / GROUP - mean * mean, 0.25))
        advantage = (reward - mean) / spread
        advantage = jnp.sum(jnp.where(lane[0:1] == NBLK, advantage, 0.0), axis=1, keepdims=True)
        scale[8 * u : 8 * u + 8] = jnp.broadcast_to(advantage, (8, LANES))


def plan(mine, other):
    return pl.pallas_call(
        plan_kernel,
        in_specs=[in_vmem()] * 2,
        out_specs=(in_vmem(),) * 3,
        **call(
            plan_kernel,
            (
                jax.ShapeDtypeStruct((NZ, HALF, 16, LANES), BF16),
                jax.ShapeDtypeStruct((WORDS, LANES), jnp.int32),
                jax.ShapeDtypeStruct((16, LANES), F32),
            ),
        ),
        name="plan",
    )(mine, other)


def deal_kernel(u, table, column, after, *outs):
    words = table[DEAL + 8 * u : DEAL + 8 * u + 8, :]
    for k in range(NY):
        for d in range(DEPTH):
            slot = (words[2 * k + d // 4, 0] >> (4 * (d % 4))) & 15
            pair = column[:, slot >> 1].astype(F32)
            rows = jnp.where((slot & 1) == 1, pair[:, 8:16], pair[:, 0:8])
            for kind in range(2):
                whole = jnp.concatenate([rows[2 * i + kind] for i in range(4)], 0)
                outs[k][d, 2 * kind : 2 * kind + 2] = whole.astype(BF16).reshape(2, 16, LANES)


def deal(u, table, column, after):
    return pl.pallas_call(
        functools.partial(deal_kernel, u),
        in_specs=[in_vmem()] * 2 + [pl.BlockSpec(memory_space=pl.ANY)],
        out_specs=(in_vmem(),) * NY,
        **call(deal_kernel, (jax.ShapeDtypeStruct(HAND, BF16),) * NY),
        name="deal",
    )(table, column, after)


def halve_kernel(queries, cotangent, own_kv, after, keep, send):
    first_core = place()[2] == 0
    for at, far in ((0, queries), (ROWS, cotangent)):
        whole = far[...].astype(F32)
        low = whole[:, 0:RATIO].reshape(ROWS, HD).astype(BF16)
        high = whole[:, RATIO:].reshape(ROWS, HD).astype(BF16)
        keep[at : at + ROWS] = jnp.where(first_core, low, high)
        send[at : at + ROWS] = jnp.where(first_core, high, low)
    for kind in range(2):
        at = 2 * ROWS + TOK * kind
        low, high = own_kv[kind], own_kv[2 + kind]
        keep[at : at + TOK] = jnp.where(first_core, low, high)
        send[at : at + TOK] = jnp.where(first_core, high, low)


def halve(queries, cotangent, own_kv, after):
    return pl.pallas_call(
        halve_kernel,
        in_specs=[in_vmem()] * 3 + [pl.BlockSpec(memory_space=pl.ANY)],
        out_specs=(in_vmem(),) * 2,
        **call(halve_kernel, (jax.ShapeDtypeStruct((2 * ROWS + 2 * TOK, HD), BF16),) * 2),
        name="halve",
    )(queries, cotangent, own_kv, after)


def prepare_kernel(scale, keep, got, q_all, g_all, kv_all):
    for u, side in enumerate((keep, got)):
        q_all[u] = side[0:ROWS]
        weight = scale[8 * u : 8 * u + 1, :]
        g_all[u] = (side[ROWS : 2 * ROWS].astype(F32) * weight).astype(BF16)
        for kind in range(2):
            at = 2 * ROWS + TOK * kind
            kv_all[2 * u + kind] = side[at : at + TOK]


def prepare(scale, keep, got):
    return pl.pallas_call(
        prepare_kernel,
        in_specs=[in_vmem()] * 3,
        out_specs=(in_vmem(),) * 3,
        **call(
            prepare_kernel,
            (jax.ShapeDtypeStruct((2, ROWS, HD), BF16),) * 2
            + (jax.ShapeDtypeStruct((4, TOK, HD), BF16),),
        ),
        name="prepare",
    )(scale, keep, got)


def rows_of(part, kind):
    return part[:, 2 * kind : 2 * kind + 2].reshape(PART, HD)


def one_part(keys, values, q, g, mask, exps, pgs, stats, at):
    s = lax.dot_general(keys, q, NT, preferred_element_type=F32) * (
        math.log2(math.e) / math.sqrt(HD)
    )
    s = mask(s)
    top = jnp.max(s, axis=0, keepdims=True)
    e = jnp.exp2(s - top)
    pg = lax.dot_general(values, g, NT, preferred_element_type=F32)
    exps[...] = e
    pgs[...] = pg
    stats[at : at + 1, :] = top
    stats[at + 1 : at + 2, :] = jnp.sum(e, axis=0, keepdims=True)
    stats[at + 2 : at + 3, :] = jnp.sum(e * pg, axis=0, keepdims=True)


def causal(s):
    key_pos = lax.broadcasted_iota(jnp.int32, s.shape, 0)
    query_pos = lax.broadcasted_iota(jnp.int32, s.shape, 1) // RATIO
    return jnp.where(key_pos <= query_pos, s, -1e30)


def listed(h, table):
    def mask(s):
        parts = []
        for d in range(DEPTH):
            seen = jnp.concatenate([table[LINE + 8 * h + d : LINE + 8 * h + d + 1, :]] * (ROWS // LANES), 1) > 0
            parts.append(jnp.where(seen, s[32 * d : 32 * d + 32], -1e30))
        return jnp.concatenate(parts, 0)

    return mask


def scores_kernel(h, table, q_all, g_all, part, after, exps, pgs, stats):
    keys, values = rows_of(part, 0), rows_of(part, 1)
    one_part(keys, values, q_all[h], g_all[h], listed(h, table), exps, pgs, stats, 0)


def first_scores_kernel(h, table, q_all, g_all, part, own_kv, exps, pgs, stats, own_exps, own_pgs):
    keys, values = rows_of(part, 0), rows_of(part, 1)
    q, g = q_all[h], g_all[h]
    one_part(keys, values, q, g, listed(h, table), exps, pgs, stats, 0)
    one_part(own_kv[2 * h], own_kv[2 * h + 1], q, g, causal, own_exps, own_pgs, stats, 4)


def wide(keys):
    return jax.ShapeDtypeStruct((keys, ROWS), F32)


STATS = jax.ShapeDtypeStruct((8, TOK * RATIO), F32)


def scores_of(h, table, q_all, g_all, part, after):
    return pl.pallas_call(
        functools.partial(scores_kernel, h),
        in_specs=[in_vmem()] * 4 + [pl.BlockSpec(memory_space=pl.ANY)],
        out_specs=(in_vmem(),) * 3,
        **call(scores_kernel, (wide(PART), wide(PART), STATS), vmem_mb=16),
        cost_estimate=cost(PART, 2),
        name="scores",
    )(table, q_all, g_all, part, after)


def first_scores_of(h, table, q_all, g_all, part, own_kv):
    return pl.pallas_call(
        functools.partial(first_scores_kernel, h),
        in_specs=[in_vmem()] * 5,
        out_specs=(in_vmem(),) * 5,
        **call(
            first_scores_kernel,
            (wide(PART), wide(PART), STATS, wide(TOK), wide(TOK)),
            vmem_mb=16,
        ),
        cost_estimate=cost(PART + TOK, 2),
        name="scores_first",
    )(table, q_all, g_all, part, own_kv)


def cost(keys, products):
    return pl.CostEstimate(
        flops=2 * products * ROWS * keys * HD,
        bytes_accessed=8 * ROWS * keys,
        transcendentals=ROWS * keys,
    )


SMALL = pl.CostEstimate(flops=1000, bytes_accessed=1000, transcendentals=0)


def merge(stats):
    rows = [(ref, 0) for ref in stats] + [(stats[0], 4)]
    tops = [ref[at : at + 1, :] for ref, at in rows]
    top = tops[0]
    for t in tops[1:]:
        top = jnp.maximum(top, t)
    shares = [jnp.exp2(t - top) for t in tops]
    norm = sum(s * ref[at + 1 : at + 2, :] for s, (ref, at) in zip(shares, rows))
    norm = 1.0 / norm
    shares = [s * norm for s in shares]
    delta = sum(s * ref[at + 2 : at + 3, :] for s, (ref, at) in zip(shares, rows))
    return shares, delta


def one_grad(e, pg, share, delta, q, g, keys):
    p = e * share
    low = p.astype(BF16)
    ds = (p * (pg - delta)).astype(BF16)
    factor = 1.0 / math.sqrt(HD)
    dv = lax.dot_general(low, g, NN, preferred_element_type=F32)
    dk = lax.dot_general(ds, q, NN, preferred_element_type=F32) * factor
    turned = keys.astype(F32).T.astype(BF16)
    dq = lax.dot_general(turned, ds, NN, preferred_element_type=F32)
    return dq, dk, dv


def part_grad(k, h, table, stats, exps, pgs, q_all, g_all, part, own_grad, contrib):
    shares, delta = merge(stats)
    dq, dk, dv = one_grad(
        exps[...], pgs[...], shares[k], delta, q_all[h], g_all[h], rows_of(part, 0)
    )
    piece = lax.rem(place()[0] + NY - k, NY)
    for kind, grad in enumerate((dk, dv)):
        own = own_grad[kind, pl.ds(pl.multiple_of(piece * 32, 32), 32), :]
        for d in range(DEPTH):
            mark = table[SELF + 8 * h + d : SELF + 8 * h + d + 1, :] > 0
            both = jnp.where(mark, own, grad[32 * d : 32 * d + 32])
            contrib[d, 2 * kind : 2 * kind + 2] = both.astype(BF16).reshape(2, 16, HD)
    return dq


def first_grads_kernel(
    k, h, table, s0, s1, s2, s3, exps, pgs, q_all, g_all, part, own_exps, own_pgs, own_kv,
    dq_sum, own_grad, contrib,
):
    stats = (s0, s1, s2, s3)
    shares, delta = merge(stats)
    dq, dk, dv = one_grad(
        own_exps[...], own_pgs[...], shares[NY], delta, q_all[h], g_all[h], own_kv[2 * h]
    )
    own_grad[0] = dk
    own_grad[1] = dv
    dq_sum[...] = dq + part_grad(
        k, h, table, stats, exps, pgs, q_all, g_all, part, own_grad, contrib
    )


def grads_kernel(
    k, h, table, s0, s1, s2, s3, exps, pgs, q_all, g_all, part, own_grad, dq_in, *outs
):
    dq_sum, contrib = outs[-2:]
    dq_sum[...] = dq_in[...] + part_grad(
        k, h, table, (s0, s1, s2, s3), exps, pgs, q_all, g_all, part, own_grad, contrib
    )


def emit_kernel(table, dq_0, dq_1, own_0, own_1, keep, send, squares):
    total = jnp.zeros((8, HD), F32)
    for u, (dq, own, out) in enumerate(((dq_0, own_0, keep), (dq_1, own_1, send))):
        dq = dq[...].T * (1.0 / math.sqrt(HD))
        total = total + jnp.sum((dq * dq).reshape(ROWS // 8, 8, HD), axis=0)
        out[0:ROWS] = dq
        own = own[...]
        own_squares = jnp.sum((own * own).reshape(2 * TOK // 8, 8, HD), axis=0)
        inner = table[INNER + 8 * u : INNER + 8 * u + 8, :] > 0
        total = total + jnp.where(inner, 0.0, own_squares)
    send[ROWS : ROWS + TOK] = own_1[0]
    send[ROWS + TOK :] = own_1[1]
    squares[...] = total


def emit(table, dqs, owns):
    return pl.pallas_call(
        emit_kernel,
        in_specs=[in_vmem()] * 5,
        out_specs=(in_vmem(),) * 3,
        **call(
            emit_kernel,
            (
                jax.ShapeDtypeStruct((ROWS, HD), F32),
                jax.ShapeDtypeStruct((ROWS + 2 * TOK, HD), F32),
                jax.ShapeDtypeStruct((8, LANES), F32),
            ),
            vmem_mb=16,
        ),
        cost_estimate=SMALL,
        name="emit",
    )(table, *dqs, *owns)


def assemble_kernel(keep, got, query_grad, token):
    first_core = place()[2] == 0
    near, far = keep[...], got[0:ROWS]
    low, high = jnp.where(first_core, near, far), jnp.where(first_core, far, near)
    query_grad[:, 0:RATIO, :] = low.reshape(TOK, RATIO, HD)
    query_grad[:, RATIO:, :] = high.reshape(TOK, RATIO, HD)
    token[...] = jnp.zeros_like(token)


def assemble(keep, got):
    return pl.pallas_call(
        assemble_kernel,
        in_specs=[in_vmem()] * 2,
        out_specs=(in_vmem(),) * 2,
        **call(
            assemble_kernel,
            (
                jax.ShapeDtypeStruct((TOK, KV * RATIO, HD), F32),
                jax.ShapeDtypeStruct((8, LANES), F32),
            ),
            vmem_mb=16,
        ),
        cost_estimate=SMALL,
        name="assemble",
    )(keep, got)


def grads_of(body, name, outs, k, h, *arrays):
    return pl.pallas_call(
        functools.partial(body, k, h),
        in_specs=[in_vmem()] * len(arrays),
        out_specs=(in_vmem(),) * len(outs),
        **call(body, outs, vmem_mb=16),
        cost_estimate=SMALL,
        name=name,
    )(*arrays)


def attend(h, table, q_all, g_all, own_kv, parts, after, hints):
    e, pg, st = [None] * NY, [None] * NY, [None] * NY
    e[0], pg[0], st[0], own_e, own_pg = first_scores_of(h, table, q_all, g_all, parts[0], own_kv)
    after = st[0] if after is None else after
    for k in (1, 2, 3):
        e[k], pg[k], st[k] = scores_of(h, table, q_all, g_all, parts[k], after)
        after = st[k]
    back = [None] * NY
    dq_type = jax.ShapeDtypeStruct((HD, ROWS), F32)
    own_type = jax.ShapeDtypeStruct((2, TOK, HD), F32)
    contrib_type = jax.ShapeDtypeStruct(HAND, BF16)

    def shared(k):
        return (table, *st, e[k], pg[k], q_all, g_all, parts[k])

    dq, own_grad, back[2] = grads_of(
        first_grads_kernel, "grads_first", (dq_type, own_type, contrib_type), 2, h,
        *shared(2), own_e, own_pg, own_kv,
    )
    for k, hint in ((1, hints[:1]), (3, hints[1:])):
        dq, back[k] = grads_of(
            grads_kernel, "grads", (dq_type, contrib_type), k, h, *shared(k), own_grad, dq, *hint
        )

    def last(after):
        return grads_of(
            grads_kernel, "grads_last", (dq_type, contrib_type), 0, h, *shared(0), own_grad, dq, after
        )

    return dq, own_grad, back, last


def add_part(k, u, table, part, acc):
    at = BACK + 8 * u + 2 * k
    words = table[at : at + 2, :]
    for d in range(DEPTH):
        slot = (words[d // 4, 0] >> (5 * (d % 4))) & 31
        acc[jnp.maximum(slot - 1, 0)] += jnp.where(slot > 0, part[d].astype(F32), 0.0)


def combine_first_kernel(table, part_1, part_2, acc, token):
    acc[...] = jnp.zeros_like(acc)
    add_part(1, 0, table, part_1, acc)
    add_part(2, 0, table, part_2, acc)
    token[...] = jnp.zeros_like(token)


def combine_kernel(ks, u, table, *refs):
    acc = refs[len(ks) + 2]
    for token in refs[len(ks) + 3 :]:
        token[...] = jnp.zeros_like(token)
    for k, part in zip(ks, refs):
        add_part(k, u, table, part, acc)


def leave_kernel(acc, halves):
    for z in range(NZ):
        at = 2 * (z % 2) + z // 4
        rows = slice(8 * (z // 2 % 2), 8 * (z // 2 % 2) + 8)
        for j in range(HALF):
            pair = [acc[2 * j + i, at, rows, :] for i in range(2)]
            halves[z, j] = jnp.concatenate(pair, 0).astype(BF16)


ACC = (2 * HALF, QUAD, 16, LANES)


def acc_and_token():
    return jax.ShapeDtypeStruct(ACC, F32), jax.ShapeDtypeStruct((8, LANES), F32)


def combine_start(table, part_1, part_2):
    return pl.pallas_call(
        combine_first_kernel,
        in_specs=[in_vmem()] * 3,
        out_specs=(in_vmem(),) * 2,
        **call(combine_first_kernel, acc_and_token(), vmem_mb=16),
        cost_estimate=SMALL,
        name="combine_first",
    )(table, part_1, part_2)


def combine_more(ks, u, table, parts, acc, after, outs=1):
    return pl.pallas_call(
        functools.partial(combine_kernel, ks, u),
        in_specs=[in_vmem()] * (2 + len(parts)) + [pl.BlockSpec(memory_space=pl.ANY)],
        out_specs=(in_vmem(),) * outs,
        input_output_aliases={1 + len(parts): 0},
        **call(combine_kernel, acc_and_token()[:outs], vmem_mb=16),
        cost_estimate=SMALL,
        name="combine",
    )(table, *parts, acc, after)


def leave(acc):
    return pl.pallas_call(
        leave_kernel,
        in_specs=[in_vmem()],
        out_specs=in_vmem(),
        **call(leave_kernel, jax.ShapeDtypeStruct((NZ, HALF, 16, LANES), BF16), vmem_mb=16),
        cost_estimate=SMALL,
        name="leave",
    )(acc)


def split_rows(value, rows):
    high = value.astype(BF16).astype(F32)
    middle = (value - high).astype(BF16).astype(F32)
    low = value - high - middle
    row = lax.broadcasted_iota(jnp.int32, (8, LANES), 0)
    tile = jnp.where(row == 0, high, jnp.where(row == 1, middle, jnp.where(row == 2, low, 0.0)))
    if rows > 8:
        tile = jnp.concatenate([tile, jnp.zeros((rows - 8, LANES), F32)], 0)
    return tile


def total_kernel(parts, squares, totals, sums):
    sums_now = parts[0].astype(F32)
    for z in range(1, NZ):
        sums_now = sums_now + parts[z].astype(F32)
    totals[...] = sums_now
    tile = squares[...] + jnp.sum((sums_now * sums_now).reshape(HALF * 2, 8, LANES), axis=0)
    sums[...] = jnp.broadcast_to(jnp.sum(tile, axis=0, keepdims=True), (8, LANES))


def route_kernel(table, parts, squares, out, room, totals, sums):
    total_kernel(parts, squares, totals, sums)
    c = place()[2]
    words = table[HOLD : HOLD + 8, :]
    blank = jnp.concatenate([jnp.zeros((16, LANES), F32), split_rows(sums[...], 8)], 0)
    room[0 : NY * NZ] = jnp.broadcast_to(blank[None], (NY * NZ, 24, LANES))
    for s in range(2 * HALF):
        block = ((words[s // 3, 0] >> (7 * (s % 3))) & 127) - 1
        side = jnp.where((block & 1) == c, 0, 8)
        to = jnp.where(block >= 0, block >> 1, NY * NZ)
        piece = totals[s // 2, 8 * (s % 2) : 8 * (s % 2) + 8, :]
        room[to, pl.ds(pl.multiple_of(side, 8), 8), :] = piece
    out[...] = room[0 : NY * NZ].astype(BF16)


def route(table, parts, squares):
    return pl.pallas_call(
        route_kernel,
        in_specs=[in_vmem()] * 3,
        out_specs=in_vmem(),
        **call(
            route_kernel,
            jax.ShapeDtypeStruct((NY * NZ, 24, LANES), BF16),
            [
                VMEM((NY * NZ + 1, 24, LANES), F32),
                VMEM((HALF, 16, LANES), F32),
                VMEM((8, LANES), F32),
            ],
        ),
        name="route",
    )(table, parts, squares)


def share_kernel(arrived, after, send, sums):
    whole = arrived[...].astype(F32)
    for i in range(NY * NZ // 2):
        pair = [whole[2 * i + j, 8:16, :] for j in range(2)]
        send[i] = jnp.concatenate(pair, 0).astype(BF16)
    tails = jnp.sum(jnp.sum(whole[:, 16:24, :], axis=0), axis=0, keepdims=True)
    value = jnp.broadcast_to(tails, (8, LANES))
    sums[...] = value
    send[NY * NZ // 2] = split_rows(value, 16).astype(BF16)


def share(arrived, after):
    return pl.pallas_call(
        share_kernel,
        in_specs=[in_vmem(), pl.BlockSpec(memory_space=pl.ANY)],
        out_specs=(in_vmem(),) * 2,
        **call(
            share_kernel,
            (
                jax.ShapeDtypeStruct((NY * NZ // 2 + 1, 16, LANES), BF16),
                jax.ShapeDtypeStruct((8, LANES), F32),
            ),
        ),
        name="share",
    )(arrived, after)


def tally_kernel(mine, got, sums):
    tails = mine[0:1, :] + jnp.sum(got[NY * NZ // 2].astype(F32), axis=0, keepdims=True)
    sums[...] = jnp.broadcast_to(jnp.sum(tails, axis=1, keepdims=True), (1, LANES))


def tally(mine, got):
    return pl.pallas_call(
        tally_kernel,
        in_specs=[in_vmem()] * 2,
        out_specs=in_vmem(),
        **call(tally_kernel, jax.ShapeDtypeStruct((1, LANES), F32)),
        name="tally",
    )(mine, got)


def finish_kernel(table, arrived, got, own, own_far, key_grad, value_grad):
    first_core = place()[2] == 0
    inner = table[INNER : INNER + 1, :] > 0
    for z in range(NZ):
        kind = z % 2
        out = value_grad if kind else key_grad
        for y in range(NY):
            at, src = row_of(y, z), y * NZ + z
            near = arrived[src].astype(F32)[0:8]
            far = got[src // 2].astype(F32)[8 * (src % 2) : 8 * (src % 2) + 8]
            near = jnp.where(inner, near, own[kind, at : at + 8, :])
            low = ROWS + TOK * kind + at
            far = jnp.where(inner, far, own_far[low : low + 8, :])
            out[at : at + 8, 0, :] = jnp.where(first_core, near, far)
            out[at : at + 8, 1, :] = jnp.where(first_core, far, near)


def finish(*arrays):
    return pl.pallas_call(
        finish_kernel,
        in_specs=[in_vmem()] * 5,
        out_specs=(in_vmem(),) * 2,
        **call(finish_kernel, (jax.ShapeDtypeStruct((TOK, KV, HD), F32),) * 2),
        cost_estimate=SMALL,
        name="finish",
    )(*arrays)


def local(queries, keys, values, cotangent, rewards, groups, ancestors, step_ids):
    packet, own_kv = packet_of(keys, values, ancestors, groups, rewards)
    mine = swap_yz(packet)
    other = other_core(mine)
    trained = (step_ids[0] % 2 == 0)[:, None, None]
    masked = jnp.where(trained, cotangent, jnp.zeros_like(cotangent))
    picked, table, scale = plan(mine, other)
    column = swap_z(picked)
    first = deal(0, table, column, table)
    keep, send = halve(queries, masked, own_kv, table)
    q_all, g_all, kv_all = prepare(scale, keep, other_core(send))
    parts = []
    for u in range(2):
        dealt = first if u == 0 else deal(u, table, column, first[0])
        parts.append([dealt[0]] + [along_y(dealt[k], k) for k in (1, 2, 3)])
    after, own_0, sent, last_0 = attend(0, table, q_all, g_all, kv_all, parts[0], None, ())
    back_0 = [None] + [along_y(sent[k], -k) for k in (1, 2, 3)]
    acc, token = combine_start(table, back_0[1], back_0[2])
    acc, late_token = combine_more((3,), 0, table, [back_0[3]], acc, table, 2)
    after, own_1, sent, last_1 = attend(
        1, table, q_all, g_all, kv_all, parts[1], after, (token, late_token)
    )
    back_1 = [None] + [along_y(sent[k], -k) for k in (1, 2, 3)]
    dq_0, back_0[0] = last_0(after)
    dq_1, back_1[0] = last_1(dq_0)
    near, far, squares = emit(table, (dq_0, dq_1), (own_0, own_1))
    far = other_core(far)
    query_grad, done = assemble(near, far)
    (acc,) = combine_more((0,), 0, table, [back_0[0]], acc, squares)
    (acc,) = combine_more((1, 0), 1, table, [back_1[1], back_1[0]], acc, squares)
    (acc,) = combine_more((2,), 1, table, [back_1[2]], acc, squares)
    (acc,) = combine_more((3,), 1, table, [back_1[3]], acc, squares)
    halves = leave(acc)
    arrived = swap_yz(route(table, swap_z(halves), squares))
    shared, mine_sum = share(arrived, done)
    shared = other_core(shared)
    mine_sum = tally(mine_sum, shared)
    all_sum = mine_sum
    for k in (1, 2, 3):
        all_sum = all_sum + along_head(mine_sum, k)
    key_grad, value_grad = finish(table, arrived, shared, own_0, far)
    count = float(NBLK * TOK * NHEAD * (KV * RATIO + 2 * KV) * HD)
    grad_rms = jnp.sqrt(all_sum[0, 0] / count)
    return query_grad, key_grad, value_grad, grad_rms


def solution(mesh):
    in_specs = (
        P("branch", "head", None),
        P("branch", "head", None),
        P("branch", "head", None),
        P("branch", "head", None),
        P("branch"),
        P("branch"),
        P("branch", None),
        P("branch", None),
    )
    out_specs = (
        P("branch", "head", None),
        P("branch", "head", None),
        P("branch", "head", None),
        P(),
    )
    return jax.shard_map(local, mesh=mesh, in_specs=in_specs, out_specs=out_specs, check_vma=False)
```

time: 122 us -> 120 us (0.984)
  blocking collectives: 67.1 us -> 14.3 us
  waiting for transfers between devices: 13.3 us -> 41.9 us
  starting transfers between devices: 21.4 us -> 42.3 us
  Pallas kernels: 15.8 us -> 17.1 us
    all_to_all x2 -> x0, blocking collectives: 38.2 us -> none  [swap_yz(): lax.all_to_all(x, 'branch', 0, 0, axis_index_groups=groups, tiled=False)]
    all_to_all x0 -> x3, waiting for transfers between devices: none -> 29.2 us  [the longest x2 20.5 us: swap_yz(): lax.all_to_all(x, 'branch', 0, 0, axis_index_groups=groups, tiled=False)]
    all_to_all x0 -> x3, starting transfers between devices: none -> 22 us  [the longest x2 16.7 us: swap_yz(): lax.all_to_all(x, 'branch', 0, 0, axis_index_groups=groups, tiled=False)]
    all_to_all x2 -> x1, blocking collectives: 28.9 us -> 14.3 us  [swap_z(): lax.all_to_all(x, 'branch', 0, 0, axis_index_groups=groups, tiled=False)]
    pallas_call x13 -> x15, Pallas kernels: 2.53 us -> 4.84 us  [the longest x1 1.1 us: assemble(): pl.pallas_call(assemble_kernel, in_specs=[in_vmem()] * 2, out_specs=(in_v...]
    ppermute x5 -> x4, waiting for transfers between devices: 4.27 us -> 2.47 us  [other_core(): return lax.ppermute(x, 'branch', pairs)]
    ppermute x12, waiting for transfers between devices: 5.99 us -> 7.25 us  [along_y(): return lax.ppermute(x, 'branch', pairs)]
  transfers between devices with their start and end apart: 20 -> 22, of which waited for: 10 -> 10; matrix products, arithmetic and copies ran while one was open for 0% -> 0% of each run, Pallas kernels for 10% -> 11%
where the time goes in v4:
time: 120 us; the launch traced here: 119 us
  starting transfers between devices  42.3 us (35%)
  waiting for transfers between devices  41.9 us (35%)
  Pallas kernels  17.1 us (14%)
  blocking collectives  14.3 us (12%)
  between operations  3.53 us (3%)
    all_to_all x2, waiting for transfers between devices, swap_yz(): lax.all_to_all(x, 'branch', 0, 0, axis_index_groups=groups, tiled=False)  20.5 us
    all_to_all x2, starting transfers between devices, swap_yz(): lax.all_to_all(x, 'branch', 0, 0, axis_index_groups=groups, tiled=False)  16.7 us
    ppermute x12, starting transfers between devices, along_y(): return lax.ppermute(x, 'branch', pairs)  15.5 us
    all_to_all x1, blocking collectives, swap_z(): lax.all_to_all(x, 'branch', 0, 0, axis_index_groups=groups, tiled=False)  14.3 us
    all_to_all x1, waiting for transfers between devices, swap_z(): lax.all_to_all(x, 'branch', 0, 0, axis_index_groups=groups, tiled=False)  8.69 us
    ppermute x12, waiting for transfers between devices, along_y(): return lax.ppermute(x, 'branch', pairs)  7.25 us
    all_to_all x1, starting transfers between devices, swap_z(): lax.all_to_all(x, 'branch', 0, 0, axis_index_groups=groups, tiled=False)  5.35 us
    pallas_call x8, Pallas kernels, grads_of(): pl.pallas_call(functools.partial(body, k, h), in_specs=[in_vmem()] * len(...  4.9 us
  transfers between devices with their start and end apart: 22, of which 10 were waited for; matrix products, arithmetic and copies ran while one was open for 0% of the time, Pallas kernels for 11%

profile of v4, /device:TPU:32, one launch (start us, length us, event | category | flops | bytes accessed | tf_op | source)
XLA Modules:
  0.0 119.3 jit_solution(6633456450738039788)
XLA Ops:
  2.0 2.2 %packet.1 = (bf16[32,24,128]{2,1,0:T(8,128)(2,1)}, bf16[4,128,128]{2,1,0:T(8,128)(2,1)}) custom-call(bf16[128,2,128]{2,1,0:T(2,128)(2,1)} %keys_far.1, bf16[128,2,128]{2,1,0:T(2,128)(2,1)} %values_far.1, s32[1,8]{1,0:T(1,128)} %ancestors_far.1, s32[1]{0:T(128)S(6)} %copy.23.group, bf16[1]{0:T(256)(128)(2,1)S(6)} %copy.22.reward), custom_call_target="tpu_custom_call" | custom-call | tf_op jit(solution)/shard_map/packet/pallas_call | solution.py:136
  4.2 11.4 %all-to-all-start = ((bf16[32,24,128]{2,1,0:T(8,128)(2,1)}), bf16[32,24,128]{2,1,0:T(8,128)(2,1)S(1)}, u32[]{:S(2)}, u32[]{:S(2)}) async-start(bf16[32,24,128]{2,1,0:T(8,128)(2,1)} %get-tuple-element.81), calls=%async_computation | async-start | bytes 393216 | tf_op jit(solution)/shard_map/all_to_all | solution.py:64
  15.6 10.9 %all-to-all-done.mine = bf16[32,24,128]{2,1,0:T(8,128)(2,1)S(1)} async-done(((bf16[32,24,128]{2,1,0:T(8,128)(2,1)}), bf16[32,24,128]{2,1,0:T(8,128)(2,1)S(1)}, u32[]{:S(2)}, u32[]{:S(2)}) %all-to-all-start) | async-done | bytes 196640 | tf_op jit(solution)/shard_map/all_to_all | solution.py:64
  26.8 1.2 %collective-permute-done.other = bf16[32,24,128]{2,1,0:T(8,128)(2,1)S(1)} collective-permute-done((bf16[32,24,128]{2,1,0:T(8,128)(2,1)S(1)}, bf16[32,24,128]{2,1,0:T(8,128)(2,1)S(1)}, u32[]{:S(2)}, u32[]{:S(2)}) %collective-permute-start) | collective-permute-done | bytes 196640 | tf_op jit(solution)/shard_map/ppermute | solution.py:49
  28.8 14.3 %all_to_all.20.column = bf16[8,8,16,128]{3,2,1,0:T(8,128)(2,1)S(1)} all-to-all(bf16[8,8,16,128]{3,2,1,0:T(8,128)(2,1)S(1)} %get-tuple-element.89), channel_id=1, replica_groups={{0,8,16,24,32,40,48,56},{4,12,20,28,36,44,52,60},{64,72,80,88,96,104,11..., dimensions={0} | all-to-all | bytes 524288 | tf_op jit(solution)/shard_map/all_to_all | solution.py:59
  43.9 2.0 %collective-permute-start.3 = (bf16[8,4,16,128]{3,2,1,0:T(8,128)(2,1)S(1)}, bf16[8,4,16,128]{3,2,1,0:T(8,128)(2,1)S(1)}, u32[]{:S(2)}, u32[]{:S(2)}) collective-permute-start(bf16[8,4,16,128]{3,2,1,0:T(8,128)(2,1)S(1)} %get-tuple-element.95), channel_id=1, source_target_pairs={{0,128},{4,132},{8,136},{12,140},{16,144},{20,148},{24,152},{28,15... | collective-permute-start | bytes 393224 | tf_op jit(solution)/shard_map/ppermute | solution.py:44
  45.9 1.3 %collective-permute-start.4 = (bf16[8,4,16,128]{3,2,1,0:T(8,128)(2,1)S(1)}, bf16[8,4,16,128]{3,2,1,0:T(8,128)(2,1)S(1)}, u32[]{:S(2)}, u32[]{:S(2)}) collective-permute-start(bf16[8,4,16,128]{3,2,1,0:T(8,128)(2,1)S(1)} %get-tuple-element.97), channel_id=1, source_target_pairs={{0,192},{4,196},{8,200},{12,204},{16,208},{20,212},{24,216},{28,22... | collective-permute-start | bytes 393224 | tf_op jit(solution)/shard_map/ppermute | solution.py:44
  48.2 1.6 %collective-permute-start.6 = (bf16[8,4,16,128]{3,2,1,0:T(8,128)(2,1)S(1)}, bf16[8,4,16,128]{3,2,1,0:T(8,128)(2,1)S(1)}, u32[]{:S(2)}, u32[]{:S(2)}) collective-permute-start(bf16[8,4,16,128]{3,2,1,0:T(8,128)(2,1)S(1)} %get-tuple-element.117), channel_id=1, source_target_pairs={{0,128},{4,132},{8,136},{12,140},{16,144},{20,148},{24,152},{28,15... | collective-permute-start | bytes 393224 | tf_op jit(solution)/shard_map/ppermute | solution.py:44
  50.7 2.8 %collective-permute-done.2.part = bf16[8,4,16,128]{3,2,1,0:T(8,128)(2,1)S(1)} collective-permute-done((bf16[8,4,16,128]{3,2,1,0:T(8,128)(2,1)S(1)}, bf16[8,4,16,128]{3,2,1,0:T(8,128)(2,1)S(1)}, u32[]{:S(2)}, u32[]{:S(2)}) %collective-permute-start.2) | collective-permute-done | bytes 131104 | tf_op jit(solution)/shard_map/ppermute | solution.py:44
  56.4 2.6 %collective-permute-start.8 = (bf16[8,4,16,128]{3,2,1,0:T(8,128)(2,1)S(1)}, bf16[8,4,16,128]{3,2,1,0:T(8,128)(2,1)S(1)}, u32[]{:S(2)}, u32[]{:S(2)}) collective-permute-start(bf16[8,4,16,128]{3,2,1,0:T(8,128)(2,1)S(1)} %get-tuple-element.131), channel_id=1, source_target_pairs={{0,192},{4,196},{8,200},{12,204},{16,208},{20,212},{24,216},{28,22... | collective-permute-start | bytes 393224 | tf_op jit(solution)/shard_map/ppermute | solution.py:44
  59.0 1.5 %collective-permute-start.9 = (bf16[8,4,16,128]{3,2,1,0:T(8,128)(2,1)S(1)}, bf16[8,4,16,128]{3,2,1,0:T(8,128)(2,1)S(1)}, u32[]{:S(2)}, u32[]{:S(2)}) collective-permute-start(bf16[8,4,16,128]{3,2,1,0:T(8,128)(2,1)S(1)} %get-tuple-element.132), channel_id=1, source_target_pairs={{0,128},{4,132},{8,136},{12,140},{16,144},{20,148},{24,152},{28,15... | collective-permute-start | bytes 393224 | tf_op jit(solution)/shard_map/ppermute | solution.py:44
  64.2 2.4 %collective-permute-start.13 = (bf16[8,4,16,128]{3,2,1,0:T(8,128)(2,1)S(1)}, bf16[8,4,16,128]{3,2,1,0:T(8,128)(2,1)S(1)}, u32[]{:S(2)}, u32[]{:S(2)}) collective-permute-start(bf16[8,4,16,128]{3,2,1,0:T(8,128)(2,1)S(1)} %get-tuple-element.147), channel_id=1, source_target_pairs={{0,128},{4,132},{8,136},{12,140},{16,144},{20,148},{24,152},{28,15... | collective-permute-start | bytes 393224 | tf_op jit(solution)/shard_map/ppermute | solution.py:44
  67.4 2.4 %collective-permute-start.14 = (bf16[8,4,16,128]{3,2,1,0:T(8,128)(2,1)S(1)}, bf16[8,4,16,128]{3,2,1,0:T(8,128)(2,1)S(1)}, u32[]{:S(2)}, u32[]{:S(2)}) collective-permute-start(bf16[8,4,16,128]{3,2,1,0:T(8,128)(2,1)S(1)} %get-tuple-element.148), channel_id=1, source_target_pairs={{0,192},{4,196},{8,200},{12,204},{16,208},{20,212},{24,216},{28,22... | collective-permute-start | bytes 393224 | tf_op jit(solution)/shard_map/ppermute | solution.py:44
  73.0 3.7 %collective-permute-done.12.refs_0_ = bf16[8,4,16,128]{3,2,1,0:T(8,128)(2,1)S(1)} collective-permute-done((bf16[8,4,16,128]{3,2,1,0:T(8,128)(2,1)S(1)}, bf16[8,4,16,128]{3,2,1,0:T(8,128)(2,1)S(1)}, u32[]{:S(2)}, u32[]{:S(2)}) %collective-permute-start.12) | collective-permute-done | bytes 131104 | tf_op jit(solution)/shard_map/ppermute | solution.py:44
  77.5 5.3 %all-to-all-start.2 = ((bf16[8,8,16,128]{3,2,1,0:T(8,128)(2,1)}), bf16[8,8,16,128]{3,2,1,0:T(8,128)(2,1)S(1)}, u32[]{:S(2)}, u32[]{:S(2)}) async-start(bf16[8,8,16,128]{3,2,1,0:T(8,128)(2,1)} %leave.1), calls=%async_computation.2 | async-start | bytes 524288 | tf_op jit(solution)/shard_map/all_to_all | solution.py:59
  82.8 8.7 %all-to-all-done.2.parts = bf16[8,8,16,128]{3,2,1,0:T(8,128)(2,1)S(1)} async-done(((bf16[8,8,16,128]{3,2,1,0:T(8,128)(2,1)}), bf16[8,8,16,128]{3,2,1,0:T(8,128)(2,1)S(1)}, u32[]{:S(2)}, u32[]{:S(2)}) %all-to-all-start.2) | async-done | bytes 262176 | tf_op jit(solution)/shard_map/all_to_all | solution.py:59
  92.4 5.3 %all-to-all-start.3 = ((bf16[32,24,128]{2,1,0:T(8,128)(2,1)}), bf16[32,24,128]{2,1,0:T(8,128)(2,1)S(1)}, u32[]{:S(2)}, u32[]{:S(2)}) async-start(bf16[32,24,128]{2,1,0:T(8,128)(2,1)} %route.1), calls=%async_computation.3 | async-start | bytes 393216 | tf_op jit(solution)/shard_map/all_to_all | solution.py:64
  97.7 1.1 assemble.1
  98.8 9.5 %all-to-all-done.3.arrived = bf16[32,24,128]{2,1,0:T(8,128)(2,1)S(1)} async-done(((bf16[32,24,128]{2,1,0:T(8,128)(2,1)}), bf16[32,24,128]{2,1,0:T(8,128)(2,1)S(1)}, u32[]{:S(2)}, u32[]{:S(2)}) %all-to-all-start.3) | async-done | bytes 196640 | tf_op jit(solution)/shard_map/all_to_all | solution.py:64
  108.5 1.2 %collective-permute-done.15.got = bf16[17,16,128]{2,1,0:T(8,128)(2,1)S(1)} collective-permute-done((bf16[17,16,128]{2,1,0:T(8,128)(2,1)S(1)}, bf16[17,16,128]{2,1,0:T(8,128)(2,1)S(1)}, u32[]{:S(2)}, u32[]{:S(2)}) %collective-permute-start.15) | collective-permute-done | bytes 69664 | tf_op jit(solution)/shard_map/ppermute | solution.py:49
  109.8 2.8 %collective-permute-start.18 = (f32[1,128]{1,0:T(1,128)S(1)}, f32[1,128]{1,0:T(1,128)S(1)}, u32[]{:S(2)}, u32[]{:S(2)}) collective-permute-start(f32[1,128]{1,0:T(1,128)S(1)} %tally.1), channel_id=1, source_target_pairs={{0,3},{1,0},{2,1},{3,2},{4,7},{5,4},{6,5},{7,6},{8,11},{9,8},{10,9... | collective-permute-start | bytes 1544 | tf_op jit(solution)/shard_map/ppermute | solution.py:54
  113.4 0.9 collective-permute-start.16
  114.3 0.9 finish.1
  115.1 2.5 %collective-permute-done.17 = f32[1,128]{1,0:T(1,128)S(1)} collective-permute-done((f32[1,128]{1,0:T(1,128)S(1)}, f32[1,128]{1,0:T(1,128)S(1)}, u32[]{:S(2)}, u32[]{:S(2)}) %collective-permute-start.17) | collective-permute-done | bytes 544 | tf_op jit(solution)/shard_map/ppermute | solution.py:54
  (67 shorter events, 17.2 us)
Async XLA Ops:
  0.6 25.9 %copy-start.2 = (bf16[128,16,128]{2,1,0:T(8,128)(2,1)S(1)}, bf16[128,16,128]{2,1,0:T(8,128)(2,1)}, u32[]{:S(2)}) copy-start(bf16[128,16,128]{2,1,0:T(8,128)(2,1)} %param.11) | copy-start | bytes 1572868
  4.2 22.4 %all-to-all-start = ((bf16[32,24,128]{2,1,0:T(8,128)(2,1)}), bf16[32,24,128]{2,1,0:T(8,128)(2,1)S(1)}, u32[]{:S(2)}, u32[]{:S(2)}) async-start(bf16[32,24,128]{2,1,0:T(8,128)(2,1)} %get-tuple-element.81), calls=%async_computation | async-start | bytes 393216 | tf_op jit(solution)/shard_map/all_to_all | solution.py:64
  15.6 12.8 %copy-start = (bf16[128,16,128]{2,1,0:T(8,128)(2,1)S(1)}, bf16[128,16,128]{2,1,0:T(8,128)(2,1)}, u32[]{:S(2)}) copy-start(bf16[128,16,128]{2,1,0:T(8,128)(2,1)} %queries.1) | copy-start | bytes 1572868
  26.5 1.4 %collective-permute-start = (bf16[32,24,128]{2,1,0:T(8,128)(2,1)S(1)}, bf16[32,24,128]{2,1,0:T(8,128)(2,1)S(1)}, u32[]{:S(2)}, u32[]{:S(2)}) collective-permute-start(bf16[32,24,128]{2,1,0:T(8,128)(2,1)S(1)} %all-to-all-done.mine), channel_id=1, source_target_pairs={{0,4},{4,0},{8,12},{12,8},{16,20},{20,16},{24,28},{28,24},{32,36},... | collective-permute-start | bytes 589832 | tf_op jit(solution)/shard_map/ppermute | solution.py:49
  28.5 19.7 %collective-permute-start.1 = (bf16[2304,128]{1,0:T(8,128)(2,1)S(1)}, bf16[2304,128]{1,0:T(8,128)(2,1)S(1)}, u32[]{:S(2)}, u32[]{:S(2)}) collective-permute-start(bf16[2304,128]{1,0:T(8,128)(2,1)S(1)} %get-tuple-element.86), channel_id=1, source_target_pairs={{0,4},{4,0},{8,12},{12,8},{16,20},{20,16},{24,28},{28,24},{32,36},... | collective-permute-start | bytes 1769480 | tf_op jit(solution)/shard_map/ppermute | solution.py:49
  43.2 10.2 %collective-permute-start.2 = (bf16[8,4,16,128]{3,2,1,0:T(8,128)(2,1)S(1)}, bf16[8,4,16,128]{3,2,1,0:T(8,128)(2,1)S(1)}, u32[]{:S(2)}, u32[]{:S(2)}) collective-permute-start(bf16[8,4,16,128]{3,2,1,0:T(8,128)(2,1)S(1)} %get-tuple-element.93), channel_id=1, source_target_pairs={{0,64},{4,68},{8,72},{12,76},{16,80},{20,84},{24,88},{28,92},{32,9... | collective-permute-start | bytes 393224 | tf_op jit(solution)/shard_map/ppermute | solution.py:44
  43.9 10.1 %collective-permute-start.3 = (bf16[8,4,16,128]{3,2,1,0:T(8,128)(2,1)S(1)}, bf16[8,4,16,128]{3,2,1,0:T(8,128)(2,1)S(1)}, u32[]{:S(2)}, u32[]{:S(2)}) collective-permute-start(bf16[8,4,16,128]{3,2,1,0:T(8,128)(2,1)S(1)} %get-tuple-element.95), channel_id=1, source_target_pairs={{0,128},{4,132},{8,136},{12,140},{16,144},{20,148},{24,152},{28,15... | collective-permute-start | bytes 393224 | tf_op jit(solution)/shard_map/ppermute | solution.py:44
  45.9 8.6 %collective-permute-start.4 = (bf16[8,4,16,128]{3,2,1,0:T(8,128)(2,1)S(1)}, bf16[8,4,16,128]{3,2,1,0:T(8,128)(2,1)S(1)}, u32[]{:S(2)}, u32[]{:S(2)}) collective-permute-start(bf16[8,4,16,128]{3,2,1,0:T(8,128)(2,1)S(1)} %get-tuple-element.97), channel_id=1, source_target_pairs={{0,192},{4,196},{8,200},{12,204},{16,208},{20,212},{24,216},{28,22... | collective-permute-start | bytes 393224 | tf_op jit(solution)/shard_map/ppermute | solution.py:44
  47.4 13.7 %collective-permute-start.5 = (bf16[8,4,16,128]{3,2,1,0:T(8,128)(2,1)S(1)}, bf16[8,4,16,128]{3,2,1,0:T(8,128)(2,1)S(1)}, u32[]{:S(2)}, u32[]{:S(2)}) collective-permute-start(bf16[8,4,16,128]{3,2,1,0:T(8,128)(2,1)S(1)} %get-tuple-element.115), channel_id=1, source_target_pairs={{0,64},{4,68},{8,72},{12,76},{16,80},{20,84},{24,88},{28,92},{32,9... | collective-permute-start | bytes 393224 | tf_op jit(solution)/shard_map/ppermute | solution.py:44
  48.2 13.5 %collective-permute-start.6 = (bf16[8,4,16,128]{3,2,1,0:T(8,128)(2,1)S(1)}, bf16[8,4,16,128]{3,2,1,0:T(8,128)(2,1)S(1)}, u32[]{:S(2)}, u32[]{:S(2)}) collective-permute-start(bf16[8,4,16,128]{3,2,1,0:T(8,128)(2,1)S(1)} %get-tuple-element.117), channel_id=1, source_target_pairs={{0,128},{4,132},{8,136},{12,140},{16,144},{20,148},{24,152},{28,15... | collective-permute-start | bytes 393224 | tf_op jit(solution)/shard_map/ppermute | solution.py:44
  53.5 8.8 %collective-permute-start.7 = (bf16[8,4,16,128]{3,2,1,0:T(8,128)(2,1)S(1)}, bf16[8,4,16,128]{3,2,1,0:T(8,128)(2,1)S(1)}, u32[]{:S(2)}, u32[]{:S(2)}) collective-permute-start(bf16[8,4,16,128]{3,2,1,0:T(8,128)(2,1)S(1)} %get-tuple-element.119), channel_id=1, source_target_pairs={{0,192},{4,196},{8,200},{12,204},{16,208},{20,212},{24,216},{28,22... | collective-permute-start | bytes 393224 | tf_op jit(solution)/shard_map/ppermute | solution.py:44
  56.4 10.3 %collective-permute-start.8 = (bf16[8,4,16,128]{3,2,1,0:T(8,128)(2,1)S(1)}, bf16[8,4,16,128]{3,2,1,0:T(8,128)(2,1)S(1)}, u32[]{:S(2)}, u32[]{:S(2)}) collective-permute-start(bf16[8,4,16,128]{3,2,1,0:T(8,128)(2,1)S(1)} %get-tuple-element.131), channel_id=1, source_target_pairs={{0,192},{4,196},{8,200},{12,204},{16,208},{20,212},{24,216},{28,22... | collective-permute-start | bytes 393224 | tf_op jit(solution)/shard_map/ppermute | solution.py:44
  59.0 7.7 %collective-permute-start.9 = (bf16[8,4,16,128]{3,2,1,0:T(8,128)(2,1)S(1)}, bf16[8,4,16,128]{3,2,1,0:T(8,128)(2,1)S(1)}, u32[]{:S(2)}, u32[]{:S(2)}) collective-permute-start(bf16[8,4,16,128]{3,2,1,0:T(8,128)(2,1)S(1)} %get-tuple-element.132), channel_id=1, source_target_pairs={{0,128},{4,132},{8,136},{12,140},{16,144},{20,148},{24,152},{28,15... | collective-permute-start | bytes 393224 | tf_op jit(solution)/shard_map/ppermute | solution.py:44
  61.1 8.7 %collective-permute-start.10 = (bf16[8,4,16,128]{3,2,1,0:T(8,128)(2,1)S(1)}, bf16[8,4,16,128]{3,2,1,0:T(8,128)(2,1)S(1)}, u32[]{:S(2)}, u32[]{:S(2)}) collective-permute-start(bf16[8,4,16,128]{3,2,1,0:T(8,128)(2,1)S(1)} %get-tuple-element.135), channel_id=1, source_target_pairs={{0,64},{4,68},{8,72},{12,76},{16,80},{20,84},{24,88},{28,92},{32,9... | collective-permute-start | bytes 393224 | tf_op jit(solution)/shard_map/ppermute | solution.py:44
  64.2 8.6 %collective-permute-start.13 = (bf16[8,4,16,128]{3,2,1,0:T(8,128)(2,1)S(1)}, bf16[8,4,16,128]{3,2,1,0:T(8,128)(2,1)S(1)}, u32[]{:S(2)}, u32[]{:S(2)}) collective-permute-start(bf16[8,4,16,128]{3,2,1,0:T(8,128)(2,1)S(1)} %get-tuple-element.147), channel_id=1, source_target_pairs={{0,128},{4,132},{8,136},{12,140},{16,144},{20,148},{24,152},{28,15... | collective-permute-start | bytes 393224 | tf_op jit(solution)/shard_map/ppermute | solution.py:44
  67.4 5.4 %collective-permute-start.14 = (bf16[8,4,16,128]{3,2,1,0:T(8,128)(2,1)S(1)}, bf16[8,4,16,128]{3,2,1,0:T(8,128)(2,1)S(1)}, u32[]{:S(2)}, u32[]{:S(2)}) collective-permute-start(bf16[8,4,16,128]{3,2,1,0:T(8,128)(2,1)S(1)} %get-tuple-element.148), channel_id=1, source_target_pairs={{0,192},{4,196},{8,200},{12,204},{16,208},{20,212},{24,216},{28,22... | collective-permute-start | bytes 393224 | tf_op jit(solution)/shard_map/ppermute | solution.py:44
  70.4 6.3 %collective-permute-start.12 = (bf16[8,4,16,128]{3,2,1,0:T(8,128)(2,1)S(1)}, bf16[8,4,16,128]{3,2,1,0:T(8,128)(2,1)S(1)}, u32[]{:S(2)}, u32[]{:S(2)}) collective-permute-start(bf16[8,4,16,128]{3,2,1,0:T(8,128)(2,1)S(1)} %get-tuple-element.146), channel_id=1, source_target_pairs={{0,64},{4,68},{8,72},{12,76},{16,80},{20,84},{24,88},{28,92},{32,9... | collective-permute-start | bytes 393224 | tf_op jit(solution)/shard_map/ppermute | solution.py:44
  77.5 14.0 %all-to-all-start.2 = ((bf16[8,8,16,128]{3,2,1,0:T(8,128)(2,1)}), bf16[8,8,16,128]{3,2,1,0:T(8,128)(2,1)S(1)}, u32[]{:S(2)}, u32[]{:S(2)}) async-start(bf16[8,8,16,128]{3,2,1,0:T(8,128)(2,1)} %leave.1), calls=%async_computation.2 | async-start | bytes 524288 | tf_op jit(solution)/shard_map/all_to_all | solution.py:59
  82.8 14.9 %collective-permute-start.11 = (f32[1280,128]{1,0:T(8,128)S(1)}, f32[1280,128]{1,0:T(8,128)S(1)}, u32[]{:S(2)}, u32[]{:S(2)}) collective-permute-start(f32[1280,128]{1,0:T(8,128)S(1)} %get-tuple-element.144), channel_id=1, source_target_pairs={{0,4},{4,0},{8,12},{12,8},{16,20},{20,16},{24,28},{28,24},{32,36},... | collective-permute-start | bytes 1966088 | tf_op jit(solution)/shard_map/ppermute | solution.py:49
  92.4 16.0 %all-to-all-start.3 = ((bf16[32,24,128]{2,1,0:T(8,128)(2,1)}), bf16[32,24,128]{2,1,0:T(8,128)(2,1)S(1)}, u32[]{:S(2)}, u32[]{:S(2)}) async-start(bf16[32,24,128]{2,1,0:T(8,128)(2,1)} %route.1), calls=%async_computation.3 | async-start | bytes 393216 | tf_op jit(solution)/shard_map/all_to_all | solution.py:64
  108.4 1.3 %collective-permute-start.15 = (bf16[17,16,128]{2,1,0:T(8,128)(2,1)S(1)}, bf16[17,16,128]{2,1,0:T(8,128)(2,1)S(1)}, u32[]{:S(2)}, u32[]{:S(2)}) collective-permute-start(bf16[17,16,128]{2,1,0:T(8,128)(2,1)S(1)} %get-tuple-element.154), channel_id=1, source_target_pairs={{0,4},{4,0},{8,12},{12,8},{16,20},{20,16},{24,28},{28,24},{32,36},... | collective-permute-start | bytes 208904 | tf_op jit(solution)/shard_map/ppermute | solution.py:49
  109.8 5.3 %collective-permute-start.18 = (f32[1,128]{1,0:T(1,128)S(1)}, f32[1,128]{1,0:T(1,128)S(1)}, u32[]{:S(2)}, u32[]{:S(2)}) collective-permute-start(f32[1,128]{1,0:T(1,128)S(1)} %tally.1), channel_id=1, source_target_pairs={{0,3},{1,0},{2,1},{3,2},{4,7},{5,4},{6,5},{7,6},{8,11},{9,8},{10,9... | collective-permute-start | bytes 1544 | tf_op jit(solution)/shard_map/ppermute | solution.py:54
  112.6 5.0 %collective-permute-start.17 = (f32[1,128]{1,0:T(1,128)S(1)}, f32[1,128]{1,0:T(1,128)S(1)}, u32[]{:S(2)}, u32[]{:S(2)}) collective-permute-start(f32[1,128]{1,0:T(1,128)S(1)} %tally.1), channel_id=1, source_target_pairs={{0,2},{1,3},{2,0},{3,1},{4,6},{5,7},{6,4},{7,5},{8,10},{9,11},{10,... | collective-permute-start | bytes 1544 | tf_op jit(solution)/shard_map/ppermute | solution.py:54
  113.4 4.8 %collective-permute-start.16 = (f32[1,128]{1,0:T(1,128)S(1)}, f32[1,128]{1,0:T(1,128)S(1)}, u32[]{:S(2)}, u32[]{:S(2)}) collective-permute-start(f32[1,128]{1,0:T(1,128)S(1)} %tally.1), channel_id=1, source_target_pairs={{0,1},{1,2},{2,3},{3,0},{4,5},{5,6},{6,7},{7,4},{8,9},{9,10},{10,1... | collective-permute-start | bytes 1544 | tf_op jit(solution)/shard_map/ppermute | solution.py:54
  (2 other events, 13.0 us)

commit v5 on v4

--- a/solution.py
+++ b/solution.py
@@ -622,9 +622,7 @@
     for z in range(NZ):
         at = 2 * (z % 2) + z // 4
         rows = slice(8 * (z // 2 % 2), 8 * (z // 2 % 2) + 8)
-        for j in range(HALF):
-            pair = [acc[2 * j + i, at, rows, :] for i in range(2)]
-            halves[z, j] = jnp.concatenate(pair, 0).astype(BF16)
+        halves[z] = acc[:, at, rows, :].reshape(HALF, 16, LANES).astype(BF16)
 
 
 ACC = (2 * HALF, QUAD, 16, LANES)
@@ -692,15 +690,15 @@
     total_kernel(parts, squares, totals, sums)
     c = place()[2]
     words = table[HOLD : HOLD + 8, :]
-    blank = jnp.concatenate([jnp.zeros((16, LANES), F32), split_rows(sums[...], 8)], 0)
-    room[0 : NY * NZ] = jnp.broadcast_to(blank[None], (NY * NZ, 24, LANES))
+    room[...] = jnp.zeros_like(room)
     for s in range(2 * HALF):
         block = ((words[s // 3, 0] >> (7 * (s % 3))) & 127) - 1
-        side = jnp.where((block & 1) == c, 0, 8)
-        to = jnp.where(block >= 0, block >> 1, NY * NZ)
-        piece = totals[s // 2, 8 * (s % 2) : 8 * (s % 2) + 8, :]
-        room[to, pl.ds(pl.multiple_of(side, 8), 8), :] = piece
-    out[...] = room[0 : NY * NZ].astype(BF16)
+        side = jnp.where((block & 1) == c, 0, 1)
+        to = jnp.where(block >= 0, (block >> 1) * 2 + side, NBLK)
+        room[to] = totals[s // 2, 8 * (s % 2) : 8 * (s % 2) + 8, :]
+    tails = jnp.broadcast_to(split_rows(sums[...], 8)[None], (NY * NZ, 8, LANES))
+    rows = room[0:NBLK].reshape(NY * NZ, 16, LANES)
+    out[...] = jnp.concatenate([rows, tails], 1).astype(BF16)
 
 
 def route(table, parts, squares):
@@ -712,7 +710,7 @@
             route_kernel,
             jax.ShapeDtypeStruct((NY * NZ, 24, LANES), BF16),
             [
-                VMEM((NY * NZ + 1, 24, LANES), F32),
+                VMEM((NBLK + 1, 8, LANES), F32),
                 VMEM((HALF, 16, LANES), F32),
                 VMEM((8, LANES), F32),
             ],
@@ -723,13 +721,9 @@
 
 def share_kernel(arrived, after, send, sums):
     whole = arrived[...].astype(F32)
-    for i in range(NY * NZ // 2):
-        pair = [whole[2 * i + j, 8:16, :] for j in range(2)]
-        send[i] = jnp.concatenate(pair, 0).astype(BF16)
+    send[...] = whole[:, 8:16, :].reshape(NY * NZ // 2, 16, LANES).astype(BF16)
     tails = jnp.sum(jnp.sum(whole[:, 16:24, :], axis=0), axis=0, keepdims=True)
-    value = jnp.broadcast_to(tails, (8, LANES))
-    sums[...] = value
-    send[NY * NZ // 2] = split_rows(value, 16).astype(BF16)
+    sums[...] = jnp.broadcast_to(jnp.sum(tails, axis=1, keepdims=True), (1, LANES))
 
 
 def share(arrived, after):
@@ -740,30 +734,16 @@
         **call(
             share_kernel,
             (
-                jax.ShapeDtypeStruct((NY * NZ // 2 + 1, 16, LANES), BF16),
-                jax.ShapeDtypeStruct((8, LANES), F32),
+                jax.ShapeDtypeStruct((NY * NZ // 2, 16, LANES), BF16),
+                jax.ShapeDtypeStruct((1, LANES), F32),
             ),
         ),
         name="share",
     )(arrived, after)
 
 
-def tally_kernel(mine, got, sums):
-    tails = mine[0:1, :] + jnp.sum(got[NY * NZ // 2].astype(F32), axis=0, keepdims=True)
-    sums[...] = jnp.broadcast_to(jnp.sum(tails, axis=1, keepdims=True), (1, LANES))
-
-
-def tally(mine, got):
-    return pl.pallas_call(
-        tally_kernel,
-        in_specs=[in_vmem()] * 2,
-        out_specs=in_vmem(),
-        **call(tally_kernel, jax.ShapeDtypeStruct((1, LANES), F32)),
-        name="tally",
-    )(mine, got)
-
-
-def finish_kernel(table, arrived, got, own, own_far, key_grad, value_grad):
+def finish_kernel(table, arrived, got, own, own_far, key_grad, value_grad, token):
+    token[...] = jnp.zeros_like(token)
     first_core = place()[2] == 0
     inner = table[INNER : INNER + 1, :] > 0
     for z in range(NZ):
@@ -784,8 +764,12 @@
     return pl.pallas_call(
         finish_kernel,
         in_specs=[in_vmem()] * 5,
-        out_specs=(in_vmem(),) * 2,
-        **call(finish_kernel, (jax.ShapeDtypeStruct((TOK, KV, HD), F32),) * 2),
+        out_specs=(in_vmem(),) * 3,
+        **call(
+            finish_kernel,
+            (jax.ShapeDtypeStruct((TOK, KV, HD), F32),) * 2
+            + (jax.ShapeDtypeStruct((1, LANES), F32),),
+        ),
         cost_estimate=SMALL,
         name="finish",
     )(*arrays)
@@ -826,12 +810,12 @@
     halves = leave(acc)
     arrived = swap_yz(route(table, swap_z(halves), squares))
     shared, mine_sum = share(arrived, done)
-    shared = other_core(shared)
-    mine_sum = tally(mine_sum, shared)
     all_sum = mine_sum
     for k in (1, 2, 3):
         all_sum = all_sum + along_head(mine_sum, k)
-    key_grad, value_grad = finish(table, arrived, shared, own_0, far)
+    shared = other_core(shared)
+    key_grad, value_grad, token = finish(table, arrived, shared, own_0, far)
+    all_sum = all_sum + (other_core(all_sum) + token)
     count = float(NBLK * TOK * NHEAD * (KV * RATIO + 2 * KV) * HD)
     grad_rms = jnp.sqrt(all_sum[0, 0] / count)
     return query_grad, key_grad, value_grad, grad_rms

time: 120 us -> 121 us (level); the launches traced: 119 us -> 119 us
    ppermute x4 -> x5, waiting for transfers between devices: 2.47 us -> 1.47 us  [other_core(): return lax.ppermute(x, 'branch', pairs)]
  transfers between devices with their start and end apart: 22 -> 23, of which waited for: 10 -> 10; matrix products, arithmetic and copies ran while one was open for 0% -> 0% of each run, Pallas kernels for 11% -> 11%
where the time goes in v5:
time: 121 us; the launch traced here: 119 us
  starting transfers between devices  42.2 us (35%)
  waiting for transfers between devices  41.7 us (34%)
  Pallas kernels  17.1 us (14%)
  blocking collectives  14.3 us (12%)
  between operations  3.52 us (3%)
    all_to_all x2, waiting for transfers between devices, swap_yz(): lax.all_to_all(x, 'branch', 0, 0, axis_index_groups=groups, tiled=False)  20.4 us
    all_to_all x2, starting transfers between devices, swap_yz(): lax.all_to_all(x, 'branch', 0, 0, axis_index_groups=groups, tiled=False)  16.7 us
    ppermute x12, starting transfers between devices, along_y(): return lax.ppermute(x, 'branch', pairs)  15.5 us
    all_to_all x1, blocking collectives, swap_z(): lax.all_to_all(x, 'branch', 0, 0, axis_index_groups=groups, tiled=False)  14.3 us
    all_to_all x1, waiting for transfers between devices, swap_z(): lax.all_to_all(x, 'branch', 0, 0, axis_index_groups=groups, tiled=False)  8.69 us
    ppermute x12, waiting for transfers between devices, along_y(): return lax.ppermute(x, 'branch', pairs)  7.24 us
    all_to_all x1, starting transfers between devices, swap_z(): lax.all_to_all(x, 'branch', 0, 0, axis_index_groups=groups, tiled=False)  5.34 us
    pallas_call x8, Pallas kernels, grads_of(): pl.pallas_call(functools.partial(body, k, h), in_specs=[in_vmem()] * len(...  4.9 us
  transfers between devices with their start and end apart: 23, of which 10 were waited for; matrix products, arithmetic and copies ran while one was open for 0% of the time, Pallas kernels for 11%

profile of v5, /device:TPU:32, one launch (start us, length us, event | category | flops | bytes accessed | tf_op | source)
XLA Modules:
  0.0 119.0 jit_solution(11976058536089069943)
XLA Ops:
  2.0 2.2 %packet.1 = (bf16[32,24,128]{2,1,0:T(8,128)(2,1)}, bf16[4,128,128]{2,1,0:T(8,128)(2,1)}) custom-call(bf16[128,2,128]{2,1,0:T(2,128)(2,1)} %keys_far.1, bf16[128,2,128]{2,1,0:T(2,128)(2,1)} %values_far.1, s32[1,8]{1,0:T(1,128)} %ancestors_far.1, s32[1]{0:T(128)S(6)} %copy.23.group, bf16[1]{0:T(256)(128)(2,1)S(6)} %copy.22.reward), custom_call_target="tpu_custom_call" | custom-call | tf_op jit(solution)/shard_map/packet/pallas_call | solution.py:136
  4.2 11.4 %all-to-all-start = ((bf16[32,24,128]{2,1,0:T(8,128)(2,1)}), bf16[32,24,128]{2,1,0:T(8,128)(2,1)S(1)}, u32[]{:S(2)}, u32[]{:S(2)}) async-start(bf16[32,24,128]{2,1,0:T(8,128)(2,1)} %get-tuple-element.82), calls=%async_computation | async-start | bytes 393216 | tf_op jit(solution)/shard_map/all_to_all | solution.py:64
  15.6 10.9 %all-to-all-done.mine = bf16[32,24,128]{2,1,0:T(8,128)(2,1)S(1)} async-done(((bf16[32,24,128]{2,1,0:T(8,128)(2,1)}), bf16[32,24,128]{2,1,0:T(8,128)(2,1)S(1)}, u32[]{:S(2)}, u32[]{:S(2)}) %all-to-all-start) | async-done | bytes 196640 | tf_op jit(solution)/shard_map/all_to_all | solution.py:64
  26.8 1.2 %collective-permute-done.other = bf16[32,24,128]{2,1,0:T(8,128)(2,1)S(1)} collective-permute-done((bf16[32,24,128]{2,1,0:T(8,128)(2,1)S(1)}, bf16[32,24,128]{2,1,0:T(8,128)(2,1)S(1)}, u32[]{:S(2)}, u32[]{:S(2)}) %collective-permute-start) | collective-permute-done | bytes 196640 | tf_op jit(solution)/shard_map/ppermute | solution.py:49
  28.8 14.3 %all_to_all.20.column = bf16[8,8,16,128]{3,2,1,0:T(8,128)(2,1)S(1)} all-to-all(bf16[8,8,16,128]{3,2,1,0:T(8,128)(2,1)S(1)} %get-tuple-element.90), channel_id=1, replica_groups={{0,8,16,24,32,40,48,56},{4,12,20,28,36,44,52,60},{64,72,80,88,96,104,11..., dimensions={0} | all-to-all | bytes 524288 | tf_op jit(solution)/shard_map/all_to_all | solution.py:59
  43.9 2.0 %collective-permute-start.3 = (bf16[8,4,16,128]{3,2,1,0:T(8,128)(2,1)S(1)}, bf16[8,4,16,128]{3,2,1,0:T(8,128)(2,1)S(1)}, u32[]{:S(2)}, u32[]{:S(2)}) collective-permute-start(bf16[8,4,16,128]{3,2,1,0:T(8,128)(2,1)S(1)} %get-tuple-element.96), channel_id=1, source_target_pairs={{0,128},{4,132},{8,136},{12,140},{16,144},{20,148},{24,152},{28,15... | collective-permute-start | bytes 393224 | tf_op jit(solution)/shard_map/ppermute | solution.py:44
  45.9 1.3 %collective-permute-start.4 = (bf16[8,4,16,128]{3,2,1,0:T(8,128)(2,1)S(1)}, bf16[8,4,16,128]{3,2,1,0:T(8,128)(2,1)S(1)}, u32[]{:S(2)}, u32[]{:S(2)}) collective-permute-start(bf16[8,4,16,128]{3,2,1,0:T(8,128)(2,1)S(1)} %get-tuple-element.98), channel_id=1, source_target_pairs={{0,192},{4,196},{8,200},{12,204},{16,208},{20,212},{24,216},{28,22... | collective-permute-start | bytes 393224 | tf_op jit(solution)/shard_map/ppermute | solution.py:44
  48.2 1.6 %collective-permute-start.6 = (bf16[8,4,16,128]{3,2,1,0:T(8,128)(2,1)S(1)}, bf16[8,4,16,128]{3,2,1,0:T(8,128)(2,1)S(1)}, u32[]{:S(2)}, u32[]{:S(2)}) collective-permute-start(bf16[8,4,16,128]{3,2,1,0:T(8,128)(2,1)S(1)} %get-tuple-element.118), channel_id=1, source_target_pairs={{0,128},{4,132},{8,136},{12,140},{16,144},{20,148},{24,152},{28,15... | collective-permute-start | bytes 393224 | tf_op jit(solution)/shard_map/ppermute | solution.py:44
  50.7 2.8 %collective-permute-done.2.part = bf16[8,4,16,128]{3,2,1,0:T(8,128)(2,1)S(1)} collective-permute-done((bf16[8,4,16,128]{3,2,1,0:T(8,128)(2,1)S(1)}, bf16[8,4,16,128]{3,2,1,0:T(8,128)(2,1)S(1)}, u32[]{:S(2)}, u32[]{:S(2)}) %collective-permute-start.2) | collective-permute-done | bytes 131104 | tf_op jit(solution)/shard_map/ppermute | solution.py:44
  56.4 2.6 %collective-permute-start.8 = (bf16[8,4,16,128]{3,2,1,0:T(8,128)(2,1)S(1)}, bf16[8,4,16,128]{3,2,1,0:T(8,128)(2,1)S(1)}, u32[]{:S(2)}, u32[]{:S(2)}) collective-permute-start(bf16[8,4,16,128]{3,2,1,0:T(8,128)(2,1)S(1)} %get-tuple-element.132), channel_id=1, source_target_pairs={{0,192},{4,196},{8,200},{12,204},{16,208},{20,212},{24,216},{28,22... | collective-permute-start | bytes 393224 | tf_op jit(solution)/shard_map/ppermute | solution.py:44
  59.0 1.5 %collective-permute-start.9 = (bf16[8,4,16,128]{3,2,1,0:T(8,128)(2,1)S(1)}, bf16[8,4,16,128]{3,2,1,0:T(8,128)(2,1)S(1)}, u32[]{:S(2)}, u32[]{:S(2)}) collective-permute-start(bf16[8,4,16,128]{3,2,1,0:T(8,128)(2,1)S(1)} %get-tuple-element.133), channel_id=1, source_target_pairs={{0,128},{4,132},{8,136},{12,140},{16,144},{20,148},{24,152},{28,15... | collective-permute-start | bytes 393224 | tf_op jit(solution)/shard_map/ppermute | solution.py:44
  64.2 2.4 %collective-permute-start.13 = (bf16[8,4,16,128]{3,2,1,0:T(8,128)(2,1)S(1)}, bf16[8,4,16,128]{3,2,1,0:T(8,128)(2,1)S(1)}, u32[]{:S(2)}, u32[]{:S(2)}) collective-permute-start(bf16[8,4,16,128]{3,2,1,0:T(8,128)(2,1)S(1)} %get-tuple-element.148), channel_id=1, source_target_pairs={{0,128},{4,132},{8,136},{12,140},{16,144},{20,148},{24,152},{28,15... | collective-permute-start | bytes 393224 | tf_op jit(solution)/shard_map/ppermute | solution.py:44
  67.4 2.4 %collective-permute-start.14 = (bf16[8,4,16,128]{3,2,1,0:T(8,128)(2,1)S(1)}, bf16[8,4,16,128]{3,2,1,0:T(8,128)(2,1)S(1)}, u32[]{:S(2)}, u32[]{:S(2)}) collective-permute-start(bf16[8,4,16,128]{3,2,1,0:T(8,128)(2,1)S(1)} %get-tuple-element.149), channel_id=1, source_target_pairs={{0,192},{4,196},{8,200},{12,204},{16,208},{20,212},{24,216},{28,22... | collective-permute-start | bytes 393224 | tf_op jit(solution)/shard_map/ppermute | solution.py:44
  73.0 3.7 %collective-permute-done.12.refs_0_ = bf16[8,4,16,128]{3,2,1,0:T(8,128)(2,1)S(1)} collective-permute-done((bf16[8,4,16,128]{3,2,1,0:T(8,128)(2,1)S(1)}, bf16[8,4,16,128]{3,2,1,0:T(8,128)(2,1)S(1)}, u32[]{:S(2)}, u32[]{:S(2)}) %collective-permute-start.12) | collective-permute-done | bytes 131104 | tf_op jit(solution)/shard_map/ppermute | solution.py:44
  77.5 5.3 %all-to-all-start.2 = ((bf16[8,8,16,128]{3,2,1,0:T(8,128)(2,1)}), bf16[8,8,16,128]{3,2,1,0:T(8,128)(2,1)S(1)}, u32[]{:S(2)}, u32[]{:S(2)}) async-start(bf16[8,8,16,128]{3,2,1,0:T(8,128)(2,1)} %leave.1), calls=%async_computation.2 | async-start | bytes 524288 | tf_op jit(solution)/shard_map/all_to_all | solution.py:59
  82.8 8.7 %all-to-all-done.2.parts = bf16[8,8,16,128]{3,2,1,0:T(8,128)(2,1)S(1)} async-done(((bf16[8,8,16,128]{3,2,1,0:T(8,128)(2,1)}), bf16[8,8,16,128]{3,2,1,0:T(8,128)(2,1)S(1)}, u32[]{:S(2)}, u32[]{:S(2)}) %all-to-all-start.2) | async-done | bytes 262176 | tf_op jit(solution)/shard_map/all_to_all | solution.py:59
  91.5 0.8 route.1
  92.3 5.3 %all-to-all-start.3 = ((bf16[32,24,128]{2,1,0:T(8,128)(2,1)}), bf16[32,24,128]{2,1,0:T(8,128)(2,1)S(1)}, u32[]{:S(2)}, u32[]{:S(2)}) async-start(bf16[32,24,128]{2,1,0:T(8,128)(2,1)} %route.1), calls=%async_computation.3 | async-start | bytes 393216 | tf_op jit(solution)/shard_map/all_to_all | solution.py:64
  97.7 1.1 assemble.1
  98.8 9.5 %all-to-all-done.3.arrived = bf16[32,24,128]{2,1,0:T(8,128)(2,1)S(1)} async-done(((bf16[32,24,128]{2,1,0:T(8,128)(2,1)}), bf16[32,24,128]{2,1,0:T(8,128)(2,1)S(1)}, u32[]{:S(2)}, u32[]{:S(2)}) %all-to-all-start.3) | async-done | bytes 196640 | tf_op jit(solution)/shard_map/all_to_all | solution.py:64
  108.4 2.8 %collective-permute-start.18 = (f32[1,128]{1,0:T(1,128)S(1)}, f32[1,128]{1,0:T(1,128)S(1)}, u32[]{:S(2)}, u32[]{:S(2)}) collective-permute-start(f32[1,128]{1,0:T(1,128)S(1)} %get-tuple-element.158), channel_id=1, source_target_pairs={{0,3},{1,0},{2,1},{3,2},{4,7},{5,4},{6,5},{7,6},{8,11},{9,8},{10,9... | collective-permute-start | bytes 1544 | tf_op jit(solution)/shard_map/ppermute | solution.py:54
  111.9 0.9 collective-permute-start.16
  112.8 3.3 %collective-permute-done.17 = f32[1,128]{1,0:T(1,128)S(1)} collective-permute-done((f32[1,128]{1,0:T(1,128)S(1)}, f32[1,128]{1,0:T(1,128)S(1)}, u32[]{:S(2)}, u32[]{:S(2)}) %collective-permute-start.17) | collective-permute-done | bytes 544 | tf_op jit(solution)/shard_map/ppermute | solution.py:54
  116.7 0.9 finish.1
  (69 shorter events, 16.6 us)
Async XLA Ops:
  0.6 25.9 %copy-start.2 = (bf16[128,16,128]{2,1,0:T(8,128)(2,1)S(1)}, bf16[128,16,128]{2,1,0:T(8,128)(2,1)}, u32[]{:S(2)}) copy-start(bf16[128,16,128]{2,1,0:T(8,128)(2,1)} %param.11) | copy-start | bytes 1572868
  4.2 22.4 %all-to-all-start = ((bf16[32,24,128]{2,1,0:T(8,128)(2,1)}), bf16[32,24,128]{2,1,0:T(8,128)(2,1)S(1)}, u32[]{:S(2)}, u32[]{:S(2)}) async-start(bf16[32,24,128]{2,1,0:T(8,128)(2,1)} %get-tuple-element.82), calls=%async_computation | async-start | bytes 393216 | tf_op jit(solution)/shard_map/all_to_all | solution.py:64
  26.5 1.4 %collective-permute-start = (bf16[32,24,128]{2,1,0:T(8,128)(2,1)S(1)}, bf16[32,24,128]{2,1,0:T(8,128)(2,1)S(1)}, u32[]{:S(2)}, u32[]{:S(2)}) collective-permute-start(bf16[32,24,128]{2,1,0:T(8,128)(2,1)S(1)} %all-to-all-done.mine), channel_id=1, source_target_pairs={{0,4},{4,0},{8,12},{12,8},{16,20},{20,16},{24,28},{28,24},{32,36},... | collective-permute-start | bytes 589832 | tf_op jit(solution)/shard_map/ppermute | solution.py:49
  28.5 19.7 %collective-permute-start.1 = (bf16[2304,128]{1,0:T(8,128)(2,1)S(1)}, bf16[2304,128]{1,0:T(8,128)(2,1)S(1)}, u32[]{:S(2)}, u32[]{:S(2)}) collective-permute-start(bf16[2304,128]{1,0:T(8,128)(2,1)S(1)} %get-tuple-element.87), channel_id=1, source_target_pairs={{0,4},{4,0},{8,12},{12,8},{16,20},{20,16},{24,28},{28,24},{32,36},... | collective-permute-start | bytes 1769480 | tf_op jit(solution)/shard_map/ppermute | solution.py:49
  43.2 10.2 %collective-permute-start.2 = (bf16[8,4,16,128]{3,2,1,0:T(8,128)(2,1)S(1)}, bf16[8,4,16,128]{3,2,1,0:T(8,128)(2,1)S(1)}, u32[]{:S(2)}, u32[]{:S(2)}) collective-permute-start(bf16[8,4,16,128]{3,2,1,0:T(8,128)(2,1)S(1)} %get-tuple-element.94), channel_id=1, source_target_pairs={{0,64},{4,68},{8,72},{12,76},{16,80},{20,84},{24,88},{28,92},{32,9... | collective-permute-start | bytes 393224 | tf_op jit(solution)/shard_map/ppermute | solution.py:44
  43.9 10.1 %collective-permute-start.3 = (bf16[8,4,16,128]{3,2,1,0:T(8,128)(2,1)S(1)}, bf16[8,4,16,128]{3,2,1,0:T(8,128)(2,1)S(1)}, u32[]{:S(2)}, u32[]{:S(2)}) collective-permute-start(bf16[8,4,16,128]{3,2,1,0:T(8,128)(2,1)S(1)} %get-tuple-element.96), channel_id=1, source_target_pairs={{0,128},{4,132},{8,136},{12,140},{16,144},{20,148},{24,152},{28,15... | collective-permute-start | bytes 393224 | tf_op jit(solution)/shard_map/ppermute | solution.py:44
  45.9 8.6 %collective-permute-start.4 = (bf16[8,4,16,128]{3,2,1,0:T(8,128)(2,1)S(1)}, bf16[8,4,16,128]{3,2,1,0:T(8,128)(2,1)S(1)}, u32[]{:S(2)}, u32[]{:S(2)}) collective-permute-start(bf16[8,4,16,128]{3,2,1,0:T(8,128)(2,1)S(1)} %get-tuple-element.98), channel_id=1, source_target_pairs={{0,192},{4,196},{8,200},{12,204},{16,208},{20,212},{24,216},{28,22... | collective-permute-start | bytes 393224 | tf_op jit(solution)/shard_map/ppermute | solution.py:44
  47.4 13.7 %collective-permute-start.5 = (bf16[8,4,16,128]{3,2,1,0:T(8,128)(2,1)S(1)}, bf16[8,4,16,128]{3,2,1,0:T(8,128)(2,1)S(1)}, u32[]{:S(2)}, u32[]{:S(2)}) collective-permute-start(bf16[8,4,16,128]{3,2,1,0:T(8,128)(2,1)S(1)} %get-tuple-element.116), channel_id=1, source_target_pairs={{0,64},{4,68},{8,72},{12,76},{16,80},{20,84},{24,88},{28,92},{32,9... | collective-permute-start | bytes 393224 | tf_op jit(solution)/shard_map/ppermute | solution.py:44
  48.2 13.5 %collective-permute-start.6 = (bf16[8,4,16,128]{3,2,1,0:T(8,128)(2,1)S(1)}, bf16[8,4,16,128]{3,2,1,0:T(8,128)(2,1)S(1)}, u32[]{:S(2)}, u32[]{:S(2)}) collective-permute-start(bf16[8,4,16,128]{3,2,1,0:T(8,128)(2,1)S(1)} %get-tuple-element.118), channel_id=1, source_target_pairs={{0,128},{4,132},{8,136},{12,140},{16,144},{20,148},{24,152},{28,15... | collective-permute-start | bytes 393224 | tf_op jit(solution)/shard_map/ppermute | solution.py:44
  53.5 8.8 %collective-permute-start.7 = (bf16[8,4,16,128]{3,2,1,0:T(8,128)(2,1)S(1)}, bf16[8,4,16,128]{3,2,1,0:T(8,128)(2,1)S(1)}, u32[]{:S(2)}, u32[]{:S(2)}) collective-permute-start(bf16[8,4,16,128]{3,2,1,0:T(8,128)(2,1)S(1)} %get-tuple-element.120), channel_id=1, source_target_pairs={{0,192},{4,196},{8,200},{12,204},{16,208},{20,212},{24,216},{28,22... | collective-permute-start | bytes 393224 | tf_op jit(solution)/shard_map/ppermute | solution.py:44
  56.4 10.3 %collective-permute-start.8 = (bf16[8,4,16,128]{3,2,1,0:T(8,128)(2,1)S(1)}, bf16[8,4,16,128]{3,2,1,0:T(8,128)(2,1)S(1)}, u32[]{:S(2)}, u32[]{:S(2)}) collective-permute-start(bf16[8,4,16,128]{3,2,1,0:T(8,128)(2,1)S(1)} %get-tuple-element.132), channel_id=1, source_target_pairs={{0,192},{4,196},{8,200},{12,204},{16,208},{20,212},{24,216},{28,22... | collective-permute-start | bytes 393224 | tf_op jit(solution)/shard_map/ppermute | solution.py:44
  59.0 7.7 %collective-permute-start.9 = (bf16[8,4,16,128]{3,2,1,0:T(8,128)(2,1)S(1)}, bf16[8,4,16,128]{3,2,1,0:T(8,128)(2,1)S(1)}, u32[]{:S(2)}, u32[]{:S(2)}) collective-permute-start(bf16[8,4,16,128]{3,2,1,0:T(8,128)(2,1)S(1)} %get-tuple-element.133), channel_id=1, source_target_pairs={{0,128},{4,132},{8,136},{12,140},{16,144},{20,148},{24,152},{28,15... | collective-permute-start | bytes 393224 | tf_op jit(solution)/shard_map/ppermute | solution.py:44
  61.1 8.7 %collective-permute-start.10 = (bf16[8,4,16,128]{3,2,1,0:T(8,128)(2,1)S(1)}, bf16[8,4,16,128]{3,2,1,0:T(8,128)(2,1)S(1)}, u32[]{:S(2)}, u32[]{:S(2)}) collective-permute-start(bf16[8,4,16,128]{3,2,1,0:T(8,128)(2,1)S(1)} %get-tuple-element.136), channel_id=1, source_target_pairs={{0,64},{4,68},{8,72},{12,76},{16,80},{20,84},{24,88},{28,92},{32,9... | collective-permute-start | bytes 393224 | tf_op jit(solution)/shard_map/ppermute | solution.py:44
  64.2 8.7 %collective-permute-start.13 = (bf16[8,4,16,128]{3,2,1,0:T(8,128)(2,1)S(1)}, bf16[8,4,16,128]{3,2,1,0:T(8,128)(2,1)S(1)}, u32[]{:S(2)}, u32[]{:S(2)}) collective-permute-start(bf16[8,4,16,128]{3,2,1,0:T(8,128)(2,1)S(1)} %get-tuple-element.148), channel_id=1, source_target_pairs={{0,128},{4,132},{8,136},{12,140},{16,144},{20,148},{24,152},{28,15... | collective-permute-start | bytes 393224 | tf_op jit(solution)/shard_map/ppermute | solution.py:44
  67.4 5.4 %collective-permute-start.14 = (bf16[8,4,16,128]{3,2,1,0:T(8,128)(2,1)S(1)}, bf16[8,4,16,128]{3,2,1,0:T(8,128)(2,1)S(1)}, u32[]{:S(2)}, u32[]{:S(2)}) collective-permute-start(bf16[8,4,16,128]{3,2,1,0:T(8,128)(2,1)S(1)} %get-tuple-element.149), channel_id=1, source_target_pairs={{0,192},{4,196},{8,200},{12,204},{16,208},{20,212},{24,216},{28,22... | collective-permute-start | bytes 393224 | tf_op jit(solution)/shard_map/ppermute | solution.py:44
  70.4 6.3 %collective-permute-start.12 = (bf16[8,4,16,128]{3,2,1,0:T(8,128)(2,1)S(1)}, bf16[8,4,16,128]{3,2,1,0:T(8,128)(2,1)S(1)}, u32[]{:S(2)}, u32[]{:S(2)}) collective-permute-start(bf16[8,4,16,128]{3,2,1,0:T(8,128)(2,1)S(1)} %get-tuple-element.147), channel_id=1, source_target_pairs={{0,64},{4,68},{8,72},{12,76},{16,80},{20,84},{24,88},{28,92},{32,9... | collective-permute-start | bytes 393224 | tf_op jit(solution)/shard_map/ppermute | solution.py:44
  77.5 14.0 %all-to-all-start.2 = ((bf16[8,8,16,128]{3,2,1,0:T(8,128)(2,1)}), bf16[8,8,16,128]{3,2,1,0:T(8,128)(2,1)S(1)}, u32[]{:S(2)}, u32[]{:S(2)}) async-start(bf16[8,8,16,128]{3,2,1,0:T(8,128)(2,1)} %leave.1), calls=%async_computation.2 | async-start | bytes 524288 | tf_op jit(solution)/shard_map/all_to_all | solution.py:59
  82.8 14.8 %collective-permute-start.11 = (f32[1280,128]{1,0:T(8,128)S(1)}, f32[1280,128]{1,0:T(8,128)S(1)}, u32[]{:S(2)}, u32[]{:S(2)}) collective-permute-start(f32[1280,128]{1,0:T(8,128)S(1)} %get-tuple-element.145), channel_id=1, source_target_pairs={{0,4},{4,0},{8,12},{12,8},{16,20},{20,16},{24,28},{28,24},{32,36},... | collective-permute-start | bytes 1966088 | tf_op jit(solution)/shard_map/ppermute | solution.py:49
  92.3 15.9 %all-to-all-start.3 = ((bf16[32,24,128]{2,1,0:T(8,128)(2,1)}), bf16[32,24,128]{2,1,0:T(8,128)(2,1)S(1)}, u32[]{:S(2)}, u32[]{:S(2)}) async-start(bf16[32,24,128]{2,1,0:T(8,128)(2,1)} %route.1), calls=%async_computation.3 | async-start | bytes 393216 | tf_op jit(solution)/shard_map/all_to_all | solution.py:64
  108.4 4.5 %collective-permute-start.18 = (f32[1,128]{1,0:T(1,128)S(1)}, f32[1,128]{1,0:T(1,128)S(1)}, u32[]{:S(2)}, u32[]{:S(2)}) collective-permute-start(f32[1,128]{1,0:T(1,128)S(1)} %get-tuple-element.158), channel_id=1, source_target_pairs={{0,3},{1,0},{2,1},{3,2},{4,7},{5,4},{6,5},{7,6},{8,11},{9,8},{10,9... | collective-permute-start | bytes 1544 | tf_op jit(solution)/shard_map/ppermute | solution.py:54
  111.1 5.0 %collective-permute-start.17 = (f32[1,128]{1,0:T(1,128)S(1)}, f32[1,128]{1,0:T(1,128)S(1)}, u32[]{:S(2)}, u32[]{:S(2)}) collective-permute-start(f32[1,128]{1,0:T(1,128)S(1)} %get-tuple-element.158), channel_id=1, source_target_pairs={{0,2},{1,3},{2,0},{3,1},{4,6},{5,7},{6,4},{7,5},{8,10},{9,11},{10,... | collective-permute-start | bytes 1544 | tf_op jit(solution)/shard_map/ppermute | solution.py:54
  111.9 4.8 %collective-permute-start.16 = (f32[1,128]{1,0:T(1,128)S(1)}, f32[1,128]{1,0:T(1,128)S(1)}, u32[]{:S(2)}, u32[]{:S(2)}) collective-permute-start(f32[1,128]{1,0:T(1,128)S(1)} %get-tuple-element.158), channel_id=1, source_target_pairs={{0,1},{1,2},{2,3},{3,0},{4,5},{5,6},{6,7},{7,4},{8,9},{9,10},{10,1... | collective-permute-start | bytes 1544 | tf_op jit(solution)/shard_map/ppermute | solution.py:54
  112.8 3.9 %collective-permute-start.15 = (bf16[16,16,128]{2,1,0:T(8,128)(2,1)S(1)}, bf16[16,16,128]{2,1,0:T(8,128)(2,1)S(1)}, u32[]{:S(2)}, u32[]{:S(2)}) collective-permute-start(bf16[16,16,128]{2,1,0:T(8,128)(2,1)S(1)} %get-tuple-element.155), channel_id=1, source_target_pairs={{0,4},{4,0},{8,12},{12,8},{16,20},{20,16},{24,28},{28,24},{32,36},... | collective-permute-start | bytes 196616 | tf_op jit(solution)/shard_map/ppermute | solution.py:49
  116.7 1.1 collective-permute-start.19
  (3 other events, 25.7 us)

commit v6 on v5

--- a/solution.py
+++ b/solution.py
@@ -525,6 +525,22 @@
     )(table, *dqs, *owns)
 
 
+def ship_kernel(far, after, out):
+    pass
+
+
+def ship(far, after):
+    return pl.pallas_call(
+        ship_kernel,
+        in_specs=[in_vmem(), pl.BlockSpec(memory_space=pl.ANY)],
+        out_specs=in_vmem(),
+        input_output_aliases={0: 0},
+        **call(ship_kernel, jax.ShapeDtypeStruct(far.shape, F32), vmem_mb=16),
+        cost_estimate=SMALL,
+        name="ship",
+    )(far, after)
+
+
 def assemble_kernel(keep, got, query_grad, token):
     first_core = place()[2] == 0
     near, far = keep[...], got[0:ROWS]
@@ -543,7 +559,7 @@
             assemble_kernel,
             (
                 jax.ShapeDtypeStruct((TOK, KV * RATIO, HD), F32),
-                jax.ShapeDtypeStruct((8, LANES), F32),
+                jax.ShapeDtypeStruct((1, LANES), F32),
             ),
             vmem_mb=16,
         ),
@@ -719,27 +735,46 @@
     )(table, parts, squares)
 
 
-def share_kernel(arrived, after, send, sums):
+def share_kernel(arrived, send, sums):
     whole = arrived[...].astype(F32)
-    send[...] = whole[:, 8:16, :].reshape(NY * NZ // 2, 16, LANES).astype(BF16)
+    for i in range(NY * NZ // 2):
+        pair = [whole[2 * i + j, 8:16, :] for j in range(2)]
+        send[i] = jnp.concatenate(pair, 0).astype(BF16)
     tails = jnp.sum(jnp.sum(whole[:, 16:24, :], axis=0), axis=0, keepdims=True)
-    sums[...] = jnp.broadcast_to(jnp.sum(tails, axis=1, keepdims=True), (1, LANES))
-
-
-def share(arrived, after):
+    value = jnp.broadcast_to(tails, (8, LANES))
+    sums[...] = value
+    send[NY * NZ // 2] = split_rows(value, 16).astype(BF16)
+
+
+def share(arrived):
     return pl.pallas_call(
         share_kernel,
-        in_specs=[in_vmem(), pl.BlockSpec(memory_space=pl.ANY)],
+        in_specs=[in_vmem()],
         out_specs=(in_vmem(),) * 2,
         **call(
             share_kernel,
             (
-                jax.ShapeDtypeStruct((NY * NZ // 2, 16, LANES), BF16),
-                jax.ShapeDtypeStruct((1, LANES), F32),
+                jax.ShapeDtypeStruct((NY * NZ // 2 + 1, 16, LANES), BF16),
+                jax.ShapeDtypeStruct((8, LANES), F32),
             ),
         ),
         name="share",
-    )(arrived, after)
+    )(arrived)
+
+
+def tally_kernel(mine, got, sums):
+    tails = mine[0:1, :] + jnp.sum(got[NY * NZ // 2].astype(F32), axis=0, keepdims=True)
+    sums[...] = jnp.broadcast_to(jnp.sum(tails, axis=1, keepdims=True), (1, LANES))
+
+
+def tally(mine, got):
+    return pl.pallas_call(
+        tally_kernel,
+        in_specs=[in_vmem()] * 2,
+        out_specs=in_vmem(),
+        **call(tally_kernel, jax.ShapeDtypeStruct((1, LANES), F32)),
+        name="tally",
+    )(mine, got)
 
 
 def finish_kernel(table, arrived, got, own, own_far, key_grad, value_grad, token):
@@ -801,21 +836,21 @@
     dq_0, back_0[0] = last_0(after)
     dq_1, back_1[0] = last_1(dq_0)
     near, far, squares = emit(table, (dq_0, dq_1), (own_0, own_1))
-    far = other_core(far)
-    query_grad, done = assemble(near, far)
     (acc,) = combine_more((0,), 0, table, [back_0[0]], acc, squares)
     (acc,) = combine_more((1, 0), 1, table, [back_1[1], back_1[0]], acc, squares)
     (acc,) = combine_more((2,), 1, table, [back_1[2]], acc, squares)
     (acc,) = combine_more((3,), 1, table, [back_1[3]], acc, squares)
     halves = leave(acc)
     arrived = swap_yz(route(table, swap_z(halves), squares))
-    shared, mine_sum = share(arrived, done)
-    all_sum = mine_sum
+    shared, mine_sum = share(arrived)
+    shared = other_core(shared)
+    mine_sum = tally(mine_sum, shared)
+    far = other_core(ship(far, mine_sum))
+    query_grad, done = assemble(near, far)
+    key_grad, value_grad, token = finish(table, arrived, shared, own_0, far)
+    all_sum = mine_sum + (done + token)
     for k in (1, 2, 3):
         all_sum = all_sum + along_head(mine_sum, k)
-    shared = other_core(shared)
-    key_grad, value_grad, token = finish(table, arrived, shared, own_0, far)
-    all_sum = all_sum + (other_core(all_sum) + token)
     count = float(NBLK * TOK * NHEAD * (KV * RATIO + 2 * KV) * HD)
     grad_rms = jnp.sqrt(all_sum[0, 0] / count)
     return query_grad, key_grad, value_grad, grad_rms

time: 121 us -> 117 us (0.967); the launches traced: 119 us -> 116 us
  blocking collectives: 14.3 us -> 42.4 us
  waiting for transfers between devices: 41.7 us -> 22.5 us
  starting transfers between devices: 42.2 us -> 31.8 us
    all_to_all x0 -> x1, blocking collectives: none -> 15 us  [swap_yz(): lax.all_to_all(x, 'branch', 0, 0, axis_index_groups=groups, tiled=False)]
    all_to_all x1 -> x2, blocking collectives: 14.3 us -> 27.4 us  [swap_z(): lax.all_to_all(x, 'branch', 0, 0, axis_index_groups=groups, tiled=False)]
    all_to_all x2 -> x1, waiting for transfers between devices: 20.4 us -> 10.9 us  [swap_yz(): lax.all_to_all(x, 'branch', 0, 0, axis_index_groups=groups, tiled=False)]
    all_to_all x1 -> x0, waiting for transfers between devices: 8.69 us -> none  [swap_z(): lax.all_to_all(x, 'branch', 0, 0, axis_index_groups=groups, tiled=False)]
    all_to_all x1 -> x0, starting transfers between devices: 5.34 us -> none  [swap_z(): lax.all_to_all(x, 'branch', 0, 0, axis_index_groups=groups, tiled=False)]
    all_to_all x2 -> x1, starting transfers between devices: 16.7 us -> 11.4 us  [swap_yz(): lax.all_to_all(x, 'branch', 0, 0, axis_index_groups=groups, tiled=False)]
    ppermute x3, waiting for transfers between devices: 3.86 us -> 1.89 us  [along_head(): return lax.ppermute(x, 'head', pairs)]
    ppermute x5 -> x4, waiting for transfers between devices: 1.47 us -> 2.47 us  [other_core(): return lax.ppermute(x, 'branch', pairs)]
  transfers between devices with their start and end apart: 23 -> 20, of which waited for: 10 -> 8; matrix products, arithmetic and copies ran while one was open for 0% -> 0% of each run, Pallas kernels for 11% -> 11%
where the time goes in v6:
time: 117 us; the launch traced here: 116 us
  blocking collectives  42.4 us (36%)
  starting transfers between devices  31.8 us (27%)
  waiting for transfers between devices  22.5 us (19%)
  Pallas kernels  15.9 us (14%)
  between operations  3.53 us (3%)
    all_to_all x2, blocking collectives, swap_z(): lax.all_to_all(x, 'branch', 0, 0, axis_index_groups=groups, tiled=False)  27.4 us
    ppermute x12, starting transfers between devices, along_y(): return lax.ppermute(x, 'branch', pairs)  15.5 us
    all_to_all x1, blocking collectives, swap_yz(): lax.all_to_all(x, 'branch', 0, 0, axis_index_groups=groups, tiled=False)  15 us
    all_to_all x1, starting transfers between devices, swap_yz(): lax.all_to_all(x, 'branch', 0, 0, axis_index_groups=groups, tiled=False)  11.4 us
    all_to_all x1, waiting for transfers between devices, swap_yz(): lax.all_to_all(x, 'branch', 0, 0, axis_index_groups=groups, tiled=False)  10.9 us
    ppermute x12, waiting for transfers between devices, along_y(): return lax.ppermute(x, 'branch', pairs)  7.2 us
    pallas_call x8, Pallas kernels, grads_of(): pl.pallas_call(functools.partial(body, k, h), in_specs=[in_vmem()] * len(...  5.09 us
    ppermute x3, starting transfers between devices, along_head(): return lax.ppermute(x, 'head', pairs)  4.47 us
  transfers between devices with their start and end apart: 20, of which 8 were waited for; matrix products, arithmetic and copies ran while one was open for 0% of the time, Pallas kernels for 11%

profile of v6, /device:TPU:32, one launch (start us, length us, event | category | flops | bytes accessed | tf_op | source)
XLA Modules:
  0.0 116.5 jit_solution(6600827351523981430)
XLA Ops:
  2.0 2.2 %packet.1 = (bf16[32,24,128]{2,1,0:T(8,128)(2,1)}, bf16[4,128,128]{2,1,0:T(8,128)(2,1)}) custom-call(bf16[128,2,128]{2,1,0:T(2,128)(2,1)} %keys_far.1, bf16[128,2,128]{2,1,0:T(2,128)(2,1)} %values_far.1, s32[1,8]{1,0:T(1,128)} %ancestors_far.1, s32[1]{0:T(128)S(6)} %copy.25.group, bf16[1]{0:T(256)(128)(2,1)S(6)} %copy.24.reward), custom_call_target="tpu_custom_call" | custom-call | tf_op jit(solution)/shard_map/packet/pallas_call | solution.py:136
  4.2 11.4 %all-to-all-start = ((bf16[32,24,128]{2,1,0:T(8,128)(2,1)}), bf16[32,24,128]{2,1,0:T(8,128)(2,1)S(1)}, u32[]{:S(2)}, u32[]{:S(2)}) async-start(bf16[32,24,128]{2,1,0:T(8,128)(2,1)} %get-tuple-element.82), calls=%async_computation | async-start | bytes 393216 | tf_op jit(solution)/shard_map/all_to_all | solution.py:64
  15.6 10.9 %all-to-all-done.mine = bf16[32,24,128]{2,1,0:T(8,128)(2,1)S(1)} async-done(((bf16[32,24,128]{2,1,0:T(8,128)(2,1)}), bf16[32,24,128]{2,1,0:T(8,128)(2,1)S(1)}, u32[]{:S(2)}, u32[]{:S(2)}) %all-to-all-start) | async-done | bytes 196640 | tf_op jit(solution)/shard_map/all_to_all | solution.py:64
  26.8 1.2 %collective-permute-done.other = bf16[32,24,128]{2,1,0:T(8,128)(2,1)S(1)} collective-permute-done((bf16[32,24,128]{2,1,0:T(8,128)(2,1)S(1)}, bf16[32,24,128]{2,1,0:T(8,128)(2,1)S(1)}, u32[]{:S(2)}, u32[]{:S(2)}) %collective-permute-start) | collective-permute-done | bytes 196640 | tf_op jit(solution)/shard_map/ppermute | solution.py:49
  28.8 14.3 %all_to_all.20.column = bf16[8,8,16,128]{3,2,1,0:T(8,128)(2,1)S(1)} all-to-all(bf16[8,8,16,128]{3,2,1,0:T(8,128)(2,1)S(1)} %get-tuple-element.90), channel_id=1, replica_groups={{0,8,16,24,32,40,48,56},{4,12,20,28,36,44,52,60},{64,72,80,88,96,104,11..., dimensions={0} | all-to-all | bytes 524288 | tf_op jit(solution)/shard_map/all_to_all | solution.py:59
  43.9 2.0 %collective-permute-start.3 = (bf16[8,4,16,128]{3,2,1,0:T(8,128)(2,1)S(1)}, bf16[8,4,16,128]{3,2,1,0:T(8,128)(2,1)S(1)}, u32[]{:S(2)}, u32[]{:S(2)}) collective-permute-start(bf16[8,4,16,128]{3,2,1,0:T(8,128)(2,1)S(1)} %get-tuple-element.96), channel_id=1, source_target_pairs={{0,128},{4,132},{8,136},{12,140},{16,144},{20,148},{24,152},{28,15... | collective-permute-start | bytes 393224 | tf_op jit(solution)/shard_map/ppermute | solution.py:44
  45.9 1.3 %collective-permute-start.4 = (bf16[8,4,16,128]{3,2,1,0:T(8,128)(2,1)S(1)}, bf16[8,4,16,128]{3,2,1,0:T(8,128)(2,1)S(1)}, u32[]{:S(2)}, u32[]{:S(2)}) collective-permute-start(bf16[8,4,16,128]{3,2,1,0:T(8,128)(2,1)S(1)} %get-tuple-element.98), channel_id=1, source_target_pairs={{0,192},{4,196},{8,200},{12,204},{16,208},{20,212},{24,216},{28,22... | collective-permute-start | bytes 393224 | tf_op jit(solution)/shard_map/ppermute | solution.py:44
  48.2 1.6 %collective-permute-start.6 = (bf16[8,4,16,128]{3,2,1,0:T(8,128)(2,1)S(1)}, bf16[8,4,16,128]{3,2,1,0:T(8,128)(2,1)S(1)}, u32[]{:S(2)}, u32[]{:S(2)}) collective-permute-start(bf16[8,4,16,128]{3,2,1,0:T(8,128)(2,1)S(1)} %get-tuple-element.118), channel_id=1, source_target_pairs={{0,128},{4,132},{8,136},{12,140},{16,144},{20,148},{24,152},{28,15... | collective-permute-start | bytes 393224 | tf_op jit(solution)/shard_map/ppermute | solution.py:44
  50.6 2.8 %collective-permute-done.2.part = bf16[8,4,16,128]{3,2,1,0:T(8,128)(2,1)S(1)} collective-permute-done((bf16[8,4,16,128]{3,2,1,0:T(8,128)(2,1)S(1)}, bf16[8,4,16,128]{3,2,1,0:T(8,128)(2,1)S(1)}, u32[]{:S(2)}, u32[]{:S(2)}) %collective-permute-start.2) | collective-permute-done | bytes 131104 | tf_op jit(solution)/shard_map/ppermute | solution.py:44
  55.0 0.8 grads_first.2
  56.5 2.6 %collective-permute-start.8 = (bf16[8,4,16,128]{3,2,1,0:T(8,128)(2,1)S(1)}, bf16[8,4,16,128]{3,2,1,0:T(8,128)(2,1)S(1)}, u32[]{:S(2)}, u32[]{:S(2)}) collective-permute-start(bf16[8,4,16,128]{3,2,1,0:T(8,128)(2,1)S(1)} %get-tuple-element.132), channel_id=1, source_target_pairs={{0,192},{4,196},{8,200},{12,204},{16,208},{20,212},{24,216},{28,22... | collective-permute-start | bytes 393224 | tf_op jit(solution)/shard_map/ppermute | solution.py:44
  59.1 1.5 %collective-permute-start.9 = (bf16[8,4,16,128]{3,2,1,0:T(8,128)(2,1)S(1)}, bf16[8,4,16,128]{3,2,1,0:T(8,128)(2,1)S(1)}, u32[]{:S(2)}, u32[]{:S(2)}) collective-permute-start(bf16[8,4,16,128]{3,2,1,0:T(8,128)(2,1)S(1)} %get-tuple-element.133), channel_id=1, source_target_pairs={{0,128},{4,132},{8,136},{12,140},{16,144},{20,148},{24,152},{28,15... | collective-permute-start | bytes 393224 | tf_op jit(solution)/shard_map/ppermute | solution.py:44
  63.5 0.8 grads_first.3
  64.4 2.4 %collective-permute-start.12 = (bf16[8,4,16,128]{3,2,1,0:T(8,128)(2,1)S(1)}, bf16[8,4,16,128]{3,2,1,0:T(8,128)(2,1)S(1)}, u32[]{:S(2)}, u32[]{:S(2)}) collective-permute-start(bf16[8,4,16,128]{3,2,1,0:T(8,128)(2,1)S(1)} %get-tuple-element.147), channel_id=1, source_target_pairs={{0,128},{4,132},{8,136},{12,140},{16,144},{20,148},{24,152},{28,15... | collective-permute-start | bytes 393224 | tf_op jit(solution)/shard_map/ppermute | solution.py:44
  67.5 2.4 %collective-permute-start.13 = (bf16[8,4,16,128]{3,2,1,0:T(8,128)(2,1)S(1)}, bf16[8,4,16,128]{3,2,1,0:T(8,128)(2,1)S(1)}, u32[]{:S(2)}, u32[]{:S(2)}) collective-permute-start(bf16[8,4,16,128]{3,2,1,0:T(8,128)(2,1)S(1)} %get-tuple-element.148), channel_id=1, source_target_pairs={{0,192},{4,196},{8,200},{12,204},{16,208},{20,212},{24,216},{28,22... | collective-permute-start | bytes 393224 | tf_op jit(solution)/shard_map/ppermute | solution.py:44
  73.1 3.7 %collective-permute-done.11.refs_0_ = bf16[8,4,16,128]{3,2,1,0:T(8,128)(2,1)S(1)} collective-permute-done((bf16[8,4,16,128]{3,2,1,0:T(8,128)(2,1)S(1)}, bf16[8,4,16,128]{3,2,1,0:T(8,128)(2,1)S(1)}, u32[]{:S(2)}, u32[]{:S(2)}) %collective-permute-start.11) | collective-permute-done | bytes 131104 | tf_op jit(solution)/shard_map/ppermute | solution.py:44
  77.0 13.1 %all_to_all.21.parts = bf16[8,8,16,128]{3,2,1,0:T(8,128)(2,1)S(1)} all-to-all(bf16[8,8,16,128]{3,2,1,0:T(8,128)(2,1)S(1)} %leave.1), channel_id=1, replica_groups={{0,8,16,24,32,40,48,56},{4,12,20,28,36,44,52,60},{64,72,80,88,96,104,11..., dimensions={0} | all-to-all | bytes 524288 | tf_op jit(solution)/shard_map/all_to_all | solution.py:59
  90.2 15.0 %all_to_all.22.arrived = bf16[32,24,128]{2,1,0:T(8,128)(2,1)S(1)} all-to-all(bf16[32,24,128]{2,1,0:T(8,128)(2,1)S(1)} %route.1), channel_id=1, replica_groups={{0,8,16,24,32,40,48,56,64,72,80,88,96,104,112,120,128,136,144,152,160,1..., dimensions={0} | all-to-all | bytes 393216 | tf_op jit(solution)/shard_map/all_to_all | solution.py:64
  105.4 1.2 %collective-permute-done.14.got = bf16[17,16,128]{2,1,0:T(8,128)(2,1)S(1)} collective-permute-done((bf16[17,16,128]{2,1,0:T(8,128)(2,1)S(1)}, bf16[17,16,128]{2,1,0:T(8,128)(2,1)S(1)}, u32[]{:S(2)}, u32[]{:S(2)}) %collective-permute-start.14) | collective-permute-done | bytes 69664 | tf_op jit(solution)/shard_map/ppermute | solution.py:49
  106.9 2.8 %collective-permute-start.18 = (f32[1,128]{1,0:T(1,128)S(1)}, f32[1,128]{1,0:T(1,128)S(1)}, u32[]{:S(2)}, u32[]{:S(2)}) collective-permute-start(f32[1,128]{1,0:T(1,128)S(1)} %tally.1.after), channel_id=1, source_target_pairs={{0,3},{1,0},{2,1},{3,2},{4,7},{5,4},{6,5},{7,6},{8,11},{9,8},{10,9... | collective-permute-start | bytes 1544 | tf_op jit(solution)/shard_map/ppermute | solution.py:54
  110.5 0.9 collective-permute-start.16
  111.4 0.9 finish.1
  112.2 1.1 assemble.1
  113.4 1.4 %collective-permute-done.17 = f32[1,128]{1,0:T(1,128)S(1)} collective-permute-done((f32[1,128]{1,0:T(1,128)S(1)}, f32[1,128]{1,0:T(1,128)S(1)}, u32[]{:S(2)}, u32[]{:S(2)}) %collective-permute-start.17) | collective-permute-done | bytes 544 | tf_op jit(solution)/shard_map/ppermute | solution.py:54
  (66 shorter events, 14.5 us)
Async XLA Ops:
  0.6 25.9 %copy-start.2 = (bf16[128,16,128]{2,1,0:T(8,128)(2,1)S(1)}, bf16[128,16,128]{2,1,0:T(8,128)(2,1)}, u32[]{:S(2)}) copy-start(bf16[128,16,128]{2,1,0:T(8,128)(2,1)} %param.11) | copy-start | bytes 1572868
  4.2 11.4 %copy-start.3 = (s32[1,128]{1,0:T(1,128)S(1)}, s32[1,128]{1,0:T(1,128)}, u32[]{:S(2)}) copy-start(s32[1,128]{1,0:T(1,128)} %param.15) | copy-start | bytes 1540
  4.2 22.4 %all-to-all-start = ((bf16[32,24,128]{2,1,0:T(8,128)(2,1)}), bf16[32,24,128]{2,1,0:T(8,128)(2,1)S(1)}, u32[]{:S(2)}, u32[]{:S(2)}) async-start(bf16[32,24,128]{2,1,0:T(8,128)(2,1)} %get-tuple-element.82), calls=%async_computation | async-start | bytes 393216 | tf_op jit(solution)/shard_map/all_to_all | solution.py:64
  15.6 12.8 %copy-start = (bf16[128,16,128]{2,1,0:T(8,128)(2,1)S(1)}, bf16[128,16,128]{2,1,0:T(8,128)(2,1)}, u32[]{:S(2)}) copy-start(bf16[128,16,128]{2,1,0:T(8,128)(2,1)} %queries.1) | copy-start | bytes 1572868
  26.5 1.4 %collective-permute-start = (bf16[32,24,128]{2,1,0:T(8,128)(2,1)S(1)}, bf16[32,24,128]{2,1,0:T(8,128)(2,1)S(1)}, u32[]{:S(2)}, u32[]{:S(2)}) collective-permute-start(bf16[32,24,128]{2,1,0:T(8,128)(2,1)S(1)} %all-to-all-done.mine), channel_id=1, source_target_pairs={{0,4},{4,0},{8,12},{12,8},{16,20},{20,16},{24,28},{28,24},{32,36},... | collective-permute-start | bytes 589832 | tf_op jit(solution)/shard_map/ppermute | solution.py:49
  26.8 1.6 %copy-start.1 = (bf16[4,128,128]{2,1,0:T(8,128)(2,1)S(1)}, bf16[4,128,128]{2,1,0:T(8,128)(2,1)}, u32[]{:S(2)}) copy-start(bf16[4,128,128]{2,1,0:T(8,128)(2,1)} %get-tuple-element.85.own_kv) | copy-start | bytes 393220
  28.5 19.7 %collective-permute-start.1 = (bf16[2304,128]{1,0:T(8,128)(2,1)S(1)}, bf16[2304,128]{1,0:T(8,128)(2,1)S(1)}, u32[]{:S(2)}, u32[]{:S(2)}) collective-permute-start(bf16[2304,128]{1,0:T(8,128)(2,1)S(1)} %get-tuple-element.87), channel_id=1, source_target_pairs={{0,4},{4,0},{8,12},{12,8},{16,20},{20,16},{24,28},{28,24},{32,36},... | collective-permute-start | bytes 1769480 | tf_op jit(solution)/shard_map/ppermute | solution.py:49
  43.2 10.2 %collective-permute-start.2 = (bf16[8,4,16,128]{3,2,1,0:T(8,128)(2,1)S(1)}, bf16[8,4,16,128]{3,2,1,0:T(8,128)(2,1)S(1)}, u32[]{:S(2)}, u32[]{:S(2)}) collective-permute-start(bf16[8,4,16,128]{3,2,1,0:T(8,128)(2,1)S(1)} %get-tuple-element.94), channel_id=1, source_target_pairs={{0,64},{4,68},{8,72},{12,76},{16,80},{20,84},{24,88},{28,92},{32,9... | collective-permute-start | bytes 393224 | tf_op jit(solution)/shard_map/ppermute | solution.py:44
  43.9 10.1 %collective-permute-start.3 = (bf16[8,4,16,128]{3,2,1,0:T(8,128)(2,1)S(1)}, bf16[8,4,16,128]{3,2,1,0:T(8,128)(2,1)S(1)}, u32[]{:S(2)}, u32[]{:S(2)}) collective-permute-start(bf16[8,4,16,128]{3,2,1,0:T(8,128)(2,1)S(1)} %get-tuple-element.96), channel_id=1, source_target_pairs={{0,128},{4,132},{8,136},{12,140},{16,144},{20,148},{24,152},{28,15... | collective-permute-start | bytes 393224 | tf_op jit(solution)/shard_map/ppermute | solution.py:44
  45.9 8.6 %collective-permute-start.4 = (bf16[8,4,16,128]{3,2,1,0:T(8,128)(2,1)S(1)}, bf16[8,4,16,128]{3,2,1,0:T(8,128)(2,1)S(1)}, u32[]{:S(2)}, u32[]{:S(2)}) collective-permute-start(bf16[8,4,16,128]{3,2,1,0:T(8,128)(2,1)S(1)} %get-tuple-element.98), channel_id=1, source_target_pairs={{0,192},{4,196},{8,200},{12,204},{16,208},{20,212},{24,216},{28,22... | collective-permute-start | bytes 393224 | tf_op jit(solution)/shard_map/ppermute | solution.py:44
  47.4 13.7 %collective-permute-start.5 = (bf16[8,4,16,128]{3,2,1,0:T(8,128)(2,1)S(1)}, bf16[8,4,16,128]{3,2,1,0:T(8,128)(2,1)S(1)}, u32[]{:S(2)}, u32[]{:S(2)}) collective-permute-start(bf16[8,4,16,128]{3,2,1,0:T(8,128)(2,1)S(1)} %get-tuple-element.116), channel_id=1, source_target_pairs={{0,64},{4,68},{8,72},{12,76},{16,80},{20,84},{24,88},{28,92},{32,9... | collective-permute-start | bytes 393224 | tf_op jit(solution)/shard_map/ppermute | solution.py:44
  48.2 13.6 %collective-permute-start.6 = (bf16[8,4,16,128]{3,2,1,0:T(8,128)(2,1)S(1)}, bf16[8,4,16,128]{3,2,1,0:T(8,128)(2,1)S(1)}, u32[]{:S(2)}, u32[]{:S(2)}) collective-permute-start(bf16[8,4,16,128]{3,2,1,0:T(8,128)(2,1)S(1)} %get-tuple-element.118), channel_id=1, source_target_pairs={{0,128},{4,132},{8,136},{12,140},{16,144},{20,148},{24,152},{28,15... | collective-permute-start | bytes 393224 | tf_op jit(solution)/shard_map/ppermute | solution.py:44
  53.5 8.8 %collective-permute-start.7 = (bf16[8,4,16,128]{3,2,1,0:T(8,128)(2,1)S(1)}, bf16[8,4,16,128]{3,2,1,0:T(8,128)(2,1)S(1)}, u32[]{:S(2)}, u32[]{:S(2)}) collective-permute-start(bf16[8,4,16,128]{3,2,1,0:T(8,128)(2,1)S(1)} %get-tuple-element.120), channel_id=1, source_target_pairs={{0,192},{4,196},{8,200},{12,204},{16,208},{20,212},{24,216},{28,22... | collective-permute-start | bytes 393224 | tf_op jit(solution)/shard_map/ppermute | solution.py:44
  56.5 10.3 %collective-permute-start.8 = (bf16[8,4,16,128]{3,2,1,0:T(8,128)(2,1)S(1)}, bf16[8,4,16,128]{3,2,1,0:T(8,128)(2,1)S(1)}, u32[]{:S(2)}, u32[]{:S(2)}) collective-permute-start(bf16[8,4,16,128]{3,2,1,0:T(8,128)(2,1)S(1)} %get-tuple-element.132), channel_id=1, source_target_pairs={{0,192},{4,196},{8,200},{12,204},{16,208},{20,212},{24,216},{28,22... | collective-permute-start | bytes 393224 | tf_op jit(solution)/shard_map/ppermute | solution.py:44
  59.1 7.7 %collective-permute-start.9 = (bf16[8,4,16,128]{3,2,1,0:T(8,128)(2,1)S(1)}, bf16[8,4,16,128]{3,2,1,0:T(8,128)(2,1)S(1)}, u32[]{:S(2)}, u32[]{:S(2)}) collective-permute-start(bf16[8,4,16,128]{3,2,1,0:T(8,128)(2,1)S(1)} %get-tuple-element.133), channel_id=1, source_target_pairs={{0,128},{4,132},{8,136},{12,140},{16,144},{20,148},{24,152},{28,15... | collective-permute-start | bytes 393224 | tf_op jit(solution)/shard_map/ppermute | solution.py:44
  61.2 8.7 %collective-permute-start.10 = (bf16[8,4,16,128]{3,2,1,0:T(8,128)(2,1)S(1)}, bf16[8,4,16,128]{3,2,1,0:T(8,128)(2,1)S(1)}, u32[]{:S(2)}, u32[]{:S(2)}) collective-permute-start(bf16[8,4,16,128]{3,2,1,0:T(8,128)(2,1)S(1)} %get-tuple-element.136), channel_id=1, source_target_pairs={{0,64},{4,68},{8,72},{12,76},{16,80},{20,84},{24,88},{28,92},{32,9... | collective-permute-start | bytes 393224 | tf_op jit(solution)/shard_map/ppermute | solution.py:44
  64.4 8.6 %collective-permute-start.12 = (bf16[8,4,16,128]{3,2,1,0:T(8,128)(2,1)S(1)}, bf16[8,4,16,128]{3,2,1,0:T(8,128)(2,1)S(1)}, u32[]{:S(2)}, u32[]{:S(2)}) collective-permute-start(bf16[8,4,16,128]{3,2,1,0:T(8,128)(2,1)S(1)} %get-tuple-element.147), channel_id=1, source_target_pairs={{0,128},{4,132},{8,136},{12,140},{16,144},{20,148},{24,152},{28,15... | collective-permute-start | bytes 393224 | tf_op jit(solution)/shard_map/ppermute | solution.py:44
  67.5 5.3 %collective-permute-start.13 = (bf16[8,4,16,128]{3,2,1,0:T(8,128)(2,1)S(1)}, bf16[8,4,16,128]{3,2,1,0:T(8,128)(2,1)S(1)}, u32[]{:S(2)}, u32[]{:S(2)}) collective-permute-start(bf16[8,4,16,128]{3,2,1,0:T(8,128)(2,1)S(1)} %get-tuple-element.148), channel_id=1, source_target_pairs={{0,192},{4,196},{8,200},{12,204},{16,208},{20,212},{24,216},{28,22... | collective-permute-start | bytes 393224 | tf_op jit(solution)/shard_map/ppermute | solution.py:44
  70.6 6.3 %collective-permute-start.11 = (bf16[8,4,16,128]{3,2,1,0:T(8,128)(2,1)S(1)}, bf16[8,4,16,128]{3,2,1,0:T(8,128)(2,1)S(1)}, u32[]{:S(2)}, u32[]{:S(2)}) collective-permute-start(bf16[8,4,16,128]{3,2,1,0:T(8,128)(2,1)S(1)} %get-tuple-element.146), channel_id=1, source_target_pairs={{0,64},{4,68},{8,72},{12,76},{16,80},{20,84},{24,88},{28,92},{32,9... | collective-permute-start | bytes 393224 | tf_op jit(solution)/shard_map/ppermute | solution.py:44
  105.3 1.3 %collective-permute-start.14 = (bf16[17,16,128]{2,1,0:T(8,128)(2,1)S(1)}, bf16[17,16,128]{2,1,0:T(8,128)(2,1)S(1)}, u32[]{:S(2)}, u32[]{:S(2)}) collective-permute-start(bf16[17,16,128]{2,1,0:T(8,128)(2,1)S(1)} %get-tuple-element.154), channel_id=1, source_target_pairs={{0,4},{4,0},{8,12},{12,8},{16,20},{20,16},{24,28},{28,24},{32,36},... | collective-permute-start | bytes 208904 | tf_op jit(solution)/shard_map/ppermute | solution.py:49
  106.7 4.6 %collective-permute-start.15 = (f32[1280,128]{1,0:T(8,128)S(1)}, f32[1280,128]{1,0:T(8,128)S(1)}, u32[]{:S(2)}, u32[]{:S(2)}) collective-permute-start(f32[1280,128]{1,0:T(8,128)S(1)} %ship.1), channel_id=1, source_target_pairs={{0,4},{4,0},{8,12},{12,8},{16,20},{20,16},{24,28},{28,24},{32,36},... | collective-permute-start | bytes 1966088 | tf_op jit(solution)/shard_map/ppermute | solution.py:49
  106.9 6.4 %collective-permute-start.18 = (f32[1,128]{1,0:T(1,128)S(1)}, f32[1,128]{1,0:T(1,128)S(1)}, u32[]{:S(2)}, u32[]{:S(2)}) collective-permute-start(f32[1,128]{1,0:T(1,128)S(1)} %tally.1.after), channel_id=1, source_target_pairs={{0,3},{1,0},{2,1},{3,2},{4,7},{5,4},{6,5},{7,6},{8,11},{9,8},{10,9... | collective-permute-start | bytes 1544 | tf_op jit(solution)/shard_map/ppermute | solution.py:54
  109.7 5.0 %collective-permute-start.17 = (f32[1,128]{1,0:T(1,128)S(1)}, f32[1,128]{1,0:T(1,128)S(1)}, u32[]{:S(2)}, u32[]{:S(2)}) collective-permute-start(f32[1,128]{1,0:T(1,128)S(1)} %tally.1.after), channel_id=1, source_target_pairs={{0,2},{1,3},{2,0},{3,1},{4,6},{5,7},{6,4},{7,5},{8,10},{9,11},{10,... | collective-permute-start | bytes 1544 | tf_op jit(solution)/shard_map/ppermute | solution.py:54
  110.5 4.8 %collective-permute-start.16 = (f32[1,128]{1,0:T(1,128)S(1)}, f32[1,128]{1,0:T(1,128)S(1)}, u32[]{:S(2)}, u32[]{:S(2)}) collective-permute-start(f32[1,128]{1,0:T(1,128)S(1)} %tally.1.after), channel_id=1, source_target_pairs={{0,1},{1,2},{2,3},{3,0},{4,5},{5,6},{6,7},{7,4},{8,9},{9,10},{10,1... | collective-permute-start | bytes 1544 | tf_op jit(solution)/shard_map/ppermute | solution.py:54

commit v7 on v6

--- a/solution.py
+++ b/solution.py
@@ -579,10 +579,9 @@
     )(*arrays)
 
 
-def attend(h, table, q_all, g_all, own_kv, parts, after, hints):
+def attend(h, table, q_all, g_all, own_kv, parts, first, after, hints):
     e, pg, st = [None] * NY, [None] * NY, [None] * NY
-    e[0], pg[0], st[0], own_e, own_pg = first_scores_of(h, table, q_all, g_all, parts[0], own_kv)
-    after = st[0] if after is None else after
+    e[0], pg[0], st[0], own_e, own_pg = first
     for k in (1, 2, 3):
         e[k], pg[k], st[k] = scores_of(h, table, q_all, g_all, parts[k], after)
         after = st[k]
@@ -825,12 +824,15 @@
     for u in range(2):
         dealt = first if u == 0 else deal(u, table, column, first[0])
         parts.append([dealt[0]] + [along_y(dealt[k], k) for k in (1, 2, 3)])
-    after, own_0, sent, last_0 = attend(0, table, q_all, g_all, kv_all, parts[0], None, ())
+    firsts = [first_scores_of(u, table, q_all, g_all, parts[u][0], kv_all) for u in range(2)]
+    after, own_0, sent, last_0 = attend(
+        0, table, q_all, g_all, kv_all, parts[0], firsts[0], firsts[1][2], ()
+    )
     back_0 = [None] + [along_y(sent[k], -k) for k in (1, 2, 3)]
     acc, token = combine_start(table, back_0[1], back_0[2])
     acc, late_token = combine_more((3,), 0, table, [back_0[3]], acc, table, 2)
     after, own_1, sent, last_1 = attend(
-        1, table, q_all, g_all, kv_all, parts[1], after, (token, late_token)
+        1, table, q_all, g_all, kv_all, parts[1], firsts[1], after, (token, late_token)
     )
     back_1 = [None] + [along_y(sent[k], -k) for k in (1, 2, 3)]
     dq_0, back_0[0] = last_0(after)

time: 117 us -> 116 us (level)
  no operation moved by 1% of the time
where the time goes in v7:
time: 116 us
  blocking collectives  42.6 us (37%)
  starting transfers between devices  31.6 us (27%)
  waiting for transfers between devices  22.2 us (19%)
  Pallas kernels  15.9 us (14%)
  between operations  3.52 us (3%)
    all_to_all x2, blocking collectives, swap_z(): lax.all_to_all(x, 'branch', 0, 0, axis_index_groups=groups, tiled=False)  27.6 us
    ppermute x12, starting transfers between devices, along_y(): return lax.ppermute(x, 'branch', pairs)  15.3 us
    all_to_all x1, blocking collectives, swap_yz(): lax.all_to_all(x, 'branch', 0, 0, axis_index_groups=groups, tiled=False)  15 us
    all_to_all x1, starting transfers between devices, swap_yz(): lax.all_to_all(x, 'branch', 0, 0, axis_index_groups=groups, tiled=False)  11.4 us
    all_to_all x1, waiting for transfers between devices, swap_yz(): lax.all_to_all(x, 'branch', 0, 0, axis_index_groups=groups, tiled=False)  10.9 us
    ppermute x12, waiting for transfers between devices, along_y(): return lax.ppermute(x, 'branch', pairs)  6.85 us
    pallas_call x8, Pallas kernels, grads_of(): pl.pallas_call(functools.partial(body, k, h), in_specs=[in_vmem()] * len(...  5.09 us
    ppermute x3, starting transfers between devices, along_head(): return lax.ppermute(x, 'head', pairs)  4.45 us
  transfers between devices with their start and end apart: 20, of which 8 were waited for; matrix products, arithmetic and copies ran while one was open for 0% of the time, Pallas kernels for 11%

profile of v7, /device:TPU:32, one launch (start us, length us, event | category | flops | bytes accessed | tf_op | source)
XLA Modules:
  0.0 116.1 jit_solution(17654178455578785351)
XLA Ops:
  2.0 2.2 %packet.1 = (bf16[32,24,128]{2,1,0:T(8,128)(2,1)}, bf16[4,128,128]{2,1,0:T(8,128)(2,1)}) custom-call(bf16[128,2,128]{2,1,0:T(2,128)(2,1)} %keys_far.1, bf16[128,2,128]{2,1,0:T(2,128)(2,1)} %values_far.1, s32[1,8]{1,0:T(1,128)} %ancestors_far.1, s32[1]{0:T(128)S(6)} %copy.25.group, bf16[1]{0:T(256)(128)(2,1)S(6)} %copy.24.reward), custom_call_target="tpu_custom_call" | custom-call | tf_op jit(solution)/shard_map/packet/pallas_call | solution.py:136
  4.2 11.4 %all-to-all-start = ((bf16[32,24,128]{2,1,0:T(8,128)(2,1)}), bf16[32,24,128]{2,1,0:T(8,128)(2,1)S(1)}, u32[]{:S(2)}, u32[]{:S(2)}) async-start(bf16[32,24,128]{2,1,0:T(8,128)(2,1)} %get-tuple-element.82), calls=%async_computation | async-start | bytes 393216 | tf_op jit(solution)/shard_map/all_to_all | solution.py:64
  15.6 10.9 %all-to-all-done.mine = bf16[32,24,128]{2,1,0:T(8,128)(2,1)S(1)} async-done(((bf16[32,24,128]{2,1,0:T(8,128)(2,1)}), bf16[32,24,128]{2,1,0:T(8,128)(2,1)S(1)}, u32[]{:S(2)}, u32[]{:S(2)}) %all-to-all-start) | async-done | bytes 196640 | tf_op jit(solution)/shard_map/all_to_all | solution.py:64
  26.8 1.2 %collective-permute-done.other = bf16[32,24,128]{2,1,0:T(8,128)(2,1)S(1)} collective-permute-done((bf16[32,24,128]{2,1,0:T(8,128)(2,1)S(1)}, bf16[32,24,128]{2,1,0:T(8,128)(2,1)S(1)}, u32[]{:S(2)}, u32[]{:S(2)}) %collective-permute-start) | collective-permute-done | bytes 196640 | tf_op jit(solution)/shard_map/ppermute | solution.py:49
  28.8 14.3 %all_to_all.20.column = bf16[8,8,16,128]{3,2,1,0:T(8,128)(2,1)S(1)} all-to-all(bf16[8,8,16,128]{3,2,1,0:T(8,128)(2,1)S(1)} %get-tuple-element.90), channel_id=1, replica_groups={{0,8,16,24,32,40,48,56},{4,12,20,28,36,44,52,60},{64,72,80,88,96,104,11..., dimensions={0} | all-to-all | bytes 524288 | tf_op jit(solution)/shard_map/all_to_all | solution.py:59
  43.9 2.0 %collective-permute-start.3 = (bf16[8,4,16,128]{3,2,1,0:T(8,128)(2,1)S(1)}, bf16[8,4,16,128]{3,2,1,0:T(8,128)(2,1)S(1)}, u32[]{:S(2)}, u32[]{:S(2)}) collective-permute-start(bf16[8,4,16,128]{3,2,1,0:T(8,128)(2,1)S(1)} %get-tuple-element.98), channel_id=1, source_target_pairs={{0,128},{4,132},{8,136},{12,140},{16,144},{20,148},{24,152},{28,15... | collective-permute-start | bytes 393224 | tf_op jit(solution)/shard_map/ppermute | solution.py:44
  45.9 1.3 %collective-permute-start.4 = (bf16[8,4,16,128]{3,2,1,0:T(8,128)(2,1)S(1)}, bf16[8,4,16,128]{3,2,1,0:T(8,128)(2,1)S(1)}, u32[]{:S(2)}, u32[]{:S(2)}) collective-permute-start(bf16[8,4,16,128]{3,2,1,0:T(8,128)(2,1)S(1)} %get-tuple-element.100), channel_id=1, source_target_pairs={{0,192},{4,196},{8,200},{12,204},{16,208},{20,212},{24,216},{28,22... | collective-permute-start | bytes 393224 | tf_op jit(solution)/shard_map/ppermute | solution.py:44
  48.2 1.6 %collective-permute-start.6 = (bf16[8,4,16,128]{3,2,1,0:T(8,128)(2,1)S(1)}, bf16[8,4,16,128]{3,2,1,0:T(8,128)(2,1)S(1)}, u32[]{:S(2)}, u32[]{:S(2)}) collective-permute-start(bf16[8,4,16,128]{3,2,1,0:T(8,128)(2,1)S(1)} %get-tuple-element.118), channel_id=1, source_target_pairs={{0,128},{4,132},{8,136},{12,140},{16,144},{20,148},{24,152},{28,15... | collective-permute-start | bytes 393224 | tf_op jit(solution)/shard_map/ppermute | solution.py:44
  50.6 2.8 %collective-permute-done.2.part = bf16[8,4,16,128]{3,2,1,0:T(8,128)(2,1)S(1)} collective-permute-done((bf16[8,4,16,128]{3,2,1,0:T(8,128)(2,1)S(1)}, bf16[8,4,16,128]{3,2,1,0:T(8,128)(2,1)S(1)}, u32[]{:S(2)}, u32[]{:S(2)}) %collective-permute-start.2) | collective-permute-done | bytes 131104 | tf_op jit(solution)/shard_map/ppermute | solution.py:44
  57.1 2.1 %collective-permute-start.8 = (bf16[8,4,16,128]{3,2,1,0:T(8,128)(2,1)S(1)}, bf16[8,4,16,128]{3,2,1,0:T(8,128)(2,1)S(1)}, u32[]{:S(2)}, u32[]{:S(2)}) collective-permute-start(bf16[8,4,16,128]{3,2,1,0:T(8,128)(2,1)S(1)} %get-tuple-element.132), channel_id=1, source_target_pairs={{0,192},{4,196},{8,200},{12,204},{16,208},{20,212},{24,216},{28,22... | collective-permute-start | bytes 393224 | tf_op jit(solution)/shard_map/ppermute | solution.py:44
  59.2 2.2 %collective-permute-start.9 = (bf16[8,4,16,128]{3,2,1,0:T(8,128)(2,1)S(1)}, bf16[8,4,16,128]{3,2,1,0:T(8,128)(2,1)S(1)}, u32[]{:S(2)}, u32[]{:S(2)}) collective-permute-start(bf16[8,4,16,128]{3,2,1,0:T(8,128)(2,1)S(1)} %get-tuple-element.133), channel_id=1, source_target_pairs={{0,128},{4,132},{8,136},{12,140},{16,144},{20,148},{24,152},{28,15... | collective-permute-start | bytes 393224 | tf_op jit(solution)/shard_map/ppermute | solution.py:44
  64.5 2.2 %collective-permute-start.12 = (bf16[8,4,16,128]{3,2,1,0:T(8,128)(2,1)S(1)}, bf16[8,4,16,128]{3,2,1,0:T(8,128)(2,1)S(1)}, u32[]{:S(2)}, u32[]{:S(2)}) collective-permute-start(bf16[8,4,16,128]{3,2,1,0:T(8,128)(2,1)S(1)} %get-tuple-element.147), channel_id=1, source_target_pairs={{0,128},{4,132},{8,136},{12,140},{16,144},{20,148},{24,152},{28,15... | collective-permute-start | bytes 393224 | tf_op jit(solution)/shard_map/ppermute | solution.py:44
  67.5 1.9 %collective-permute-start.13 = (bf16[8,4,16,128]{3,2,1,0:T(8,128)(2,1)S(1)}, bf16[8,4,16,128]{3,2,1,0:T(8,128)(2,1)S(1)}, u32[]{:S(2)}, u32[]{:S(2)}) collective-permute-start(bf16[8,4,16,128]{3,2,1,0:T(8,128)(2,1)S(1)} %get-tuple-element.148), channel_id=1, source_target_pairs={{0,192},{4,196},{8,200},{12,204},{16,208},{20,212},{24,216},{28,22... | collective-permute-start | bytes 393224 | tf_op jit(solution)/shard_map/ppermute | solution.py:44
  72.1 1.0 collective-permute-done.13.refs_0_
  73.3 3.0 %collective-permute-done.11.refs_0_ = bf16[8,4,16,128]{3,2,1,0:T(8,128)(2,1)S(1)} collective-permute-done((bf16[8,4,16,128]{3,2,1,0:T(8,128)(2,1)S(1)}, bf16[8,4,16,128]{3,2,1,0:T(8,128)(2,1)S(1)}, u32[]{:S(2)}, u32[]{:S(2)}) %collective-permute-start.11) | collective-permute-done | bytes 131104 | tf_op jit(solution)/shard_map/ppermute | solution.py:44
  76.4 13.3 %all_to_all.21.parts = bf16[8,8,16,128]{3,2,1,0:T(8,128)(2,1)S(1)} all-to-all(bf16[8,8,16,128]{3,2,1,0:T(8,128)(2,1)S(1)} %leave.1), channel_id=1, replica_groups={{0,8,16,24,32,40,48,56},{4,12,20,28,36,44,52,60},{64,72,80,88,96,104,11..., dimensions={0} | all-to-all | bytes 524288 | tf_op jit(solution)/shard_map/all_to_all | solution.py:59
  89.9 15.0 %all_to_all.22.arrived = bf16[32,24,128]{2,1,0:T(8,128)(2,1)S(1)} all-to-all(bf16[32,24,128]{2,1,0:T(8,128)(2,1)S(1)} %route.1), channel_id=1, replica_groups={{0,8,16,24,32,40,48,56,64,72,80,88,96,104,112,120,128,136,144,152,160,1..., dimensions={0} | all-to-all | bytes 393216 | tf_op jit(solution)/shard_map/all_to_all | solution.py:64
  105.0 1.2 %collective-permute-done.14.got = bf16[17,16,128]{2,1,0:T(8,128)(2,1)S(1)} collective-permute-done((bf16[17,16,128]{2,1,0:T(8,128)(2,1)S(1)}, bf16[17,16,128]{2,1,0:T(8,128)(2,1)S(1)}, u32[]{:S(2)}, u32[]{:S(2)}) %collective-permute-start.14) | collective-permute-done | bytes 69664 | tf_op jit(solution)/shard_map/ppermute | solution.py:49
  106.6 2.8 %collective-permute-start.18 = (f32[1,128]{1,0:T(1,128)S(1)}, f32[1,128]{1,0:T(1,128)S(1)}, u32[]{:S(2)}, u32[]{:S(2)}) collective-permute-start(f32[1,128]{1,0:T(1,128)S(1)} %tally.1.after), channel_id=1, source_target_pairs={{0,3},{1,0},{2,1},{3,2},{4,7},{5,4},{6,5},{7,6},{8,11},{9,8},{10,9... | collective-permute-start | bytes 1544 | tf_op jit(solution)/shard_map/ppermute | solution.py:54
  109.3 0.8 collective-permute-start.17
  110.1 0.9 collective-permute-start.16
  111.0 0.9 finish.1
  111.9 1.1 assemble.1
  113.0 1.4 %collective-permute-done.17 = f32[1,128]{1,0:T(1,128)S(1)} collective-permute-done((f32[1,128]{1,0:T(1,128)S(1)}, f32[1,128]{1,0:T(1,128)S(1)}, u32[]{:S(2)}, u32[]{:S(2)}) %collective-permute-start.17) | collective-permute-done | bytes 544 | tf_op jit(solution)/shard_map/ppermute | solution.py:54
  (66 shorter events, 15.0 us)
Async XLA Ops:
  0.6 25.9 %copy-start.2 = (bf16[128,16,128]{2,1,0:T(8,128)(2,1)S(1)}, bf16[128,16,128]{2,1,0:T(8,128)(2,1)}, u32[]{:S(2)}) copy-start(bf16[128,16,128]{2,1,0:T(8,128)(2,1)} %param.11) | copy-start | bytes 1572868
  4.2 11.4 %copy-start.3 = (s32[1,128]{1,0:T(1,128)S(1)}, s32[1,128]{1,0:T(1,128)}, u32[]{:S(2)}) copy-start(s32[1,128]{1,0:T(1,128)} %param.15) | copy-start | bytes 1540
  4.2 22.4 %all-to-all-start = ((bf16[32,24,128]{2,1,0:T(8,128)(2,1)}), bf16[32,24,128]{2,1,0:T(8,128)(2,1)S(1)}, u32[]{:S(2)}, u32[]{:S(2)}) async-start(bf16[32,24,128]{2,1,0:T(8,128)(2,1)} %get-tuple-element.82), calls=%async_computation | async-start | bytes 393216 | tf_op jit(solution)/shard_map/all_to_all | solution.py:64
  15.6 12.8 %copy-start = (bf16[128,16,128]{2,1,0:T(8,128)(2,1)S(1)}, bf16[128,16,128]{2,1,0:T(8,128)(2,1)}, u32[]{:S(2)}) copy-start(bf16[128,16,128]{2,1,0:T(8,128)(2,1)} %queries.1) | copy-start | bytes 1572868
  26.5 1.4 %collective-permute-start = (bf16[32,24,128]{2,1,0:T(8,128)(2,1)S(1)}, bf16[32,24,128]{2,1,0:T(8,128)(2,1)S(1)}, u32[]{:S(2)}, u32[]{:S(2)}) collective-permute-start(bf16[32,24,128]{2,1,0:T(8,128)(2,1)S(1)} %all-to-all-done.mine), channel_id=1, source_target_pairs={{0,4},{4,0},{8,12},{12,8},{16,20},{20,16},{24,28},{28,24},{32,36},... | collective-permute-start | bytes 589832 | tf_op jit(solution)/shard_map/ppermute | solution.py:49
  26.8 1.6 %copy-start.1 = (bf16[4,128,128]{2,1,0:T(8,128)(2,1)S(1)}, bf16[4,128,128]{2,1,0:T(8,128)(2,1)}, u32[]{:S(2)}) copy-start(bf16[4,128,128]{2,1,0:T(8,128)(2,1)} %get-tuple-element.85.own_kv) | copy-start | bytes 393220
  28.5 19.7 %collective-permute-start.1 = (bf16[2304,128]{1,0:T(8,128)(2,1)S(1)}, bf16[2304,128]{1,0:T(8,128)(2,1)S(1)}, u32[]{:S(2)}, u32[]{:S(2)}) collective-permute-start(bf16[2304,128]{1,0:T(8,128)(2,1)S(1)} %get-tuple-element.87), channel_id=1, source_target_pairs={{0,4},{4,0},{8,12},{12,8},{16,20},{20,16},{24,28},{28,24},{32,36},... | collective-permute-start | bytes 1769480 | tf_op jit(solution)/shard_map/ppermute | solution.py:49
  43.2 10.2 %collective-permute-start.2 = (bf16[8,4,16,128]{3,2,1,0:T(8,128)(2,1)S(1)}, bf16[8,4,16,128]{3,2,1,0:T(8,128)(2,1)S(1)}, u32[]{:S(2)}, u32[]{:S(2)}) collective-permute-start(bf16[8,4,16,128]{3,2,1,0:T(8,128)(2,1)S(1)} %get-tuple-element.94), channel_id=1, source_target_pairs={{0,64},{4,68},{8,72},{12,76},{16,80},{20,84},{24,88},{28,92},{32,9... | collective-permute-start | bytes 393224 | tf_op jit(solution)/shard_map/ppermute | solution.py:44
  43.9 10.8 %collective-permute-start.3 = (bf16[8,4,16,128]{3,2,1,0:T(8,128)(2,1)S(1)}, bf16[8,4,16,128]{3,2,1,0:T(8,128)(2,1)S(1)}, u32[]{:S(2)}, u32[]{:S(2)}) collective-permute-start(bf16[8,4,16,128]{3,2,1,0:T(8,128)(2,1)S(1)} %get-tuple-element.98), channel_id=1, source_target_pairs={{0,128},{4,132},{8,136},{12,140},{16,144},{20,148},{24,152},{28,15... | collective-permute-start | bytes 393224 | tf_op jit(solution)/shard_map/ppermute | solution.py:44
  45.9 9.3 %collective-permute-start.4 = (bf16[8,4,16,128]{3,2,1,0:T(8,128)(2,1)S(1)}, bf16[8,4,16,128]{3,2,1,0:T(8,128)(2,1)S(1)}, u32[]{:S(2)}, u32[]{:S(2)}) collective-permute-start(bf16[8,4,16,128]{3,2,1,0:T(8,128)(2,1)S(1)} %get-tuple-element.100), channel_id=1, source_target_pairs={{0,192},{4,196},{8,200},{12,204},{16,208},{20,212},{24,216},{28,22... | collective-permute-start | bytes 393224 | tf_op jit(solution)/shard_map/ppermute | solution.py:44
  47.4 14.6 %collective-permute-start.5 = (bf16[8,4,16,128]{3,2,1,0:T(8,128)(2,1)S(1)}, bf16[8,4,16,128]{3,2,1,0:T(8,128)(2,1)S(1)}, u32[]{:S(2)}, u32[]{:S(2)}) collective-permute-start(bf16[8,4,16,128]{3,2,1,0:T(8,128)(2,1)S(1)} %get-tuple-element.116), channel_id=1, source_target_pairs={{0,64},{4,68},{8,72},{12,76},{16,80},{20,84},{24,88},{28,92},{32,9... | collective-permute-start | bytes 393224 | tf_op jit(solution)/shard_map/ppermute | solution.py:44
  48.2 14.4 %collective-permute-start.6 = (bf16[8,4,16,128]{3,2,1,0:T(8,128)(2,1)S(1)}, bf16[8,4,16,128]{3,2,1,0:T(8,128)(2,1)S(1)}, u32[]{:S(2)}, u32[]{:S(2)}) collective-permute-start(bf16[8,4,16,128]{3,2,1,0:T(8,128)(2,1)S(1)} %get-tuple-element.118), channel_id=1, source_target_pairs={{0,128},{4,132},{8,136},{12,140},{16,144},{20,148},{24,152},{28,15... | collective-permute-start | bytes 393224 | tf_op jit(solution)/shard_map/ppermute | solution.py:44
  53.5 9.7 %collective-permute-start.7 = (bf16[8,4,16,128]{3,2,1,0:T(8,128)(2,1)S(1)}, bf16[8,4,16,128]{3,2,1,0:T(8,128)(2,1)S(1)}, u32[]{:S(2)}, u32[]{:S(2)}) collective-permute-start(bf16[8,4,16,128]{3,2,1,0:T(8,128)(2,1)S(1)} %get-tuple-element.120), channel_id=1, source_target_pairs={{0,192},{4,196},{8,200},{12,204},{16,208},{20,212},{24,216},{28,22... | collective-permute-start | bytes 393224 | tf_op jit(solution)/shard_map/ppermute | solution.py:44
  57.1 9.6 %collective-permute-start.8 = (bf16[8,4,16,128]{3,2,1,0:T(8,128)(2,1)S(1)}, bf16[8,4,16,128]{3,2,1,0:T(8,128)(2,1)S(1)}, u32[]{:S(2)}, u32[]{:S(2)}) collective-permute-start(bf16[8,4,16,128]{3,2,1,0:T(8,128)(2,1)S(1)} %get-tuple-element.132), channel_id=1, source_target_pairs={{0,192},{4,196},{8,200},{12,204},{16,208},{20,212},{24,216},{28,22... | collective-permute-start | bytes 393224 | tf_op jit(solution)/shard_map/ppermute | solution.py:44
  59.2 7.5 %collective-permute-start.9 = (bf16[8,4,16,128]{3,2,1,0:T(8,128)(2,1)S(1)}, bf16[8,4,16,128]{3,2,1,0:T(8,128)(2,1)S(1)}, u32[]{:S(2)}, u32[]{:S(2)}) collective-permute-start(bf16[8,4,16,128]{3,2,1,0:T(8,128)(2,1)S(1)} %get-tuple-element.133), channel_id=1, source_target_pairs={{0,128},{4,132},{8,136},{12,140},{16,144},{20,148},{24,152},{28,15... | collective-permute-start | bytes 393224 | tf_op jit(solution)/shard_map/ppermute | solution.py:44
  62.1 7.3 %collective-permute-start.10 = (bf16[8,4,16,128]{3,2,1,0:T(8,128)(2,1)S(1)}, bf16[8,4,16,128]{3,2,1,0:T(8,128)(2,1)S(1)}, u32[]{:S(2)}, u32[]{:S(2)}) collective-permute-start(bf16[8,4,16,128]{3,2,1,0:T(8,128)(2,1)S(1)} %get-tuple-element.136), channel_id=1, source_target_pairs={{0,64},{4,68},{8,72},{12,76},{16,80},{20,84},{24,88},{28,92},{32,9... | collective-permute-start | bytes 393224 | tf_op jit(solution)/shard_map/ppermute | solution.py:44
  64.5 8.6 %collective-permute-start.12 = (bf16[8,4,16,128]{3,2,1,0:T(8,128)(2,1)S(1)}, bf16[8,4,16,128]{3,2,1,0:T(8,128)(2,1)S(1)}, u32[]{:S(2)}, u32[]{:S(2)}) collective-permute-start(bf16[8,4,16,128]{3,2,1,0:T(8,128)(2,1)S(1)} %get-tuple-element.147), channel_id=1, source_target_pairs={{0,128},{4,132},{8,136},{12,140},{16,144},{20,148},{24,152},{28,15... | collective-permute-start | bytes 393224 | tf_op jit(solution)/shard_map/ppermute | solution.py:44
  67.5 5.5 %collective-permute-start.13 = (bf16[8,4,16,128]{3,2,1,0:T(8,128)(2,1)S(1)}, bf16[8,4,16,128]{3,2,1,0:T(8,128)(2,1)S(1)}, u32[]{:S(2)}, u32[]{:S(2)}) collective-permute-start(bf16[8,4,16,128]{3,2,1,0:T(8,128)(2,1)S(1)} %get-tuple-element.148), channel_id=1, source_target_pairs={{0,192},{4,196},{8,200},{12,204},{16,208},{20,212},{24,216},{28,22... | collective-permute-start | bytes 393224 | tf_op jit(solution)/shard_map/ppermute | solution.py:44
  70.0 6.3 %collective-permute-start.11 = (bf16[8,4,16,128]{3,2,1,0:T(8,128)(2,1)S(1)}, bf16[8,4,16,128]{3,2,1,0:T(8,128)(2,1)S(1)}, u32[]{:S(2)}, u32[]{:S(2)}) collective-permute-start(bf16[8,4,16,128]{3,2,1,0:T(8,128)(2,1)S(1)} %get-tuple-element.146), channel_id=1, source_target_pairs={{0,64},{4,68},{8,72},{12,76},{16,80},{20,84},{24,88},{28,92},{32,9... | collective-permute-start | bytes 393224 | tf_op jit(solution)/shard_map/ppermute | solution.py:44
  105.0 1.3 %collective-permute-start.14 = (bf16[17,16,128]{2,1,0:T(8,128)(2,1)S(1)}, bf16[17,16,128]{2,1,0:T(8,128)(2,1)S(1)}, u32[]{:S(2)}, u32[]{:S(2)}) collective-permute-start(bf16[17,16,128]{2,1,0:T(8,128)(2,1)S(1)} %get-tuple-element.154), channel_id=1, source_target_pairs={{0,4},{4,0},{8,12},{12,8},{16,20},{20,16},{24,28},{28,24},{32,36},... | collective-permute-start | bytes 208904 | tf_op jit(solution)/shard_map/ppermute | solution.py:49
  106.4 4.6 %collective-permute-start.15 = (f32[1280,128]{1,0:T(8,128)S(1)}, f32[1280,128]{1,0:T(8,128)S(1)}, u32[]{:S(2)}, u32[]{:S(2)}) collective-permute-start(f32[1280,128]{1,0:T(8,128)S(1)} %ship.1), channel_id=1, source_target_pairs={{0,4},{4,0},{8,12},{12,8},{16,20},{20,16},{24,28},{28,24},{32,36},... | collective-permute-start | bytes 1966088 | tf_op jit(solution)/shard_map/ppermute | solution.py:49
  106.6 6.4 %collective-permute-start.18 = (f32[1,128]{1,0:T(1,128)S(1)}, f32[1,128]{1,0:T(1,128)S(1)}, u32[]{:S(2)}, u32[]{:S(2)}) collective-permute-start(f32[1,128]{1,0:T(1,128)S(1)} %tally.1.after), channel_id=1, source_target_pairs={{0,3},{1,0},{2,1},{3,2},{4,7},{5,4},{6,5},{7,6},{8,11},{9,8},{10,9... | collective-permute-start | bytes 1544 | tf_op jit(solution)/shard_map/ppermute | solution.py:54
  109.3 5.0 %collective-permute-start.17 = (f32[1,128]{1,0:T(1,128)S(1)}, f32[1,128]{1,0:T(1,128)S(1)}, u32[]{:S(2)}, u32[]{:S(2)}) collective-permute-start(f32[1,128]{1,0:T(1,128)S(1)} %tally.1.after), channel_id=1, source_target_pairs={{0,2},{1,3},{2,0},{3,1},{4,6},{5,7},{6,4},{7,5},{8,10},{9,11},{10,... | collective-permute-start | bytes 1544 | tf_op jit(solution)/shard_map/ppermute | solution.py:54
  110.1 4.8 %collective-permute-start.16 = (f32[1,128]{1,0:T(1,128)S(1)}, f32[1,128]{1,0:T(1,128)S(1)}, u32[]{:S(2)}, u32[]{:S(2)}) collective-permute-start(f32[1,128]{1,0:T(1,128)S(1)} %tally.1.after), channel_id=1, source_target_pairs={{0,1},{1,2},{2,3},{3,0},{4,5},{5,6},{6,7},{7,4},{8,9},{9,10},{10,1... | collective-permute-start | bytes 1544 | tf_op jit(solution)/shard_map/ppermute | solution.py:54

commit v8 on v7

--- a/solution.py
+++ b/solution.py
@@ -381,6 +381,25 @@
     one_part(own_kv[2 * h], own_kv[2 * h + 1], q, g, causal, own_exps, own_pgs, stats, 4)
 
 
+def all_scores_kernel(h, table, q_all, g_all, p1, p2, p3, after, *outs):
+    for i, part in enumerate((p1, p2, p3)):
+        keys, values = rows_of(part, 0), rows_of(part, 1)
+        one_part(
+            keys, values, q_all[h], g_all[h], listed(h, table), *outs[3 * i : 3 * i + 3], 0
+        )
+
+
+def all_scores_of(h, table, q_all, g_all, parts, after):
+    return pl.pallas_call(
+        functools.partial(all_scores_kernel, h),
+        in_specs=[in_vmem()] * 6 + [pl.BlockSpec(memory_space=pl.ANY)],
+        out_specs=(in_vmem(),) * 9,
+        **call(all_scores_kernel, (wide(PART), wide(PART), STATS) * 3, vmem_mb=16),
+        cost_estimate=cost(3 * PART, 2),
+        name="scores_all",
+    )(table, q_all, g_all, *parts, after)
+
+
 def wide(keys):
     return jax.ShapeDtypeStruct((keys, ROWS), F32)
 
@@ -582,9 +601,14 @@
 def attend(h, table, q_all, g_all, own_kv, parts, first, after, hints):
     e, pg, st = [None] * NY, [None] * NY, [None] * NY
     e[0], pg[0], st[0], own_e, own_pg = first
-    for k in (1, 2, 3):
-        e[k], pg[k], st[k] = scores_of(h, table, q_all, g_all, parts[k], after)
-        after = st[k]
+    if h == 0:
+        for k in (1, 2, 3):
+            e[k], pg[k], st[k] = scores_of(h, table, q_all, g_all, parts[k], after)
+            after = st[0] if k == 1 else st[k]
+    else:
+        outs = all_scores_of(h, table, q_all, g_all, parts[1:], after)
+        for k in (1, 2, 3):
+            e[k], pg[k], st[k] = outs[3 * k - 3 : 3 * k]
     back = [None] * NY
     dq_type = jax.ShapeDtypeStruct((HD, ROWS), F32)
     own_type = jax.ShapeDtypeStruct((2, TOK, HD), F32)

time: 116 us -> 116 us (level)
    pallas_call x6 -> x3, Pallas kernels: 3.03 us -> 1.51 us  [scores_of(): pl.pallas_call(functools.partial(scores_kernel, h), in_specs=[in_vmem()]...]
    pallas_call x0 -> x1, Pallas kernels: none -> 1.28 us  [all_scores_of(): pl.pallas_call(functools.partial(all_scores_kernel, h), in_specs=[in_vmem...]
where the time goes in v8:
time: 116 us
  blocking collectives  42.5 us (37%)
  starting transfers between devices  32.4 us (28%)
  waiting for transfers between devices  21.7 us (19%)
  Pallas kernels  15.7 us (14%)
  between operations  3.53 us (3%)
    all_to_all x2, blocking collectives, swap_z(): lax.all_to_all(x, 'branch', 0, 0, axis_index_groups=groups, tiled=False)  27.8 us
    ppermute x12, starting transfers between devices, along_y(): return lax.ppermute(x, 'branch', pairs)  16.1 us
    all_to_all x1, blocking collectives, swap_yz(): lax.all_to_all(x, 'branch', 0, 0, axis_index_groups=groups, tiled=False)  14.7 us
    all_to_all x1, starting transfers between devices, swap_yz(): lax.all_to_all(x, 'branch', 0, 0, axis_index_groups=groups, tiled=False)  11.4 us
    all_to_all x1, waiting for transfers between devices, swap_yz(): lax.all_to_all(x, 'branch', 0, 0, axis_index_groups=groups, tiled=False)  10.9 us
    ppermute x12, waiting for transfers between devices, along_y(): return lax.ppermute(x, 'branch', pairs)  6.45 us
    pallas_call x8, Pallas kernels, grads_of(): pl.pallas_call(functools.partial(body, k, h), in_specs=[in_vmem()] * len(...  5.1 us
    ppermute x3, starting transfers between devices, along_head(): return lax.ppermute(x, 'head', pairs)  4.48 us
  transfers between devices with their start and end apart: 20, of which 8 were waited for; matrix products, arithmetic and copies ran while one was open for 0% of the time, Pallas kernels for 11%

profile of v8, /device:TPU:32, one launch (start us, length us, event | category | flops | bytes accessed | tf_op | source)
XLA Modules:
  0.0 116.1 jit_solution(4128521295813967838)
XLA Ops:
  2.0 2.2 %packet.1 = (bf16[32,24,128]{2,1,0:T(8,128)(2,1)}, bf16[4,128,128]{2,1,0:T(8,128)(2,1)}) custom-call(bf16[128,2,128]{2,1,0:T(2,128)(2,1)} %keys_far.1, bf16[128,2,128]{2,1,0:T(2,128)(2,1)} %values_far.1, s32[1,8]{1,0:T(1,128)} %ancestors_far.1, s32[1]{0:T(128)S(6)} %copy.25.group, bf16[1]{0:T(256)(128)(2,1)S(6)} %copy.24.reward), custom_call_target="tpu_custom_call" | custom-call | tf_op jit(solution)/shard_map/packet/pallas_call | solution.py:136
  4.2 11.4 %all-to-all-start = ((bf16[32,24,128]{2,1,0:T(8,128)(2,1)}), bf16[32,24,128]{2,1,0:T(8,128)(2,1)S(1)}, u32[]{:S(2)}, u32[]{:S(2)}) async-start(bf16[32,24,128]{2,1,0:T(8,128)(2,1)} %get-tuple-element.82), calls=%async_computation | async-start | bytes 393216 | tf_op jit(solution)/shard_map/all_to_all | solution.py:64
  15.6 10.9 %all-to-all-done.mine = bf16[32,24,128]{2,1,0:T(8,128)(2,1)S(1)} async-done(((bf16[32,24,128]{2,1,0:T(8,128)(2,1)}), bf16[32,24,128]{2,1,0:T(8,128)(2,1)S(1)}, u32[]{:S(2)}, u32[]{:S(2)}) %all-to-all-start) | async-done | bytes 196640 | tf_op jit(solution)/shard_map/all_to_all | solution.py:64
  26.8 1.2 %collective-permute-done.other = bf16[32,24,128]{2,1,0:T(8,128)(2,1)S(1)} collective-permute-done((bf16[32,24,128]{2,1,0:T(8,128)(2,1)S(1)}, bf16[32,24,128]{2,1,0:T(8,128)(2,1)S(1)}, u32[]{:S(2)}, u32[]{:S(2)}) %collective-permute-start) | collective-permute-done | bytes 196640 | tf_op jit(solution)/shard_map/ppermute | solution.py:49
  28.8 14.3 %all_to_all.20.column = bf16[8,8,16,128]{3,2,1,0:T(8,128)(2,1)S(1)} all-to-all(bf16[8,8,16,128]{3,2,1,0:T(8,128)(2,1)S(1)} %get-tuple-element.90), channel_id=1, replica_groups={{0,8,16,24,32,40,48,56},{4,12,20,28,36,44,52,60},{64,72,80,88,96,104,11..., dimensions={0} | all-to-all | bytes 524288 | tf_op jit(solution)/shard_map/all_to_all | solution.py:59
  43.9 2.0 %collective-permute-start.3 = (bf16[8,4,16,128]{3,2,1,0:T(8,128)(2,1)S(1)}, bf16[8,4,16,128]{3,2,1,0:T(8,128)(2,1)S(1)}, u32[]{:S(2)}, u32[]{:S(2)}) collective-permute-start(bf16[8,4,16,128]{3,2,1,0:T(8,128)(2,1)S(1)} %get-tuple-element.98), channel_id=1, source_target_pairs={{0,128},{4,132},{8,136},{12,140},{16,144},{20,148},{24,152},{28,15... | collective-permute-start | bytes 393224 | tf_op jit(solution)/shard_map/ppermute | solution.py:44
  45.9 1.3 %collective-permute-start.4 = (bf16[8,4,16,128]{3,2,1,0:T(8,128)(2,1)S(1)}, bf16[8,4,16,128]{3,2,1,0:T(8,128)(2,1)S(1)}, u32[]{:S(2)}, u32[]{:S(2)}) collective-permute-start(bf16[8,4,16,128]{3,2,1,0:T(8,128)(2,1)S(1)} %get-tuple-element.100), channel_id=1, source_target_pairs={{0,192},{4,196},{8,200},{12,204},{16,208},{20,212},{24,216},{28,22... | collective-permute-start | bytes 393224 | tf_op jit(solution)/shard_map/ppermute | solution.py:44
  48.2 1.6 %collective-permute-start.6 = (bf16[8,4,16,128]{3,2,1,0:T(8,128)(2,1)S(1)}, bf16[8,4,16,128]{3,2,1,0:T(8,128)(2,1)S(1)}, u32[]{:S(2)}, u32[]{:S(2)}) collective-permute-start(bf16[8,4,16,128]{3,2,1,0:T(8,128)(2,1)S(1)} %get-tuple-element.117), channel_id=1, source_target_pairs={{0,128},{4,132},{8,136},{12,140},{16,144},{20,148},{24,152},{28,15... | collective-permute-start | bytes 393224 | tf_op jit(solution)/shard_map/ppermute | solution.py:44
  51.4 2.1 %collective-permute-done.2.part = bf16[8,4,16,128]{3,2,1,0:T(8,128)(2,1)S(1)} collective-permute-done((bf16[8,4,16,128]{3,2,1,0:T(8,128)(2,1)S(1)}, bf16[8,4,16,128]{3,2,1,0:T(8,128)(2,1)S(1)}, u32[]{:S(2)}, u32[]{:S(2)}) %collective-permute-start.2) | collective-permute-done | bytes 131104 | tf_op jit(solution)/shard_map/ppermute | solution.py:44
  55.5 0.8 grads_first.2
  56.9 2.3 %collective-permute-start.8 = (bf16[8,4,16,128]{3,2,1,0:T(8,128)(2,1)S(1)}, bf16[8,4,16,128]{3,2,1,0:T(8,128)(2,1)S(1)}, u32[]{:S(2)}, u32[]{:S(2)}) collective-permute-start(bf16[8,4,16,128]{3,2,1,0:T(8,128)(2,1)S(1)} %get-tuple-element.132), channel_id=1, source_target_pairs={{0,192},{4,196},{8,200},{12,204},{16,208},{20,212},{24,216},{28,22... | collective-permute-start | bytes 393224 | tf_op jit(solution)/shard_map/ppermute | solution.py:44
  59.2 1.5 %collective-permute-start.9 = (bf16[8,4,16,128]{3,2,1,0:T(8,128)(2,1)S(1)}, bf16[8,4,16,128]{3,2,1,0:T(8,128)(2,1)S(1)}, u32[]{:S(2)}, u32[]{:S(2)}) collective-permute-start(bf16[8,4,16,128]{3,2,1,0:T(8,128)(2,1)S(1)} %get-tuple-element.133), channel_id=1, source_target_pairs={{0,128},{4,132},{8,136},{12,140},{16,144},{20,148},{24,152},{28,15... | collective-permute-start | bytes 393224 | tf_op jit(solution)/shard_map/ppermute | solution.py:44
  61.5 1.3 %scores_all.1 = (f32[256,1024]{1,0:T(8,128)S(1)}, f32[256,1024]{1,0:T(8,128)S(1)}, f32[8,1024]{1,0:T(8,128)S(1)}, f32[256,1024]{1,0:T(8,128)S(1)}, f32[256,1024]...) custom-call(s32[88,128]{1,0:T(8,128)S(1)} %get-tuple-element.83.afte, ...), custom_call_target="tpu_custom_call" | custom-call | flops 402653184 | bytes 6291456 | tf_op jit(solution)/shard_map/scores_all/pallas_call | solution.py:393
  63.6 2.6 %collective-permute-start.12 = (bf16[8,4,16,128]{3,2,1,0:T(8,128)(2,1)S(1)}, bf16[8,4,16,128]{3,2,1,0:T(8,128)(2,1)S(1)}, u32[]{:S(2)}, u32[]{:S(2)}) collective-permute-start(bf16[8,4,16,128]{3,2,1,0:T(8,128)(2,1)S(1)} %get-tuple-element.147), channel_id=1, source_target_pairs={{0,128},{4,132},{8,136},{12,140},{16,144},{20,148},{24,152},{28,15... | collective-permute-start | bytes 393224 | tf_op jit(solution)/shard_map/ppermute | solution.py:44
  67.0 2.5 %collective-permute-start.13 = (bf16[8,4,16,128]{3,2,1,0:T(8,128)(2,1)S(1)}, bf16[8,4,16,128]{3,2,1,0:T(8,128)(2,1)S(1)}, u32[]{:S(2)}, u32[]{:S(2)}) collective-permute-start(bf16[8,4,16,128]{3,2,1,0:T(8,128)(2,1)S(1)} %get-tuple-element.148), channel_id=1, source_target_pairs={{0,192},{4,196},{8,200},{12,204},{16,208},{20,212},{24,216},{28,22... | collective-permute-start | bytes 393224 | tf_op jit(solution)/shard_map/ppermute | solution.py:44
  72.3 4.1 %collective-permute-done.11.refs_0_ = bf16[8,4,16,128]{3,2,1,0:T(8,128)(2,1)S(1)} collective-permute-done((bf16[8,4,16,128]{3,2,1,0:T(8,128)(2,1)S(1)}, bf16[8,4,16,128]{3,2,1,0:T(8,128)(2,1)S(1)}, u32[]{:S(2)}, u32[]{:S(2)}) %collective-permute-start.11) | collective-permute-done | bytes 131104 | tf_op jit(solution)/shard_map/ppermute | solution.py:44
  76.6 13.5 %all_to_all.21.parts = bf16[8,8,16,128]{3,2,1,0:T(8,128)(2,1)S(1)} all-to-all(bf16[8,8,16,128]{3,2,1,0:T(8,128)(2,1)S(1)} %leave.1), channel_id=1, replica_groups={{0,8,16,24,32,40,48,56},{4,12,20,28,36,44,52,60},{64,72,80,88,96,104,11..., dimensions={0} | all-to-all | bytes 524288 | tf_op jit(solution)/shard_map/all_to_all | solution.py:59
  90.2 14.7 %all_to_all.22.arrived = bf16[32,24,128]{2,1,0:T(8,128)(2,1)S(1)} all-to-all(bf16[32,24,128]{2,1,0:T(8,128)(2,1)S(1)} %route.1), channel_id=1, replica_groups={{0,8,16,24,32,40,48,56,64,72,80,88,96,104,112,120,128,136,144,152,160,1..., dimensions={0} | all-to-all | bytes 393216 | tf_op jit(solution)/shard_map/all_to_all | solution.py:64
  105.1 1.2 %collective-permute-done.14.got = bf16[17,16,128]{2,1,0:T(8,128)(2,1)S(1)} collective-permute-done((bf16[17,16,128]{2,1,0:T(8,128)(2,1)S(1)}, bf16[17,16,128]{2,1,0:T(8,128)(2,1)S(1)}, u32[]{:S(2)}, u32[]{:S(2)}) %collective-permute-start.14) | collective-permute-done | bytes 69664 | tf_op jit(solution)/shard_map/ppermute | solution.py:49
  106.6 2.8 %collective-permute-start.18 = (f32[1,128]{1,0:T(1,128)S(1)}, f32[1,128]{1,0:T(1,128)S(1)}, u32[]{:S(2)}, u32[]{:S(2)}) collective-permute-start(f32[1,128]{1,0:T(1,128)S(1)} %tally.1.after), channel_id=1, source_target_pairs={{0,3},{1,0},{2,1},{3,2},{4,7},{5,4},{6,5},{7,6},{8,11},{9,8},{10,9... | collective-permute-start | bytes 1544 | tf_op jit(solution)/shard_map/ppermute | solution.py:54
  110.2 0.9 collective-permute-start.16
  111.1 0.9 finish.1
  111.9 1.1 assemble.1
  113.1 1.4 %collective-permute-done.17 = f32[1,128]{1,0:T(1,128)S(1)} collective-permute-done((f32[1,128]{1,0:T(1,128)S(1)}, f32[1,128]{1,0:T(1,128)S(1)}, u32[]{:S(2)}, u32[]{:S(2)}) %collective-permute-start.17) | collective-permute-done | bytes 544 | tf_op jit(solution)/shard_map/ppermute | solution.py:54
  (64 shorter events, 13.8 us)
Async XLA Ops:
  0.6 25.9 %copy-start.2 = (bf16[128,16,128]{2,1,0:T(8,128)(2,1)S(1)}, bf16[128,16,128]{2,1,0:T(8,128)(2,1)}, u32[]{:S(2)}) copy-start(bf16[128,16,128]{2,1,0:T(8,128)(2,1)} %param.11) | copy-start | bytes 1572868
  4.2 11.4 %copy-start.3 = (s32[1,128]{1,0:T(1,128)S(1)}, s32[1,128]{1,0:T(1,128)}, u32[]{:S(2)}) copy-start(s32[1,128]{1,0:T(1,128)} %param.15) | copy-start | bytes 1540
  4.2 22.4 %all-to-all-start = ((bf16[32,24,128]{2,1,0:T(8,128)(2,1)}), bf16[32,24,128]{2,1,0:T(8,128)(2,1)S(1)}, u32[]{:S(2)}, u32[]{:S(2)}) async-start(bf16[32,24,128]{2,1,0:T(8,128)(2,1)} %get-tuple-element.82), calls=%async_computation | async-start | bytes 393216 | tf_op jit(solution)/shard_map/all_to_all | solution.py:64
  15.6 12.8 %copy-start = (bf16[128,16,128]{2,1,0:T(8,128)(2,1)S(1)}, bf16[128,16,128]{2,1,0:T(8,128)(2,1)}, u32[]{:S(2)}) copy-start(bf16[128,16,128]{2,1,0:T(8,128)(2,1)} %queries.1) | copy-start | bytes 1572868
  26.5 1.4 %collective-permute-start = (bf16[32,24,128]{2,1,0:T(8,128)(2,1)S(1)}, bf16[32,24,128]{2,1,0:T(8,128)(2,1)S(1)}, u32[]{:S(2)}, u32[]{:S(2)}) collective-permute-start(bf16[32,24,128]{2,1,0:T(8,128)(2,1)S(1)} %all-to-all-done.mine), channel_id=1, source_target_pairs={{0,4},{4,0},{8,12},{12,8},{16,20},{20,16},{24,28},{28,24},{32,36},... | collective-permute-start | bytes 589832 | tf_op jit(solution)/shard_map/ppermute | solution.py:49
  26.8 1.6 %copy-start.1 = (bf16[4,128,128]{2,1,0:T(8,128)(2,1)S(1)}, bf16[4,128,128]{2,1,0:T(8,128)(2,1)}, u32[]{:S(2)}) copy-start(bf16[4,128,128]{2,1,0:T(8,128)(2,1)} %get-tuple-element.85.own_kv) | copy-start | bytes 393220
  28.5 19.7 %collective-permute-start.1 = (bf16[2304,128]{1,0:T(8,128)(2,1)S(1)}, bf16[2304,128]{1,0:T(8,128)(2,1)S(1)}, u32[]{:S(2)}, u32[]{:S(2)}) collective-permute-start(bf16[2304,128]{1,0:T(8,128)(2,1)S(1)} %get-tuple-element.87), channel_id=1, source_target_pairs={{0,4},{4,0},{8,12},{12,8},{16,20},{20,16},{24,28},{28,24},{32,36},... | collective-permute-start | bytes 1769480 | tf_op jit(solution)/shard_map/ppermute | solution.py:49
  43.2 10.2 %collective-permute-start.2 = (bf16[8,4,16,128]{3,2,1,0:T(8,128)(2,1)S(1)}, bf16[8,4,16,128]{3,2,1,0:T(8,128)(2,1)S(1)}, u32[]{:S(2)}, u32[]{:S(2)}) collective-permute-start(bf16[8,4,16,128]{3,2,1,0:T(8,128)(2,1)S(1)} %get-tuple-element.94), channel_id=1, source_target_pairs={{0,64},{4,68},{8,72},{12,76},{16,80},{20,84},{24,88},{28,92},{32,9... | collective-permute-start | bytes 393224 | tf_op jit(solution)/shard_map/ppermute | solution.py:44
  43.9 10.6 %collective-permute-start.3 = (bf16[8,4,16,128]{3,2,1,0:T(8,128)(2,1)S(1)}, bf16[8,4,16,128]{3,2,1,0:T(8,128)(2,1)S(1)}, u32[]{:S(2)}, u32[]{:S(2)}) collective-permute-start(bf16[8,4,16,128]{3,2,1,0:T(8,128)(2,1)S(1)} %get-tuple-element.98), channel_id=1, source_target_pairs={{0,128},{4,132},{8,136},{12,140},{16,144},{20,148},{24,152},{28,15... | collective-permute-start | bytes 393224 | tf_op jit(solution)/shard_map/ppermute | solution.py:44
  45.9 9.1 %collective-permute-start.4 = (bf16[8,4,16,128]{3,2,1,0:T(8,128)(2,1)S(1)}, bf16[8,4,16,128]{3,2,1,0:T(8,128)(2,1)S(1)}, u32[]{:S(2)}, u32[]{:S(2)}) collective-permute-start(bf16[8,4,16,128]{3,2,1,0:T(8,128)(2,1)S(1)} %get-tuple-element.100), channel_id=1, source_target_pairs={{0,192},{4,196},{8,200},{12,204},{16,208},{20,212},{24,216},{28,22... | collective-permute-start | bytes 393224 | tf_op jit(solution)/shard_map/ppermute | solution.py:44
  47.4 13.9 %collective-permute-start.5 = (bf16[8,4,16,128]{3,2,1,0:T(8,128)(2,1)S(1)}, bf16[8,4,16,128]{3,2,1,0:T(8,128)(2,1)S(1)}, u32[]{:S(2)}, u32[]{:S(2)}) collective-permute-start(bf16[8,4,16,128]{3,2,1,0:T(8,128)(2,1)S(1)} %get-tuple-element.116), channel_id=1, source_target_pairs={{0,64},{4,68},{8,72},{12,76},{16,80},{20,84},{24,88},{28,92},{32,9... | collective-permute-start | bytes 393224 | tf_op jit(solution)/shard_map/ppermute | solution.py:44
  48.2 13.2 %collective-permute-start.6 = (bf16[8,4,16,128]{3,2,1,0:T(8,128)(2,1)S(1)}, bf16[8,4,16,128]{3,2,1,0:T(8,128)(2,1)S(1)}, u32[]{:S(2)}, u32[]{:S(2)}) collective-permute-start(bf16[8,4,16,128]{3,2,1,0:T(8,128)(2,1)S(1)} %get-tuple-element.117), channel_id=1, source_target_pairs={{0,128},{4,132},{8,136},{12,140},{16,144},{20,148},{24,152},{28,15... | collective-permute-start | bytes 393224 | tf_op jit(solution)/shard_map/ppermute | solution.py:44
  53.5 8.0 %collective-permute-start.7 = (bf16[8,4,16,128]{3,2,1,0:T(8,128)(2,1)S(1)}, bf16[8,4,16,128]{3,2,1,0:T(8,128)(2,1)S(1)}, u32[]{:S(2)}, u32[]{:S(2)}) collective-permute-start(bf16[8,4,16,128]{3,2,1,0:T(8,128)(2,1)S(1)} %get-tuple-element.118), channel_id=1, source_target_pairs={{0,192},{4,196},{8,200},{12,204},{16,208},{20,212},{24,216},{28,22... | collective-permute-start | bytes 393224 | tf_op jit(solution)/shard_map/ppermute | solution.py:44
  56.9 9.3 %collective-permute-start.8 = (bf16[8,4,16,128]{3,2,1,0:T(8,128)(2,1)S(1)}, bf16[8,4,16,128]{3,2,1,0:T(8,128)(2,1)S(1)}, u32[]{:S(2)}, u32[]{:S(2)}) collective-permute-start(bf16[8,4,16,128]{3,2,1,0:T(8,128)(2,1)S(1)} %get-tuple-element.132), channel_id=1, source_target_pairs={{0,192},{4,196},{8,200},{12,204},{16,208},{20,212},{24,216},{28,22... | collective-permute-start | bytes 393224 | tf_op jit(solution)/shard_map/ppermute | solution.py:44
  59.2 7.0 %collective-permute-start.9 = (bf16[8,4,16,128]{3,2,1,0:T(8,128)(2,1)S(1)}, bf16[8,4,16,128]{3,2,1,0:T(8,128)(2,1)S(1)}, u32[]{:S(2)}, u32[]{:S(2)}) collective-permute-start(bf16[8,4,16,128]{3,2,1,0:T(8,128)(2,1)S(1)} %get-tuple-element.133), channel_id=1, source_target_pairs={{0,128},{4,132},{8,136},{12,140},{16,144},{20,148},{24,152},{28,15... | collective-permute-start | bytes 393224 | tf_op jit(solution)/shard_map/ppermute | solution.py:44
  61.4 8.1 %collective-permute-start.10 = (bf16[8,4,16,128]{3,2,1,0:T(8,128)(2,1)S(1)}, bf16[8,4,16,128]{3,2,1,0:T(8,128)(2,1)S(1)}, u32[]{:S(2)}, u32[]{:S(2)}) collective-permute-start(bf16[8,4,16,128]{3,2,1,0:T(8,128)(2,1)S(1)} %get-tuple-element.136), channel_id=1, source_target_pairs={{0,64},{4,68},{8,72},{12,76},{16,80},{20,84},{24,88},{28,92},{32,9... | collective-permute-start | bytes 393224 | tf_op jit(solution)/shard_map/ppermute | solution.py:44
  63.6 8.6 %collective-permute-start.12 = (bf16[8,4,16,128]{3,2,1,0:T(8,128)(2,1)S(1)}, bf16[8,4,16,128]{3,2,1,0:T(8,128)(2,1)S(1)}, u32[]{:S(2)}, u32[]{:S(2)}) collective-permute-start(bf16[8,4,16,128]{3,2,1,0:T(8,128)(2,1)S(1)} %get-tuple-element.147), channel_id=1, source_target_pairs={{0,128},{4,132},{8,136},{12,140},{16,144},{20,148},{24,152},{28,15... | collective-permute-start | bytes 393224 | tf_op jit(solution)/shard_map/ppermute | solution.py:44
  67.0 5.1 %collective-permute-start.13 = (bf16[8,4,16,128]{3,2,1,0:T(8,128)(2,1)S(1)}, bf16[8,4,16,128]{3,2,1,0:T(8,128)(2,1)S(1)}, u32[]{:S(2)}, u32[]{:S(2)}) collective-permute-start(bf16[8,4,16,128]{3,2,1,0:T(8,128)(2,1)S(1)} %get-tuple-element.148), channel_id=1, source_target_pairs={{0,192},{4,196},{8,200},{12,204},{16,208},{20,212},{24,216},{28,22... | collective-permute-start | bytes 393224 | tf_op jit(solution)/shard_map/ppermute | solution.py:44
  70.2 6.3 %collective-permute-start.11 = (bf16[8,4,16,128]{3,2,1,0:T(8,128)(2,1)S(1)}, bf16[8,4,16,128]{3,2,1,0:T(8,128)(2,1)S(1)}, u32[]{:S(2)}, u32[]{:S(2)}) collective-permute-start(bf16[8,4,16,128]{3,2,1,0:T(8,128)(2,1)S(1)} %get-tuple-element.146), channel_id=1, source_target_pairs={{0,64},{4,68},{8,72},{12,76},{16,80},{20,84},{24,88},{28,92},{32,9... | collective-permute-start | bytes 393224 | tf_op jit(solution)/shard_map/ppermute | solution.py:44
  105.0 1.3 %collective-permute-start.14 = (bf16[17,16,128]{2,1,0:T(8,128)(2,1)S(1)}, bf16[17,16,128]{2,1,0:T(8,128)(2,1)S(1)}, u32[]{:S(2)}, u32[]{:S(2)}) collective-permute-start(bf16[17,16,128]{2,1,0:T(8,128)(2,1)S(1)} %get-tuple-element.154), channel_id=1, source_target_pairs={{0,4},{4,0},{8,12},{12,8},{16,20},{20,16},{24,28},{28,24},{32,36},... | collective-permute-start | bytes 208904 | tf_op jit(solution)/shard_map/ppermute | solution.py:49
  106.4 4.7 %collective-permute-start.15 = (f32[1280,128]{1,0:T(8,128)S(1)}, f32[1280,128]{1,0:T(8,128)S(1)}, u32[]{:S(2)}, u32[]{:S(2)}) collective-permute-start(f32[1280,128]{1,0:T(8,128)S(1)} %ship.1), channel_id=1, source_target_pairs={{0,4},{4,0},{8,12},{12,8},{16,20},{20,16},{24,28},{28,24},{32,36},... | collective-permute-start | bytes 1966088 | tf_op jit(solution)/shard_map/ppermute | solution.py:49
  106.6 6.5 %collective-permute-start.18 = (f32[1,128]{1,0:T(1,128)S(1)}, f32[1,128]{1,0:T(1,128)S(1)}, u32[]{:S(2)}, u32[]{:S(2)}) collective-permute-start(f32[1,128]{1,0:T(1,128)S(1)} %tally.1.after), channel_id=1, source_target_pairs={{0,3},{1,0},{2,1},{3,2},{4,7},{5,4},{6,5},{7,6},{8,11},{9,8},{10,9... | collective-permute-start | bytes 1544 | tf_op jit(solution)/shard_map/ppermute | solution.py:54
  109.4 5.0 %collective-permute-start.17 = (f32[1,128]{1,0:T(1,128)S(1)}, f32[1,128]{1,0:T(1,128)S(1)}, u32[]{:S(2)}, u32[]{:S(2)}) collective-permute-start(f32[1,128]{1,0:T(1,128)S(1)} %tally.1.after), channel_id=1, source_target_pairs={{0,2},{1,3},{2,0},{3,1},{4,6},{5,7},{6,4},{7,5},{8,10},{9,11},{10,... | collective-permute-start | bytes 1544 | tf_op jit(solution)/shard_map/ppermute | solution.py:54
  110.2 4.8 %collective-permute-start.16 = (f32[1,128]{1,0:T(1,128)S(1)}, f32[1,128]{1,0:T(1,128)S(1)}, u32[]{:S(2)}, u32[]{:S(2)}) collective-permute-start(f32[1,128]{1,0:T(1,128)S(1)} %tally.1.after), channel_id=1, source_target_pairs={{0,1},{1,2},{2,3},{3,0},{4,5},{5,6},{6,7},{7,4},{8,9},{9,10},{10,1... | collective-permute-start | bytes 1544 | tf_op jit(solution)/shard_map/ppermute | solution.py:54
